TPU v7x, 32 devices: a whole 2x2x4 slice. The times are simulated.
32 devices in a mesh: shard: 8 (over z, y), rep: 4 (over x, core).
Axes of the slice: x: 2, y: 2, z: 4, core: 2. Of those that a mesh axis runs over, the one named last changes fastest.
Arguments:
- tokens: bfloat16 [16, 1024, 1024], P('rep', 'shard'), may hold values from -6 to 6
- attn_gain: bfloat16 [1024], replicated, may hold values from 0.5 to 1.5
- w_query: bfloat16 [1024, 512], P('shard'), may hold values from -0.1875 to 0.1875
- w_key: bfloat16 [1024, 512], P('shard'), may hold values from -0.1875 to 0.1875
- w_value: bfloat16 [1024, 1024], P('shard'), may hold values from -0.1875 to 0.1875
- w_outgate: bfloat16 [1024, 1024], P('shard'), may hold values from -0.1875 to 0.1875
- w_rank_in: bfloat16 [1024, 16], P('shard'), may hold values from -0.1875 to 0.1875
- w_rank_out: bfloat16 [512, 16], P('shard'), may hold values from -1.5 to 1.5
- fgate_bias: bfloat16 [512], replicated, may hold values from -1 to 11
- head_gain: bfloat16 [256], replicated, may hold values from 0.5 to 1.5
- w_output: bfloat16 [1024, 1024], P('shard'), may hold values from -0.1875 to 0.1875
- ffn_gain: bfloat16 [1024], replicated, may hold values from 0.5 to 1.5
- w_gate: bfloat16 [1024, 2816], P('shard'), may hold values from -0.1875 to 0.1875
- w_up: bfloat16 [1024, 2816], P('shard'), may hold values from -0.1875 to 0.1875
- w_down: bfloat16 [2816, 1024], P('shard'), may hold values from -0.109375 to 0.109375
- out_grad: bfloat16 [16, 1024, 1024], P('rep', 'shard'), may hold values from -6 to 6
Outputs:
- block_out: bfloat16 [16, 1024, 1024], P('rep', 'shard')
- tokens_grad: bfloat16 [16, 1024, 1024], P('rep', 'shard')
- attn_gain_grad: float32 [1024], replicated
- w_query_grad: float32 [1024, 512], P('shard')
- w_key_grad: float32 [1024, 512], P('shard')
- w_value_grad: float32 [1024, 1024], P('shard')
- w_outgate_grad: float32 [1024, 1024], P('shard')
- w_rank_in_grad: float32 [1024, 16], P('shard')
- w_rank_out_grad: float32 [512, 16], P('shard')
- fgate_bias_grad: float32 [512], replicated
- head_gain_grad: float32 [256], replicated
- w_output_grad: float32 [1024, 1024], P('shard')
- ffn_gain_grad: float32 [1024], replicated
- w_gate_grad: float32 [1024, 2816], P('shard')
- w_up_grad: float32 [1024, 2816], P('shard')
- w_down_grad: float32 [2816, 1024], P('shard')
All inputs are finite; a program needn't handle non-finite values.
Results may differ from a plain program's by a relative error of at most 0.009.
The roundings to bfloat16 on the way count: a program that leaves them out, or rounds other values in their place, can miss the bound.
Values may be sent and summed in bfloat16 or wider, within the bound.
No kernel may reach another device: no remote copies, remote signals or barrier semaphores. Data moves between devices by JAX's collectives and lax.ppermute only.
A program may use at most 384 MiB of HBM per device.

v0:
```python
import jax
import jax.numpy as jnp
from jax import lax
from jax.sharding import PartitionSpec as P

HEADS = 4
KD = 512
VD = 1024
SPAN = 64
DK = 128
DV = 256


PRECISE = lax.Precision.HIGHEST
EPSILON = 1e-06
GATE_NORM = 16.0


def entering(part, axis, combine, identity, reverse):
    count = lax.axis_size(axis)
    place = lax.axis_index(axis)
    ahead = count - 1 - place if reverse else place
    gathered = jax.tree.map(lambda a: lax.all_gather(a, axis), part)
    state = jax.tree.map(lambda a, e: jnp.zeros_like(a) + jnp.asarray(e, a.dtype), part, identity)

    def one(hop, state):
        source = count - 1 - hop if reverse else hop
        return combine(
            state, jax.tree.map(lambda a: lax.dynamic_index_in_dim(a, source, 0, False), gathered)
        )

    return lax.fori_loop(0, ahead, one, state)


def product(left_side, right_side):
    return jnp.dot(left_side, right_side, preferred_element_type=jnp.float32)


def times_transpose(left_side, right_side):
    return lax.dot_general(
        left_side, right_side, (((1,), (1,)), ((), ())), preferred_element_type=jnp.float32
    )


def outer_sum(left_side, right_side):
    return lax.dot_general(
        left_side, right_side, (((0,), (0,)), ((), ())), preferred_element_type=jnp.float32
    )


def root_norm(values, gain_row):
    return (
        values * lax.rsqrt(jnp.mean(values * values, axis=-1, keepdims=True) + EPSILON) * gain_row
    )


def gated_heads(mixed_rows, gain_row, out_gate):
    heads_normed = root_norm(mixed_rows, gain_row)
    return (heads_normed * jax.nn.silu(out_gate.reshape(mixed_rows.shape))).reshape(out_gate.shape)


def silu_product(gate_rows, up_rows):
    return jax.nn.silu(gate_rows) * up_rows


def forget_log(logits):
    return jax.nn.log_sigmoid(logits) / GATE_NORM


def chain_link(earlier, later):
    return (earlier[0] * later[0], later[0][..., None] * earlier[1] + later[1])


def local_mixing(queries, key_rows, value_rows, decays, start_state):
    cumulated = jnp.cumsum(decays, axis=2)
    closing = cumulated[:, :, -1]
    causal_mask = jnp.arange(SPAN)[:, None] >= jnp.arange(SPAN)[None, :]
    differences = cumulated[:, :, :, None] - cumulated[:, :, None, :]
    differences = jnp.where(causal_mask[:, :, None, None], differences, 0.0)
    weights = jnp.exp(differences)
    scores = jnp.einsum("bntha,bnsha,bntsha->bnhts", queries, key_rows, weights, precision=PRECISE)
    scores = jnp.where(causal_mask, scores, 0.0)
    query_scaled = queries * jnp.exp(cumulated)
    key_tail = key_rows * jnp.exp(closing[:, :, None] - cumulated)
    inner = jnp.einsum("bnhts,bnshe->bnthe", scores, value_rows, precision=PRECISE)
    pieces = jnp.einsum("bnsha,bnshe->nbhae", key_tail, value_rows, precision=PRECISE)
    rates = jnp.exp(jnp.moveaxis(closing, 1, 0))

    def advance(carried, item):
        piece, rate = item
        return (rate[..., None] * carried + piece, carried)

    final_state, starts = lax.scan(advance, start_state, (pieces, rates))
    carried_part = jnp.einsum("bntha,nbhae->bnthe", query_scaled, starts, precision=PRECISE)
    return (inner + carried_part, final_state)


def body(
    tokens,
    attn_gain,
    w_query,
    w_key,
    w_value,
    w_outgate,
    w_rank_in,
    w_rank_out,
    fgate_bias,
    head_gain,
    w_output,
    ffn_gain,
    w_gate,
    w_up,
    w_down,
    out_grad,
):
    seqs, tok_dev, width = tokens.shape
    blocks = tok_dev // SPAN
    count = seqs * tok_dev
    gathered = (
        lax.all_gather(w_query, "shard", axis=0, tiled=True),
        lax.all_gather(w_key, "shard", axis=0, tiled=True),
        lax.all_gather(w_value, "shard", axis=0, tiled=True),
        lax.all_gather(w_outgate, "shard", axis=0, tiled=True),
        lax.all_gather(w_rank_in, "shard", axis=0, tiled=True),
        lax.all_gather(w_rank_out, "shard", axis=0, tiled=True),
        lax.all_gather(w_output, "shard", axis=0, tiled=True),
        lax.all_gather(w_gate, "shard", axis=0, tiled=True),
        lax.all_gather(w_up, "shard", axis=0, tiled=True),
        lax.all_gather(w_down, "shard", axis=0, tiled=True),
    )
    (
        query_full,
        key_full,
        value_full,
        outgate_full,
        rank_in_full,
        rank_out_full,
        output_full,
        gate_full,
        up_full,
        down_full,
    ) = gathered
    inputs = tokens.reshape(count, width).astype(jnp.float32)
    normed, norm_back = jax.vjp(root_norm, inputs, attn_gain.astype(jnp.float32))
    normed_low = normed.astype(jnp.bfloat16)
    queries = product(normed_low, query_full).astype(jnp.bfloat16)
    key_rows = product(normed_low, key_full).astype(jnp.bfloat16)
    value_rows = product(normed_low, value_full).astype(jnp.bfloat16)
    out_gate = product(normed_low, outgate_full)
    rank_rows = product(normed_low, rank_in_full).astype(jnp.bfloat16)
    logits = times_transpose(rank_rows, rank_out_full) + fgate_bias.astype(jnp.float32)
    decays, gate_back = jax.vjp(forget_log, logits)
    shape_key = (seqs, blocks, SPAN, HEADS, DK)
    shape_value = (seqs, blocks, SPAN, HEADS, DV)
    query_blocks = queries.astype(jnp.float32).reshape(shape_key)
    key_blocks = key_rows.astype(jnp.float32).reshape(shape_key)
    value_blocks = value_rows.astype(jnp.float32).reshape(shape_value)
    decay_blocks = decays.reshape(shape_key)
    cumulated = jnp.cumsum(decay_blocks, axis=2)
    block_total = cumulated[:, :, -1]
    running = jnp.cumsum(block_total, axis=1)
    preceding = running - block_total
    device_total = running[:, -1]
    tail_keys = key_blocks * jnp.exp(
        device_total[:, None, None] - preceding[:, :, None] - cumulated
    )
    local_end = jnp.einsum("bntha,bnthe->bhae", tail_keys, value_blocks, precision=PRECISE)
    total_rate = jnp.exp(device_total)
    unit_rate = jnp.ones_like(total_rate)
    scanned = entering(
        (total_rate, local_end), "shard", chain_link, (unit_rate, jnp.zeros_like(local_end)), False
    )
    (mixed, final_state), mix_back = jax.vjp(
        local_mixing, query_blocks, key_blocks, value_blocks, decay_blocks, scanned[1]
    )
    mixed_rows = mixed.reshape(count, HEADS, DV)
    gated, gated_back = jax.vjp(gated_heads, mixed_rows, head_gain.astype(jnp.float32), out_gate)
    gated_low = gated.astype(jnp.bfloat16)
    residual = inputs + product(gated_low, output_full)
    normed_ffn, ffn_norm_back = jax.vjp(root_norm, residual, ffn_gain.astype(jnp.float32))
    ffn_input = normed_ffn.astype(jnp.bfloat16)
    gate_rows = product(ffn_input, gate_full)
    up_rows = product(ffn_input, up_full)
    hidden, act_back = jax.vjp(silu_product, gate_rows, up_rows)
    hidden_low = hidden.astype(jnp.bfloat16)
    block_out = (residual + product(hidden_low, down_full)).astype(jnp.bfloat16)
    grad_rows = out_grad.reshape(count, width)
    down_grad = outer_sum(hidden_low, grad_rows)
    hidden_grad = times_transpose(grad_rows, down_full)
    gate_grad, up_grad = act_back(hidden_grad)
    gate_grad_low = gate_grad.astype(jnp.bfloat16)
    up_grad_low = up_grad.astype(jnp.bfloat16)
    gate_w_grad = outer_sum(ffn_input, gate_grad_low)
    up_w_grad = outer_sum(ffn_input, up_grad_low)
    ffn_input_grad = times_transpose(gate_grad_low, gate_full) + times_transpose(
        up_grad_low, up_full
    )
    residual_part, ffn_gain_grad = ffn_norm_back(ffn_input_grad)
    residual_grad = grad_rows.astype(jnp.float32) + residual_part
    branch_grad = residual_grad.astype(jnp.bfloat16)
    output_w_grad = outer_sum(gated_low, branch_grad)
    gated_grad = times_transpose(branch_grad, output_full)
    mixed_grad, head_gain_grad, out_gate_grad = gated_back(gated_grad)
    mixed_grad_blocks = mixed_grad.reshape(shape_value)
    early_queries = query_blocks * jnp.exp(preceding[:, :, None] + cumulated)
    back_part = jnp.einsum("bntha,bnthe->bhae", early_queries, mixed_grad_blocks, precision=PRECISE)
    rescanned = entering(
        (total_rate, back_part), "shard", chain_link, (unit_rate, jnp.zeros_like(back_part)), True
    )
    pulled = mix_back((mixed_grad_blocks, rescanned[1]))
    query_grad_low = pulled[0].reshape(count, KD).astype(jnp.bfloat16)
    key_grad_low = pulled[1].reshape(count, KD).astype(jnp.bfloat16)
    value_grad_low = pulled[2].reshape(count, VD).astype(jnp.bfloat16)
    logit_grad = gate_back(pulled[3].reshape(count, KD))[0]
    logit_grad_low = logit_grad.astype(jnp.bfloat16)
    out_gate_low = out_gate_grad.astype(jnp.bfloat16)
    bias_grad = jnp.sum(logit_grad_low.astype(jnp.float32), axis=0)
    rank_out_grad = outer_sum(logit_grad_low, rank_rows)
    rank_grad_low = product(logit_grad_low, rank_out_full).astype(jnp.bfloat16)
    rank_in_grad = outer_sum(normed_low, rank_grad_low)
    query_w_grad = outer_sum(normed_low, query_grad_low)
    key_w_grad = outer_sum(normed_low, key_grad_low)
    value_w_grad = outer_sum(normed_low, value_grad_low)
    outgate_w_grad = outer_sum(normed_low, out_gate_low)
    normed_grad = (
        times_transpose(query_grad_low, query_full)
        + times_transpose(key_grad_low, key_full)
        + times_transpose(value_grad_low, value_full)
        + times_transpose(out_gate_low, outgate_full)
        + times_transpose(rank_grad_low, rank_in_full)
    )
    input_part, attn_gain_grad = norm_back(normed_grad)
    tokens_grad = (residual_grad + input_part).astype(jnp.bfloat16).reshape(tokens.shape)
    matrices = (
        query_w_grad,
        key_w_grad,
        value_w_grad,
        outgate_w_grad,
        rank_in_grad,
        rank_out_grad,
        output_w_grad,
        gate_w_grad,
        up_w_grad,
        down_grad,
    )
    owned = (
        lax.psum_scatter(matrices[0], "shard", scatter_dimension=0, tiled=True),
        lax.psum_scatter(matrices[1], "shard", scatter_dimension=0, tiled=True),
        lax.psum_scatter(matrices[2], "shard", scatter_dimension=0, tiled=True),
        lax.psum_scatter(matrices[3], "shard", scatter_dimension=0, tiled=True),
        lax.psum_scatter(matrices[4], "shard", scatter_dimension=0, tiled=True),
        lax.psum_scatter(matrices[5], "shard", scatter_dimension=0, tiled=True),
        lax.psum_scatter(matrices[6], "shard", scatter_dimension=0, tiled=True),
        lax.psum_scatter(matrices[7], "shard", scatter_dimension=0, tiled=True),
        lax.psum_scatter(matrices[8], "shard", scatter_dimension=0, tiled=True),
        lax.psum_scatter(matrices[9], "shard", scatter_dimension=0, tiled=True),
    )
    owned = lax.psum(
        (
            owned[0],
            owned[1],
            owned[2],
            owned[3],
            owned[4],
            owned[5],
            owned[6],
            owned[7],
            owned[8],
            owned[9],
        ),
        "rep",
    )
    small = lax.psum((attn_gain_grad, bias_grad, head_gain_grad, ffn_gain_grad), ("shard", "rep"))
    return (
        block_out.reshape(tokens.shape),
        tokens_grad,
        small[0],
        owned[0],
        owned[1],
        owned[2],
        owned[3],
        owned[4],
        owned[5],
        small[1],
        small[2],
        owned[6],
        small[3],
        owned[7],
        owned[8],
        owned[9],
    )


def solution(mesh):
    in_specs = (
        P("rep", "shard", None),
        P(),
        P("shard", None),
        P("shard", None),
        P("shard", None),
        P("shard", None),
        P("shard", None),
        P("shard", None),
        P(),
        P(),
        P("shard", None),
        P(),
        P("shard", None),
        P("shard", None),
        P("shard", None),
        P("rep", "shard", None),
    )
    out_specs = (
        P("rep", "shard", None),
        P("rep", "shard", None),
        P(),
        P("shard", None),
        P("shard", None),
        P("shard", None),
        P("shard", None),
        P("shard", None),
        P("shard", None),
        P(),
        P(),
        P("shard", None),
        P(),
        P("shard", None),
        P("shard", None),
        P("shard", None),
    )
    return jax.shard_map(body, mesh=mesh, in_specs=in_specs, out_specs=out_specs, check_vma=False)
```

profile of v0, /device:TPU:0, one launch (start us, length us, event | category | flops | bytes accessed | tf_op | source)
XLA Modules:
  0.0 2281.2 jit_solution(13749352053330989199)
XLA Ops:
  12.2 28.1 %all_gather.49 = bf16[1024,16]{0,1:T(8,128)(2,1)S(1)} all-gather(bf16[128,16]{0,1:T(8,128)(2,1)} %param.30), channel_id=1, replica_groups=mesh['shard'=8,'rep'=4] {'shard'}, dimensions={0}, use_global_device_ids=true | all-gather | bytes 36864 | tf_op jit(solution)/shard_map/all_gather | solution.py:124
  40.3 30.7 %all-gather.3 = bf16[8,64,16]{1,2,0:T(8,128)(2,1)S(1)} all-gather(bf16[1,64,16]{1,2,0:T(8,128)(2,1)} %bitcast.328), channel_id=1, replica_groups=mesh['shard'=8,'rep'=4] {'shard'}, dimensions={0}, use_global_device_ids=true | all-gather | bytes 18432 | tf_op jit(solution)/shard_map/all_gather | solution.py:125
  81.9 12.6 all-gather.19.cloned.1.call-done
  101.4 43.3 %all-gather.15.cloned.1.call-done = bf16[1024,1024]{1,0:T(8,128)(2,1)} async-done(((bf16[128,1024]{1,0:T(8,128)(2,1)}), bf16[1024,1024]{1,0:T(8,128)(2,1)}) %all-gather.15.cloned.1.call-update) | async-done | bytes 2097168 | tf_op jit(solution)/shard_map/all_gather | solution.py:122
  144.7 4.1 convolution_convert_fusion
  158.4 31.1 %all-gather = f32[32,1,4,128]{3,2,1,0:T(4,128)S(1)} all-gather(f32[4,1,4,128]{3,2,1,0:T(4,128)S(1)} %get-tuple-element.445), channel_id=2, replica_groups=mesh['shard'=8,'rep'=4] {'shard'}, dimensions={0}, use_global_device_ids=true | all-gather | bytes 73728 | tf_op jit(solution)/shard_map/all_gather | solution.py:23
  193.7 23.3 %fusion.2 = f32[4,2,4,64,64]{4,2,3,1,0:T(4,128)} fusion(f32[4,2,4,128,64]{3,2,4,1,0:T(4,128)} %copy.204, f32[4,2,4,128,64]{3,4,2,1,0:T(8,128)} %convert_bitcast_fusion.1, f32[4,2,64,4,128]{4,2,3,1,0:T(8,128)S(1)} %copy-done.45, f32[4,2,64,4,128]{4,3,2,1,0:T(4,128)S(1)} %copy-done.21, pred[64,64]{1,0:T(8,128)(4,1)S(1)} %iota_compare_fusion), kind=kLoop, calls=%fused_computation.17 | loop fusion | flops 83755008 | bytes 4722688
  217.0 4.0 copy.219
  224.9 198.3 %all-gather.31.cloned.1.call-done = f32[32,4,128,256]{3,2,1,0:T(8,128)} async-done(((f32[4,4,128,256]{3,2,1,0:T(8,128)}), f32[32,4,128,256]{3,2,1,0:T(8,128)}) %all-gather.31.cloned.1.call-update) | async-done | bytes 16777232 | tf_op jit(solution)/shard_map/all_gather | solution.py:23
  426.4 7.1 while.59
  433.6 5.1 fusion.18
  444.7 5.4 multiply_convert_fusion.3
  450.1 22.7 all-gather.23.cloned.1.call-done
  477.7 88.5 %all-gather.25.cloned.1.call-done = bf16[1024,2816]{1,0:T(8,128)(2,1)} async-done(((bf16[128,2816]{1,0:T(8,128)(2,1)}), bf16[1024,2816]{1,0:T(8,128)(2,1)}) %all-gather.25.cloned.1.call-update) | async-done | bytes 5767184 | tf_op jit(solution)/shard_map/all_gather | solution.py:127
  566.2 7.6 fusion.113
  573.8 85.5 %all-gather.27.cloned.1.call-done = bf16[1024,2816]{1,0:T(8,128)(2,1)} async-done(((bf16[128,2816]{1,0:T(8,128)(2,1)}), bf16[1024,2816]{1,0:T(8,128)(2,1)}) %all-gather.27.cloned.1.call-update) | async-done | bytes 5767184 | tf_op jit(solution)/shard_map/all_gather | solution.py:128
  659.2 7.5 fusion.114
  666.7 85.5 %all-gather.29.cloned.1.call-done = bf16[2816,1024]{1,0:T(8,128)(2,1)} async-done(((bf16[352,1024]{1,0:T(8,128)(2,1)}), bf16[2816,1024]{1,0:T(8,128)(2,1)}) %all-gather.29.cloned.1.call-update) | async-done | bytes 5767184 | tf_op jit(solution)/shard_map/all_gather | solution.py:129
  752.3 11.2 multiply_convert_fusion
  763.5 7.3 fusion.115
  785.8 5.2 fusion.45
  791.1 5.1 fusion.96
  796.3 5.3 fusion.119
  801.6 9.6 fusion.120
  811.3 9.5 fusion.121
  820.9 9.6 fusion.122
  838.8 5.2 fusion.40
  844.0 28.1 %fusion.7 = f32[4,2,4,128,64]{3,2,4,1,0:T(4,128)} fusion(f32[4,2,4,128,64]{3,4,2,1,0:T(8,128)} %copy.282, f32[4,2,4,64,64]{4,2,3,1,0:T(4,128)} %copy.228, f32[4,2,64,4,128]{4,2,3,1,0:T(8,128)} %get-tuple-element.443, f32[4,2,64,4,128]{4,3,2,1,0:T(4,128)} %copy-done.20, pred[64,64]{1,0:T(8,128)(4,1)S(1)} %iota_compare_fusion), kind=kLoop, calls=%fused_computation.24 | loop fusion | flops 83623936 | bytes 4722688
  872.2 21.8 fusion.6
  893.9 33.8 %fusion.9 = (f32[4,2,64,4,128]{4,2,3,1,0:T(8,128)}, f32[4,2,64,4,128]{4,3,2,1,0:T(4,128)}) fusion(f32[4,2,64,64,4]{3,4,2,1,0:T(4,128)} %copy.242, f32[4,2,4,128,64]{3,2,4,1,0:T(4,128)} %copy.204, f32[4,2,4,128,64]{3,4,2,1,0:T(8,128)} %convert_bitcast_fusion.1, f32[4,2,64,4,128]{4,2,3,1,0:T(8,128)S(1)} %copy-done.46, f32[4,2,64,4,128]{4,3,2,1,0:T(4,128)S(1)} %copy-done.22, ...), kind=kLoop, calls=%fused_computation.28 | loop fusion | flops 133693440 | bytes 6819840 | tf_op jit(solution)/shard_map/transpose(jvp())/reduce_sum | solution.py:78
  927.8 89.2 %all-gather.33.cloned.1.call-done = f32[32,4,128,256]{3,2,1,0:T(8,128)} async-done(((f32[4,4,128,256]{3,2,1,0:T(8,128)}), f32[32,4,128,256]{3,2,1,0:T(8,128)}) %all-gather.33.cloned.1.call-update) | async-done | bytes 16777232 | tf_op jit(solution)/shard_map/all_gather | solution.py:23
  1017.2 19.9 while.60
  1039.6 11.6 while.61
  1051.3 5.5 fusion.87
  1056.8 7.6 fusion.65
  1090.5 16.2 reduce-scatter.23.cloned.1.call-done
  1106.7 91.6 %reduce-scatter.19.cloned.1.call-done = f32[128,1024]{1,0:T(8,128)} async-done(((f32[1024,1024]{1,0:T(8,128)}), f32[128,1024]{1,0:T(8,128)}) %reduce-scatter.19.cloned.1.call-update) | async-done | bytes 524304 | tf_op jit(solution)/shard_map/reduce_scatter | solution.py:250
  1198.4 196.1 %reduce-scatter.25.cloned.1.call-done = f32[128,2816]{1,0:T(8,128)} async-done(((f32[1024,2816]{1,0:T(8,128)}), f32[128,2816]{1,0:T(8,128)}) %reduce-scatter.25.cloned.1.call-update) | async-done | bytes 1441808 | tf_op jit(solution)/shard_map/reduce_scatter | solution.py:254
  1394.4 195.2 %reduce-scatter.27.cloned.1.call-done = f32[128,2816]{1,0:T(8,128)} async-done(((f32[1024,2816]{1,0:T(8,128)}), f32[128,2816]{1,0:T(8,128)}) %reduce-scatter.27.cloned.1.call-update) | async-done | bytes 1441808 | tf_op jit(solution)/shard_map/reduce_scatter | solution.py:255
  1589.6 195.2 %reduce-scatter.29.cloned.1.call-done = f32[352,1024]{1,0:T(8,128)} async-done(((f32[2816,1024]{1,0:T(8,128)}), f32[352,1024]{1,0:T(8,128)}) %reduce-scatter.29.cloned.1.call-update) | async-done | bytes 1441808 | tf_op jit(solution)/shard_map/reduce_scatter | solution.py:256
  1784.9 70.4 %reduce-scatter.13.cloned.1.call-done = f32[128,512]{1,0:T(8,128)} async-done(((f32[1024,512]{1,0:T(8,128)}), f32[128,512]{1,0:T(8,128)}) %reduce-scatter.13.cloned.1.call-update) | async-done | bytes 262160 | tf_op jit(solution)/shard_map/reduce_scatter | solution.py:247
  1855.3 70.0 %reduce-scatter.15.cloned.1.call-done = f32[128,512]{1,0:T(8,128)} async-done(((f32[1024,512]{1,0:T(8,128)}), f32[128,512]{1,0:T(8,128)}) %reduce-scatter.15.cloned.1.call-update) | async-done | bytes 262160 | tf_op jit(solution)/shard_map/reduce_scatter | solution.py:248
  1925.3 90.4 %reduce-scatter.17.cloned.1.call-done = f32[128,1024]{1,0:T(8,128)} async-done(((f32[1024,1024]{1,0:T(8,128)}), f32[128,1024]{1,0:T(8,128)}) %reduce-scatter.17.cloned.1.call-update) | async-done | bytes 524304 | tf_op jit(solution)/shard_map/reduce_scatter | solution.py:249
  2020.0 6.9 add_convert_fusion
  2033.8 40.5 %all-reduce.1 = (f32[1024]{0:T(1024)}, f32[512]{0:T(512)}, f32[256]{0:T(256)}, f32[1024]{0:T(1024)}) all-reduce(f32[1024]{0:T(1024)S(1)} %get-tuple-element.361, f32[512]{0:T(512)S(1)} %get-tuple-element.423, f32[256]{0:T(256)S(1)} %get-tuple-element.359, ...), channel_id=1, replica_groups=mesh['shard'=8,'rep'=4] {'shard','rep'}, use_global_device_ids=true, to_apply=%region_22.23 | all-reduce | flops 2816 | bytes 22528 | tf_op jit(solution)/shard_map/psum | solution.py:273
  2081.8 55.8 %reduce-scatter.21.cloned.1.call-done = f32[128,16]{0,1:T(8,128)} async-done(((f32[1024,16]{0,1:T(8,128)}), f32[128,16]{0,1:T(8,128)}) %reduce-scatter.21.cloned.1.call-update) | async-done | bytes 8208 | tf_op jit(solution)/shard_map/reduce_scatter | solution.py:251
  2137.6 10.7 all-reduce.2
  2148.4 114.5 %all-reduce.6.cloned.1.call-done = (f32[128,512]{1,0:T(8,128)}, f32[128,512]{1,0:T(8,128)}, f32[128,1024]{1,0:T(8,128)}, f32[128,1024]{1,0:T(8,128)}, f32[128,10...) async-done(((f32[128,512]{1,0:T(8,128)}, f32[128,512]{1,0:T(8,128)}, f32[128,1024]{1,0:T(8,128)}, f32[128,1024]{1,0:T(8,128)}, ...) | async-done | bytes 6422544 | tf_op jit(solution)/shard_map/psum | solution.py:258
  (321 shorter events, 174.0 us)
Async XLA Ops:
  7.2 65.2 %copy-start.5 = (bf16[4,128,1024]{2,1,0:T(8,128)(2,1)S(1)}, bf16[4,128,1024]{2,1,0:T(8,128)(2,1)}, u32[]{:S(2)}) copy-start(bf16[4,128,1024]{2,1,0:T(8,128)(2,1)} %param.24) | copy-start | bytes 3145732
  7.2 70.5 %all-gather.17.cloned.1.call-start = ((), (), s32[]{:S(2)}) async-start(), calls=%async_computation.11 | async-start | bytes 1179648 | tf_op jit(solution)/shard_map/all_gather | solution.py:121
  7.9 86.6 %all-gather.19.cloned.1.call-start = ((), (), s32[]{:S(2)}) async-start(), calls=%async_computation.12 | async-start | bytes 1179648 | tf_op jit(solution)/shard_map/all_gather | solution.py:120
  8.7 136.1 %all-gather.15.cloned.1.call-start = ((), (), s32[]{:S(2)}) async-start(), calls=%async_computation.10 | async-start | bytes 2359296 | tf_op jit(solution)/shard_map/all_gather | solution.py:122
  9.4 207.6 %all-gather.21.cloned.1.call-start = ((), (), s32[]{:S(2)}) async-start(), calls=%async_computation.13 | async-start | bytes 2359296 | tf_op jit(solution)/shard_map/all_gather | solution.py:123
  10.0 413.2 %all-gather.31.cloned.1.call-start = ((), (), s32[]{:S(2)}) async-start(), calls=%async_computation.27 | async-start | bytes 18874368 | tf_op jit(solution)/shard_map/all_gather | solution.py:23
  11.5 146.8 %copy-start.65 = (f32[4,128]{1,0:T(4,128)}, f32[4,128]{1,0:T(4,128)S(1)}, u32[]{:S(2)}) copy-start(f32[4,128]{1,0:T(4,128)S(1)} %fusion.31) | copy-start | bytes 6148
  12.2 177.2 %copy-start.57 = (f32[1024]{0:T(1024)}, f32[1024]{0:T(1024)S(1)}, u32[]{:S(2)}) copy-start(f32[1024]{0:T(1024)S(1)} %convert_element_type.123) | copy-start | bytes 12292
  40.3 32.4 %copy-start.53 = (bf16[1024,16]{0,1:T(8,128)(2,1)}, bf16[1024,16]{0,1:T(8,128)(2,1)S(1)}, u32[]{:S(2)}) copy-start(bf16[1024,16]{0,1:T(8,128)(2,1)S(1)} %all_gather.49) | copy-start | bytes 98308
  77.6 21.1 copy-start.20
  77.7 21.1 copy-start.55
  81.9 108.8 %copy-start.13 = (bf16[4,2,64,4,128]{4,3,2,1,0:T(4,128)(2,1)}, bf16[4,2,64,4,128]{4,3,2,1,0:T(4,128)(2,1)S(1)}, u32[]{:S(2)}) copy-start(bf16[4,2,64,4,128]{4,3,2,1,0:T(4,128)(2,1)S(1)} %reshape.260) | copy-start | bytes 1572868
  98.7 93.2 %copy-start.24 = (bf16[4,2,64,4,128]{4,3,2,1,0:T(4,128)(2,1)}, bf16[4,2,64,4,128]{4,3,2,1,0:T(4,128)(2,1)S(1)}, u32[]{:S(2)}) copy-start(bf16[4,2,64,4,128]{4,3,2,1,0:T(4,128)(2,1)S(1)} %reshape.261) | copy-start | bytes 1572868
  150.7 70.3 %copy-start.8 = (bf16[4,2,64,4,256]{4,3,2,1,0:T(4,128)(2,1)}, bf16[4,2,64,4,256]{4,3,2,1,0:T(4,128)(2,1)S(1)}, u32[]{:S(2)}) copy-start(bf16[4,2,64,4,256]{4,3,2,1,0:T(4,128)(2,1)S(1)} %reshape.258) | copy-start | bytes 3145732
  154.7 318.1 %all-gather.23.cloned.1.call-start = ((), (), s32[]{:S(2)}) async-start(), calls=%async_computation.14 | async-start | bytes 2359296 | tf_op jit(solution)/shard_map/all_gather | solution.py:126
  155.3 35.5 %copy-start.70 = (bf16[256]{0:T(256)(128)(2,1)S(1)}, bf16[256]{0:T(256)(128)(2,1)}, u32[]{:S(2)}) copy-start(bf16[256]{0:T(256)(128)(2,1)} %param.33) | copy-start | bytes 1540
  155.3 35.5 %copy-start.67 = (bf16[1024]{0:T(1024)(128)(2,1)S(1)}, bf16[1024]{0:T(1024)(128)(2,1)}, u32[]{:S(2)}) copy-start(bf16[1024]{0:T(1024)(128)(2,1)} %param.35) | copy-start | bytes 6148
  155.3 410.9 %all-gather.25.cloned.1.call-start = ((), (), s32[]{:S(2)}) async-start(), calls=%async_computation.15 | async-start | bytes 6488064 | tf_op jit(solution)/shard_map/all_gather | solution.py:127
  156.1 503.2 %all-gather.27.cloned.1.call-start = ((), (), s32[]{:S(2)}) async-start(), calls=%async_computation.16 | async-start | bytes 6488064 | tf_op jit(solution)/shard_map/all_gather | solution.py:128
  156.8 595.5 %all-gather.29.cloned.1.call-start = ((), (), s32[]{:S(2)}) async-start(), calls=%async_computation.17 | async-start | bytes 6488064 | tf_op jit(solution)/shard_map/all_gather | solution.py:129
  157.5 859.4 %all-gather.33.cloned.1.call-start = ((), (), s32[]{:S(2)}) async-start(), calls=%async_computation.28 | async-start | bytes 18874368 | tf_op jit(solution)/shard_map/all_gather | solution.py:23
  477.7 181.6 %copy-start.48 = (bf16[512,1024]{1,0:T(8,128)(2,1)}, bf16[512,1024]{1,0:T(8,128)(2,1)S(1)}, u32[]{:S(2)}) copy-start(bf16[512,1024]{1,0:T(8,128)(2,1)S(1)} %multiply_convert_fusion.2) | copy-start | bytes 3145732
  573.8 178.5 %copy-start.49 = (bf16[4,128,1024]{2,1,0:T(8,128)(2,1)S(1)}, bf16[4,128,1024]{2,1,0:T(8,128)(2,1)}, u32[]{:S(2)}) copy-start(bf16[4,128,1024]{2,1,0:T(8,128)(2,1)} %param.39) | copy-start | bytes 3145732
  763.4 7.4 copy-start.72
  763.4 7.4 copy-start.71
  763.4 7.4 copy-start.18
  763.5 7.4 copy-start.68
  785.8 53.1 %copy-start.2 = (f32[512,4,256]{2,0,1:T(8,128)}, f32[512,4,256]{2,0,1:T(8,128)S(1)}, u32[]{:S(2)}) copy-start(f32[512,4,256]{2,0,1:T(8,128)S(1)} %copy.223) | copy-start | bytes 6291460
  791.0 315.7 %reduce-scatter.23.cloned.1.call-start = ((), (), s32[]{:S(2)}) async-start(), calls=%async_computation.23 | async-start | bytes 4718592 | tf_op jit(solution)/shard_map/reduce_scatter | solution.py:253
  796.2 402.1 %reduce-scatter.19.cloned.1.call-start = ((), (), s32[]{:S(2)}) async-start(), calls=%async_computation.21 | async-start | bytes 4718592 | tf_op jit(solution)/shard_map/reduce_scatter | solution.py:250
  801.6 592.8 %reduce-scatter.25.cloned.1.call-start = ((), (), s32[]{:S(2)}) async-start(), calls=%async_computation.24 | async-start | bytes 12976128 | tf_op jit(solution)/shard_map/reduce_scatter | solution.py:254
  811.2 778.4 %reduce-scatter.27.cloned.1.call-start = ((), (), s32[]{:S(2)}) async-start(), calls=%async_computation.25 | async-start | bytes 12976128 | tf_op jit(solution)/shard_map/reduce_scatter | solution.py:255
  820.9 964.0 %reduce-scatter.29.cloned.1.call-start = ((), (), s32[]{:S(2)}) async-start(), calls=%async_computation.26 | async-start | bytes 12976128 | tf_op jit(solution)/shard_map/reduce_scatter | solution.py:256
  830.5 1024.8 %reduce-scatter.13.cloned.1.call-start = ((), (), s32[]{:S(2)}) async-start(), calls=%async_computation.18 | async-start | bytes 2359296 | tf_op jit(solution)/shard_map/reduce_scatter | solution.py:247
  844.0 28.1 %copy-start.22 = (f32[4,2,64,4,128]{4,3,2,1,0:T(4,128)S(1)}, f32[4,2,64,4,128]{4,3,2,1,0:T(4,128)}, u32[]{:S(2)}) copy-start(f32[4,2,64,4,128]{4,3,2,1,0:T(4,128)} %copy-done.20) | copy-start | bytes 3145732
  844.0 28.1 %copy-start.46 = (f32[4,2,64,4,128]{4,2,3,1,0:T(8,128)S(1)}, f32[4,2,64,4,128]{4,2,3,1,0:T(8,128)}, u32[]{:S(2)}) copy-start(f32[4,2,64,4,128]{4,2,3,1,0:T(8,128)} %get-tuple-element.443) | copy-start | bytes 3145732
  1039.6 11.6 copy-start.56
  1056.8 8.8 copy-start.11
  1067.8 857.5 %reduce-scatter.15.cloned.1.call-start = ((), (), s32[]{:S(2)}) async-start(), calls=%async_computation.19 | async-start | bytes 2359296 | tf_op jit(solution)/shard_map/reduce_scatter | solution.py:248
  1072.2 943.6 %reduce-scatter.17.cloned.1.call-start = ((), (), s32[]{:S(2)}) async-start(), calls=%async_computation.20 | async-start | bytes 4718592 | tf_op jit(solution)/shard_map/reduce_scatter | solution.py:249
  1083.0 998.0 %reduce-scatter.31.cloned.1.call-start = ((), (), s32[]{:S(2)}) async-start(), calls=%async_computation.29 | async-start | bytes 294912
  1089.2 1048.4 %reduce-scatter.21.cloned.1.call-start = ((), (), s32[]{:S(2)}) async-start(), calls=%async_computation.22 | async-start | bytes 73728 | tf_op jit(solution)/shard_map/reduce_scatter | solution.py:251
  1090.2 1172.7 %all-reduce.6.cloned.1.call-start = ((), (), s32[]{:S(2)}) async-start(), calls=%async_computation.30 | async-start | bytes 12845056 | tf_op jit(solution)/shard_map/psum | solution.py:258
  2020.0 6.9 copy-start.35
  2020.0 6.9 copy-start.42
  2031.2 43.0 %copy-start.66 = (f32[4,128]{1,0:T(4,128)S(1)}, f32[4,128]{1,0:T(4,128)}, u32[]{:S(2)}) copy-start(f32[4,128]{1,0:T(4,128)} %copy-done.65) | copy-start | bytes 6148
  2031.2 43.0 %copy-start.16 = (f32[512,1024]{1,0:T(8,128)S(1)}, f32[512,1024]{1,0:T(8,128)}, u32[]{:S(2)}) copy-start(f32[512,1024]{1,0:T(8,128)} %copy-done.15) | copy-start | bytes 6291460
  2262.9 7.0 copy-start.41
  (49 other events, 138.1 us)
Sparse Core Ops, SparseCore 0:
  10.2 43.0 all-gather.16
  55.4 39.1 all-gather.18
  96.6 48.0 all-gather.14
  146.7 48.2 all-gather.20
  197.0 226.1 all-gather.30
  425.2 47.6 all-gather.22
  475.0 91.1 all-gather.24
  568.4 90.8 all-gather.26
  661.4 90.8 all-gather.28
  791.1 225.7 all-gather.32
  1020.6 86.0 reduce-scatter.22
  1110.6 87.6 reduce-scatter.18
  1201.9 192.4 reduce-scatter.24
  1397.9 191.7 reduce-scatter.26
  1593.1 191.7 reduce-scatter.28
  1788.2 66.9 reduce-scatter.12
  1858.7 66.5 reduce-scatter.14
  1928.8 86.9 reduce-scatter.16
  2020.0 60.9 reduce-scatter.30
  2084.8 52.7 reduce-scatter.20
  2140.8 122.0 all-reduce.5
where the time goes:
time: 2290 us; the launch traced here: 2280 us
  waiting for transfers between devices  1730 us (76%)
  matrix products  168 us (7%)
  other arithmetic  153 us (7%)
  blocking collectives  141 us (6%)
  local copies, waits for them, and re-layouts  70.5 us (3%)
    all_gather x2, waiting for transfers between devices, entering(): gathered = jax.tree.map(lambda a: lax.all_gather(a, axis), part)  288 us
    reduce_scatter x1, waiting for transfers between devices, body(): lax.psum_scatter(matrices[7], 'shard', scatter_dimension=0, tiled=True)  196 us
    reduce_scatter x1, waiting for transfers between devices, body(): lax.psum_scatter(matrices[9], 'shard', scatter_dimension=0, tiled=True)  195 us
    reduce_scatter x1, waiting for transfers between devices, body(): lax.psum_scatter(matrices[8], 'shard', scatter_dimension=0, tiled=True)  195 us
    psum x1, waiting for transfers between devices, body(): lax.psum((owned[0], owned[1], owned[2], owned[3], owned[4], owned[5], own...  114 us
    reduce_scatter x1, waiting for transfers between devices, body(): lax.psum_scatter(matrices[3], 'shard', scatter_dimension=0, tiled=True)  91.6 us
    reduce_scatter x1, waiting for transfers between devices, body(): lax.psum_scatter(matrices[2], 'shard', scatter_dimension=0, tiled=True)  90.4 us
    all_gather x1, waiting for transfers between devices, body(): lax.all_gather(w_gate, 'shard', axis=0, tiled=True)  88.5 us
  transfers between devices with their start and end apart: 21, of which 19 were waited for; matrix products, arithmetic and copies ran while one was open for 14% of the time, Pallas kernels for 0%

commit v1 on v0

--- a/solution.py
+++ b/solution.py
@@ -1,6 +1,10 @@
 import jax
 import jax.numpy as jnp
 from jax import lax
+import numpy as np
+from jax.experimental import pallas as pl
+from jax.experimental.pallas import tpu as pltpu
+from jax.sharding import Mesh
 from jax.sharding import PartitionSpec as P
 
 HEADS = 4
@@ -95,7 +99,7 @@
     return (inner + carried_part, final_state)
 
 
-def body(
+def wide_body(
     tokens,
     attn_gain,
     w_query,
@@ -291,41 +295,530 @@
     )
 
 
+CHUNK = 128
+LEVELS = (64, 32, 16, 8, 4, 2, 1)
+PAIR = 2
+AXES = ("shard", "x", "core")
+BF16 = jnp.bfloat16
+F32 = jnp.float32
+
+
+def level_tables():
+    rows = np.arange(CHUNK)
+    t, u = rows[:, None], rows[None, :]
+    sums = [(u <= t), (u > t)]
+    masks = [(t == u)]
+    for size in LEVELS:
+        same = (t // (2 * size)) == (u // (2 * size))
+        late_t = (t % (2 * size)) >= size
+        late_u = (u % (2 * size)) >= size
+        sums.append(
+            same & ((late_t & late_u & (u <= t)) | (~late_t & ~late_u & (u > t)))
+        )
+        masks.append(same & late_t & ~late_u)
+    sums = np.concatenate(sums, 0).astype(np.float32)
+    masks = np.stack(masks, 0).astype(np.float32)
+    upper = (u >= t).astype(np.float32)
+    return (
+        np.concatenate([sums, sums], 1),
+        masks,
+        np.concatenate([upper, upper], 1),
+    )
+
+
+def dot_nn(a, b):
+    return lax.dot_general(a, b, (((1,), (0,)), ((), ())), preferred_element_type=F32)
+
+
+def dot_nt(a, b):
+    return lax.dot_general(a, b, (((1,), (1,)), ((), ())), preferred_element_type=F32)
+
+
+def dot_tn(a, b):
+    return lax.dot_general(a, b, (((0,), (0,)), ((), ())), preferred_element_type=F32)
+
+
+def split(a):
+    high = a.astype(BF16)
+    return high, (a - high.astype(F32)).astype(BF16)
+
+
+def fine(dot, a, b):
+    ah, al = split(a)
+    bh, bl = split(b)
+    return dot(ah, bh) + (dot(ah, bl) + dot(al, bh))
+
+
+def half_fine(dot, a, b):
+    ah, al = split(a)
+    return dot(ah, b) + dot(al, b)
+
+
+def summed(table, values):
+    high = values.astype(BF16)
+    rest = (values - high.astype(F32)).astype(BF16)
+    return dot_nn(table, jnp.concatenate([high, rest], 0))
+
+
+def log_decay(logits):
+    return (jnp.minimum(logits, 0.0) - jnp.log(1.0 + jnp.exp(-jnp.abs(logits)))) / GATE_NORM
+
+
+def sigmoid(z):
+    return 1.0 / (1.0 + jnp.exp(-z))
+
+
+def mix_forward_kernel(
+    order, q_ref, k_ref, v_ref, lg_ref, og_ref, gain_ref, sums_ref, mask_ref,
+    gated_ref, mixed_ref, states_ref, state
+):
+    @pl.when(pl.program_id(0) == 0)
+    def _():
+        state[...] = jnp.zeros_like(state)
+
+    factors = jnp.exp(summed(sums_ref[...], log_decay(lg_ref[...])))
+    for head in range(PAIR):
+        kc = slice(head * DK, (head + 1) * DK)
+        vc = slice(head * DV, (head + 1) * DV)
+        q_low, k_low, v_low = q_ref[:, kc], k_ref[:, kc], v_ref[:, vc]
+        q, k = q_low.astype(F32), k_low.astype(F32)
+        scores = mask_ref[0] * dot_nt(q_low, k_low)
+        for level in range(len(LEVELS)):
+            e = factors[(level + 2) * CHUNK : (level + 3) * CHUNK, kc]
+            scores += mask_ref[level + 1] * fine(dot_nt, q * e, k * e)
+        before = factors[:CHUNK, kc]
+        after = factors[CHUNK : 2 * CHUNK, kc]
+        carried = state[head]
+        states_ref[0, head] = carried
+        mixed = half_fine(dot_nn, scores, v_low) + fine(dot_nt, q * before, carried)
+        k_high, k_rest = split(k * after)
+        state[head] = carried * before[CHUNK - 1 :] + (
+            dot_tn(v_low, k_high) + dot_tn(v_low, k_rest)
+        )
+        mixed_ref[:, vc] = mixed
+        normed = mixed * lax.rsqrt(jnp.mean(mixed * mixed, axis=1, keepdims=True) + EPSILON)
+        og = og_ref[:, vc]
+        gated_ref[:, vc] = (normed * gain_ref[...] * (og * sigmoid(og))).astype(BF16)
+
+
+def mix_backward_kernel(
+    order, q_ref, k_ref, v_ref, lg_ref, og_ref, mixed_ref, dg_ref, states_ref, gain_ref,
+    sums_ref, mask_ref, upper_ref,
+    dall_ref, dlog_ref, hgain_ref, bias_ref, dstate, carry
+):
+    @pl.when(pl.program_id(0) == 0)
+    def _():
+        dstate[...] = jnp.zeros_like(dstate)
+        carry[...] = jnp.zeros_like(carry)
+        hgain_ref[...] = jnp.zeros_like(hgain_ref)
+        bias_ref[...] = jnp.zeros_like(bias_ref)
+
+    logits = lg_ref[...]
+    factors = jnp.exp(summed(sums_ref[...], log_decay(logits)))
+    gain = gain_ref[...]
+    flows = []
+    for head in range(PAIR):
+        kc = slice(head * DK, (head + 1) * DK)
+        vc = slice(head * DV, (head + 1) * DV)
+        og, m, dg = og_ref[:, vc], mixed_ref[:, vc], dg_ref[:, vc]
+        sig = sigmoid(og)
+        r = lax.rsqrt(jnp.mean(m * m, axis=1, keepdims=True) + EPSILON)
+        n = m * r
+        dn = dg * (og * sig)
+        hgain_ref[...] += jnp.sum(dn * n, axis=0, keepdims=True)
+        u = gain * dn
+        dm = r * (u - n * jnp.mean(u * n, axis=1, keepdims=True))
+        dog = dg * (n * gain) * (sig * (1.0 + og * (1.0 - sig)))
+        dall_ref[:, 2 * PAIR * DK + PAIR * DV + head * DV : 2 * PAIR * DK + PAIR * DV + (head + 1) * DV] = dog.astype(BF16)
+        dm_low = dm.astype(BF16)
+        q_low, k_low, v_low = q_ref[:, kc], k_ref[:, kc], v_ref[:, vc]
+        q, k = q_low.astype(F32), k_low.astype(F32)
+        dm_rest = (dm - dm_low.astype(F32)).astype(BF16)
+        da = dot_nt(dm_low, v_low) + dot_nt(dm_rest, v_low)
+        before = factors[:CHUNK, kc]
+        after = factors[CHUNK : 2 * CHUNK, kc]
+        carried = states_ref[0, head]
+        ds = dstate[head]
+        ds_low = ds.astype(BF16)
+        q_in = (q * before).astype(BF16)
+        k_out = (k * after).astype(BF16)
+        scores = mask_ref[0] * dot_nt(q_low, k_low)
+        part = (mask_ref[0] * da).astype(BF16)
+        dq = dot_nn(part, k_low) + before * dot_nn(dm_low, carried.astype(BF16))
+        dk = dot_tn(part, q_low) + after * dot_nn(v_low, ds_low)
+        for level in range(len(LEVELS)):
+            e = factors[(level + 2) * CHUNK : (level + 3) * CHUNK, kc]
+            q_e, k_e = (q * e).astype(BF16), (k * e).astype(BF16)
+            scores += mask_ref[level + 1] * dot_nt(q_e, k_e)
+            part = (mask_ref[level + 1] * da).astype(BF16)
+            dq += e * dot_nn(part, k_e)
+            dk += e * dot_tn(part, q_e)
+        dv = dot_tn(scores.astype(BF16), dm_low) + dot_nt(k_out, ds_low)
+        dall_ref[:, kc] = dq.astype(BF16)
+        dall_ref[:, PAIR * DK + head * DK : PAIR * DK + (head + 1) * DK] = dk.astype(BF16)
+        dall_ref[:, 2 * PAIR * DK + head * DV : 2 * PAIR * DK + (head + 1) * DV] = dv.astype(BF16)
+        ds = ds * before[CHUNK - 1 :] + dot_tn(dm_low, q_in)
+        dstate[head] = ds
+        flows.append(q * dq - k * dk)
+        carried_flow = jnp.sum(carried * ds, axis=0, keepdims=True)
+        flows.append(carried_flow)
+    flow = jnp.concatenate([flows[0], flows[2]], 1)
+    d_decay = summed(upper_ref[...], flow) + carry[...]
+    carry[...] = jnp.concatenate([flows[1], flows[3]], 1)
+    dlog = (d_decay * (sigmoid(-logits) * (1.0 / GATE_NORM))).astype(BF16)
+    dlog_ref[...] = dlog
+    bias_ref[...] += jnp.sum(dlog.astype(F32), axis=0, keepdims=True)
+
+
+def mix_forward(order, q, k, v, logits, og, gain, sums, masks):
+    rows = q.shape[0]
+    steps = rows // CHUNK
+    ck, cv = PAIR * DK, PAIR * DV
+
+    def row_block(width):
+        return pl.BlockSpec((CHUNK, width), lambda g, o: (o[g], 0))
+
+    def whole(a):
+        return pl.BlockSpec(a.shape, lambda g, o: (0,) * a.ndim)
+
+    return pl.pallas_call(
+        mix_forward_kernel,
+        grid_spec=pltpu.PrefetchScalarGridSpec(
+            num_scalar_prefetch=1,
+            grid=(steps,),
+            in_specs=[row_block(ck), row_block(ck), row_block(cv), row_block(ck), row_block(cv),
+                      whole(gain), whole(sums), whole(masks)],
+            out_specs=[row_block(cv), row_block(cv),
+                       pl.BlockSpec((1, PAIR, DV, DK), lambda g, o: (g, 0, 0, 0))],
+            scratch_shapes=[pltpu.VMEM((PAIR, DV, DK), F32)],
+        ),
+        out_shape=[jax.ShapeDtypeStruct((rows, cv), BF16), jax.ShapeDtypeStruct((rows, cv), F32),
+                   jax.ShapeDtypeStruct((steps, PAIR, DV, DK), F32)],
+        compiler_params=pltpu.CompilerParams(vmem_limit_bytes=40 * 1024 * 1024),
+        name="mix_forward",
+    )(order, q, k, v, logits, og, gain, sums, masks)
+
+
+def mix_backward(order, q, k, v, logits, og, mixed, d_gated, states, gain, sums, masks, upper):
+    rows = q.shape[0]
+    steps = rows // CHUNK
+    ck, cv = PAIR * DK, PAIR * DV
+
+    def row_block(width):
+        return pl.BlockSpec((CHUNK, width), lambda g, o: (o[steps - 1 - g], 0))
+
+    def whole(a):
+        return pl.BlockSpec(a.shape, lambda g, o: (0,) * a.ndim)
+
+    return pl.pallas_call(
+        mix_backward_kernel,
+        grid_spec=pltpu.PrefetchScalarGridSpec(
+            num_scalar_prefetch=1,
+            grid=(steps,),
+            in_specs=[row_block(ck), row_block(ck), row_block(cv), row_block(ck), row_block(cv),
+                      row_block(cv), row_block(cv),
+                      pl.BlockSpec((1, PAIR, DV, DK), lambda g, o: (steps - 1 - g, 0, 0, 0)),
+                      whole(gain), whole(sums), whole(masks), whole(upper)],
+            out_specs=[row_block(2 * ck + 2 * cv), row_block(ck),
+                       pl.BlockSpec((1, DV), lambda g, o: (0, 0)),
+                       pl.BlockSpec((1, ck), lambda g, o: (0, 0))],
+            scratch_shapes=[pltpu.VMEM((PAIR, DV, DK), F32), pltpu.VMEM((1, ck), F32)],
+        ),
+        out_shape=[jax.ShapeDtypeStruct((rows, 2 * ck + 2 * cv), BF16), jax.ShapeDtypeStruct((rows, ck), BF16),
+                   jax.ShapeDtypeStruct((1, DV), F32), jax.ShapeDtypeStruct((1, ck), F32)],
+        compiler_params=pltpu.CompilerParams(vmem_limit_bytes=40 * 1024 * 1024),
+        name="mix_backward",
+    )(order, q, k, v, logits, og, mixed, d_gated, states, gain, sums, masks, upper)
+
+
+def device_of(shard, x, core, xs):
+    return (shard * xs + x) * 2 + core
+
+
+def core_swap(a):
+    return lax.ppermute(a, "core", [(0, 1), (1, 0)])
+
+
+def x_swap(a):
+    return lax.ppermute(a, "x", [(0, 1), (1, 0)])
+
+
+def by_core(mine, other, axis):
+    first = lax.axis_index("core") == 0
+    return jnp.concatenate(
+        [jnp.where(first, mine, other), jnp.where(first, other, mine)], axis
+    )
+
+
+def swap_rows(a):
+    half = a.shape[0] // 2
+    return jnp.concatenate([a[half:], a[:half]], 0)
+
+
+def core_half(a, axis):
+    half = a.shape[axis] // 2
+    return lax.dynamic_slice_in_dim(a, lax.axis_index("core") * half, half, axis)
+
+
+def body(
+    tokens,
+    attn_gain,
+    w_query,
+    w_key,
+    w_value,
+    w_outgate,
+    w_rank_in,
+    w_rank_out,
+    fgate_bias,
+    head_gain,
+    w_output,
+    ffn_gain,
+    w_gate,
+    w_up,
+    w_down,
+    out_grad,
+):
+    seqs, tok_dev, width = tokens.shape
+    shards = lax.axis_size("shard")
+    xs = lax.axis_size("x")
+    core = lax.axis_index("core")
+    place = lax.axis_index("shard")
+    piece = place % seqs
+
+    def to_chip(step):
+        pairs = []
+        for j in range(shards):
+            for x in range(xs):
+                for c in range(2):
+                    target = c * seqs + (step + j % seqs) % seqs
+                    pairs.append(
+                        (device_of(j, x, c, xs), device_of(target, x, j // seqs, xs))
+                    )
+        return pairs
+
+    def rows_in(a):
+        return jnp.concatenate(
+            [
+                lax.ppermute(
+                    lax.dynamic_index_in_dim(a, (step + piece) % seqs, 0, False),
+                    AXES,
+                    to_chip(step),
+                )
+                for step in range(seqs)
+            ],
+            0,
+        )
+
+    def rows_out(a):
+        back = [
+            lax.ppermute(
+                a[step * tok_dev : (step + 1) * tok_dev],
+                AXES,
+                [(t, s) for s, t in to_chip(step)],
+            )
+            for step in range(seqs)
+        ]
+        twice = jnp.stack(back + back, 0)
+        return lax.dynamic_slice_in_dim(twice, (seqs - piece) % seqs, seqs, 0)
+
+    counter = jnp.arange(shards, dtype=jnp.int32)
+    order = ((counter // seqs) ^ core) * seqs + (piece - counter) % seqs
+    order = order.astype(jnp.int32)
+    sums, masks, upper = level_tables()
+    sums, masks, upper = jnp.asarray(sums, BF16), jnp.asarray(masks, F32), jnp.asarray(upper, BF16)
+
+    rank_pack = jnp.concatenate(
+        [
+            w_rank_in,
+            jnp.pad(w_rank_out, ((0, w_rank_in.shape[0] - w_rank_out.shape[0]), (0, 0))),
+            jnp.zeros((w_rank_in.shape[0], 96), BF16),
+        ],
+        1,
+    )
+    ck, cv = PAIR * DK, PAIR * DV
+    packed = jnp.concatenate(
+        [core_half(w, 1) for w in (w_query, w_key, w_value, w_outgate, w_output)] + [rank_pack], 1
+    )
+    wide = 2 * ck + 2 * cv
+    own = rows_in(tokens)
+    attn_full = lax.all_gather(packed, "shard", axis=0, tiled=True)
+    ffn_cols = lax.all_gather(
+        jnp.concatenate([core_half(w_gate, 1), core_half(w_up, 1)], 1), "shard", axis=0, tiled=True
+    )
+    down_rows = lax.all_gather(core_half(w_down, 0), "shard", axis=0)
+    own_grad = rows_in(out_grad)
+
+    x_low = jnp.concatenate([own, core_swap(own)], 0)
+    inputs = x_low.astype(F32)
+    r_in = lax.rsqrt(jnp.mean(inputs * inputs, axis=1, keepdims=True) + EPSILON)
+    attn_row = attn_gain.astype(F32)
+    normed = (inputs * r_in * attn_row).astype(BF16)
+
+    w_qkvo = attn_full[:, :wide]
+    rank_in = attn_full[:, wide + cv : wide + cv + 16]
+    rank_out = attn_full[:, wide + cv + 16 : wide + cv + 32]
+    rank_out = rank_out.reshape(shards, -1, 16)[:, : w_rank_out.shape[0]].reshape(-1, 16)
+    rank_out = core_half(rank_out, 0)
+    queries = product(normed, w_qkvo[:, :ck]).astype(BF16)
+    keys = product(normed, w_qkvo[:, ck : 2 * ck]).astype(BF16)
+    values = product(normed, w_qkvo[:, 2 * ck : 2 * ck + cv]).astype(BF16)
+    out_gate = product(normed, w_qkvo[:, 2 * ck + cv :])
+    rank_rows = product(normed, rank_in).astype(BF16)
+    logits = times_transpose(rank_rows, rank_out) + core_half(fgate_bias, 0).astype(F32)
+    gain = head_gain.astype(F32)[None]
+    gated, mixed, states = mix_forward(
+        order, queries, keys, values, logits, out_gate, gain, sums, masks
+    )
+    gated_full = by_core(gated, swap_rows(core_swap(gated)), 1)
+    out_mine = attn_full[:, wide : wide + cv]
+    w_out_full = by_core(out_mine, core_swap(out_mine), 1)
+    residual = inputs + product(gated_full, w_out_full)
+    r_ffn = lax.rsqrt(jnp.mean(residual * residual, axis=1, keepdims=True) + EPSILON)
+    ffn_row = ffn_gain.astype(F32)
+    ffn_in = (residual * r_ffn * ffn_row).astype(BF16)
+
+    ff_half = w_gate.shape[1] // 2
+    group = shards // 2
+    mine_down = lax.dynamic_slice_in_dim(down_rows, core * group, group, 0)
+    send_down = lax.dynamic_slice_in_dim(down_rows, (1 - core) * group, group, 0)
+    other_down = core_swap(send_down)
+    w_down_half = by_core(mine_down, other_down, 1).reshape(ff_half, width)
+    w_gate_half, w_up_half = ffn_cols[:, :ff_half], ffn_cols[:, ff_half:]
+
+    dy = jnp.concatenate([own_grad, core_swap(own_grad)], 0)
+    gate = product(ffn_in, w_gate_half)
+    up = product(ffn_in, w_up_half)
+    sig = sigmoid(gate)
+    act = gate * sig
+    hidden = (act * up).astype(BF16)
+    d_hidden = times_transpose(dy, w_down_half)
+    d_gate = (d_hidden * up * (sig * (1.0 + gate * (1.0 - sig)))).astype(BF16)
+    d_up = (d_hidden * act).astype(BF16)
+    half_rows = x_low.shape[0] // 2
+    block_part = product(hidden, w_down_half)
+    block_own = (
+        residual[:half_rows] + block_part[:half_rows] + core_swap(block_part[half_rows:])
+    ).astype(BF16)
+    block_out = rows_out(block_own)
+
+    down_grad = outer_sum(hidden, dy).astype(BF16).reshape(group, 2, -1, width)
+    mine_dg = lax.dynamic_index_in_dim(down_grad, core, 1, False)
+    other_dg = core_swap(lax.dynamic_index_in_dim(down_grad, 1 - core, 1, False))
+    down_grad = by_core(mine_dg, other_dg, 0)
+    down_own = lax.psum_scatter(
+        down_grad.reshape(-1, width), "shard", scatter_dimension=0, tiled=True
+    )
+    gateup_grad = jnp.concatenate([outer_sum(ffn_in, d_gate), outer_sum(ffn_in, d_up)], 1)
+    gateup_own = lax.psum_scatter(
+        gateup_grad.astype(BF16), "shard", scatter_dimension=0, tiled=True
+    )
+
+    dn_part = times_transpose(d_gate, w_gate_half) + times_transpose(d_up, w_up_half)
+    dn_ffn = dn_part + swap_rows(core_swap(dn_part))
+    u = ffn_row * dn_ffn
+    d_residual = dy.astype(F32) + r_ffn * (
+        u - residual * (r_ffn * r_ffn) * jnp.mean(u * residual, axis=1, keepdims=True)
+    )
+    ffn_gain_grad = jnp.sum((dn_ffn * residual * r_ffn)[:half_rows], axis=0)
+    d_branch = d_residual.astype(BF16)
+    out_w_grad = outer_sum(gated_full, core_half(d_branch, 1))
+    d_gated = times_transpose(d_branch, core_half(w_out_full, 0))
+    d_all, d_logits, hgain_part, bias_part = mix_backward(
+        order, queries, keys, values, logits, out_gate, mixed, d_gated, states, gain,
+        sums, masks, upper
+    )
+    rank_out_grad = outer_sum(d_logits, rank_rows)
+    rank_part = product(d_logits, rank_out)
+    d_rank = (rank_part + swap_rows(core_swap(rank_part))).astype(BF16)
+    rank_in_grad = outer_sum(normed[:half_rows], d_rank[:half_rows])
+    qkvo_grad = outer_sum(normed, d_all)
+    attn_own = lax.psum_scatter(
+        jnp.concatenate([qkvo_grad, out_w_grad], 1).astype(BF16),
+        "shard",
+        scatter_dimension=0,
+        tiled=True,
+    )
+    dn_attn = times_transpose(d_all, w_qkvo)
+    dn_own = (
+        dn_attn[:half_rows]
+        + core_swap(dn_attn[half_rows:])
+        + times_transpose(d_rank[:half_rows], rank_in)
+    )
+    own_in, own_r = inputs[:half_rows], r_in[:half_rows]
+    u = attn_row * dn_own
+    tok_grad = (
+        d_residual[:half_rows]
+        + own_r * (u - own_in * (own_r * own_r) * jnp.mean(u * own_in, axis=1, keepdims=True))
+    ).astype(BF16)
+    tokens_grad = rows_out(tok_grad)
+    attn_gain_grad = jnp.sum(dn_own * own_in * own_r, axis=0)
+
+    first = (core == 0).astype(F32)
+    bias_both = jnp.concatenate([bias_part[0] * first, bias_part[0] * (1.0 - first)], 0)
+    rank_out_both = jnp.concatenate([rank_out_grad * first, rank_out_grad * (1.0 - first)], 0)
+    small = lax.psum(
+        (attn_gain_grad, bias_both, hgain_part[0], ffn_gain_grad, rank_in_grad, rank_out_both),
+        AXES,
+    )
+    rin_rows, rout_rows = w_rank_in.shape[0], w_rank_out.shape[0]
+    rank_in_own = lax.dynamic_slice_in_dim(small[4], place * rin_rows, rin_rows, 0)
+    rank_out_own = lax.dynamic_slice_in_dim(small[5], place * rout_rows, rout_rows, 0)
+
+    def settle(a):
+        total = a.astype(F32)
+        if xs == 2:
+            total = total + x_swap(a).astype(F32)
+        return total, core_swap(total)
+
+    attn_mine, attn_other = settle(attn_own)
+    gu_mine, gu_other = settle(gateup_own)
+    down_mine, down_other = settle(down_own)
+
+    def columns(mine, other, start, size):
+        return by_core(mine[:, start : start + size], other[:, start : start + size], 1)
+
+    return (
+        block_out,
+        tokens_grad,
+        small[0],
+        columns(attn_mine, attn_other, 0, ck),
+        columns(attn_mine, attn_other, ck, ck),
+        columns(attn_mine, attn_other, 2 * ck, cv),
+        columns(attn_mine, attn_other, 2 * ck + cv, cv),
+        rank_in_own,
+        rank_out_own,
+        small[1],
+        small[2],
+        columns(attn_mine, attn_other, wide, cv),
+        small[3],
+        columns(gu_mine, gu_other, 0, ff_half),
+        columns(gu_mine, gu_other, ff_half, ff_half),
+        by_core(down_mine, down_other, 0),
+    )
+
+
 def solution(mesh):
-    in_specs = (
-        P("rep", "shard", None),
-        P(),
-        P("shard", None),
-        P("shard", None),
-        P("shard", None),
-        P("shard", None),
-        P("shard", None),
-        P("shard", None),
-        P(),
-        P(),
-        P("shard", None),
-        P(),
-        P("shard", None),
-        P("shard", None),
-        P("shard", None),
-        P("rep", "shard", None),
-    )
-    out_specs = (
-        P("rep", "shard", None),
-        P("rep", "shard", None),
-        P(),
-        P("shard", None),
-        P("shard", None),
-        P("shard", None),
-        P("shard", None),
-        P("shard", None),
-        P("shard", None),
-        P(),
-        P(),
-        P("shard", None),
-        P(),
-        P("shard", None),
-        P("shard", None),
-        P("shard", None),
-    )
-    return jax.shard_map(body, mesh=mesh, in_specs=in_specs, out_specs=out_specs, check_vma=False)
+    shards = mesh.shape["shard"]
+    reps = mesh.shape["rep"]
+
+    def run(*arrays):
+        tokens = arrays[0]
+        seqs = tokens.shape[0] // reps
+        narrow = reps == 4 and shards == 2 * seqs and tokens.shape[1] // shards == CHUNK
+        if narrow:
+            grid = Mesh(mesh.devices.reshape(shards, reps // 2, 2), AXES)
+            rep = ("x", "core")
+        else:
+            grid, rep = mesh, "rep"
+        rows, cols = P(rep, "shard", None), P("shard", None)
+        in_specs = (rows, P()) + (cols,) * 6 + (P(), P(), cols, P()) + (cols,) * 3 + (rows,)
+        out_specs = (rows, rows, P()) + (cols,) * 6 + (P(), P(), cols, P()) + (cols,) * 3
+        return jax.shard_map(
+            body if narrow else wide_body,
+            mesh=grid,
+            in_specs=in_specs,
+            out_specs=out_specs,
+            check_vma=False,
+        )(*arrays)
+
+    return run

time: 2290 us -> 794 us (0.35)
  waiting for transfers between devices: 1730 us -> 397 us
  other arithmetic: 153 us -> 45 us
  matrix products: 168 us -> 79.9 us
  starting transfers between devices: 1.71 us -> 84.1 us
  blocking collectives: 141 us -> 65.8 us
  Pallas kernels: 0 us -> 33.6 us
    reduce_scatter x9 -> x3, waiting for transfers between devices: 981 us -> 195 us  [the longest x1 111 us: body(): lax.psum_scatter(gateup_grad.astype(BF16), 'shard', scatter_dimension=0,...]
    all_gather x10 -> x3, waiting for transfers between devices: 626 us -> 87.1 us  [the longest x1 47.8 us: body(): lax.all_gather(jnp.concatenate([core_half(w_gate, 1), core_half(w_up, 1)]...]
    all_gather x3 -> x0, blocking collectives: 89.8 us -> none  [the longest x1 31.1 us: entering(): gathered = jax.tree.map(lambda a: lax.all_gather(a, axis), part)]
    ppermute x0 -> x32, starting transfers between devices: none -> 83.7 us  [the longest x13 58.4 us: core_swap(): return lax.ppermute(a, 'core', [(0, 1), (1, 0)])]
    unnamed x4 -> x0, other arithmetic: 53.7 us -> none
    psum x1, waiting for transfers between devices: 114 us -> 62.3 us  [body(): lax.psum((attn_gain_grad, bias_both, hgain_part[0], ffn_gain_grad, rank_i...]
    ppermute x0 -> x32, waiting for transfers between devices: none -> 51.8 us  [the longest x8 31.3 us: rows_in(): lax.ppermute(lax.dynamic_index_in_dim(a, (step + piece) % seqs, 0, False)...]
    dot_general x11 -> x0, matrix products: 45 us -> none  [the longest x3 17.9 us: local_mixing(): jnp.einsum('bntha,nbhae->bnthe', query_scaled, starts, precision=PRECISE)]
  transfers between devices with their start and end apart: 21 -> 39, of which waited for: 19 -> 13; matrix products, arithmetic and copies ran while one was open for 14% -> 17% of each run, Pallas kernels for 0% -> 4%
where the time goes in v1:
time: 794 us; the launch traced here: 786 us
  waiting for transfers between devices  397 us (50%)
  starting transfers between devices  84.1 us (11%)
  matrix products  79.9 us (10%)
  blocking collectives  65.8 us (8%)
  local copies, waits for them, and re-layouts  64.6 us (8%)
  other arithmetic  45 us (6%)
  Pallas kernels  33.6 us (4%)
  between operations  15.9 us (2%)
    reduce_scatter x1, waiting for transfers between devices, body(): lax.psum_scatter(gateup_grad.astype(BF16), 'shard', scatter_dimension=0,...  111 us
    reduce_scatter x1, waiting for transfers between devices, body(): lax.psum_scatter(jnp.concatenate([qkvo_grad, out_w_grad], 1).astype(BF16)...  71.7 us
    psum x1, blocking collectives, body(): lax.psum((attn_gain_grad, bias_both, hgain_part[0], ffn_gain_grad, rank_i...  65.8 us
    psum x1, waiting for transfers between devices, body(): lax.psum((attn_gain_grad, bias_both, hgain_part[0], ffn_gain_grad, rank_i...  62.3 us
    ppermute x13, starting transfers between devices, core_swap(): return lax.ppermute(a, 'core', [(0, 1), (1, 0)])  58.4 us
    all_gather x1, waiting for transfers between devices, body(): lax.all_gather(jnp.concatenate([core_half(w_gate, 1), core_half(w_up, 1)]...  47.8 us
    all_gather x1, waiting for transfers between devices, body(): attn_full = lax.all_gather(packed, 'shard', axis=0, tiled=True)  39.2 us
    dot_general x7, matrix products, times_transpose(): lax.dot_general(left_side, right_side, (((1,), (1,)), ((), ())), preferre...  33.4 us
  transfers between devices with their start and end apart: 39, of which 13 were waited for; matrix products, arithmetic and copies ran while one was open for 17% of the time, Pallas kernels for 4%

profile of v1, /device:TPU:0, one launch (start us, length us, event | category | flops | bytes accessed | tf_op | source)
XLA Modules:
  0.0 785.9 jit_solution(17226007654240989657)
XLA Ops:
  18.4 3.0 collective-permute-start.1
  25.9 7.8 collective-permute-done.1
  33.7 5.1 collective-permute-done.2
  38.7 6.5 collective-permute-done.3
  45.3 33.3 %collective-permute-start.4 = (bf16[512,1024]{0,1:T(8,128)(2,1)S(1)}, bf16[512,1024]{0,1:T(8,128)(2,1)S(1)}, u32[]{:S(2)}, u32[]{:S(2)}) collective-permute-start(bf16[512,1024]{0,1:T(8,128)(2,1)S(1)} %pad_maximum_fusion.14), channel_id=1, source_target_pairs={{0,1},{1,0},{2,3},{3,2},{4,5},{5,4},{6,7},{7,6},{8,9},{9,8},{10,11... | collective-permute-start | bytes 3145736 | tf_op jit(solution)/shard_map/ppermute | solution.py:539
  85.8 2.6 collective-permute-start.16
  89.1 5.3 collective-permute-done.14
  94.5 6.6 collective-permute-done.16
  102.2 23.3 %collective-permute-start.17 = (bf16[512,1024]{0,1:T(8,128)(2,1)}, bf16[512,1024]{0,1:T(8,128)(2,1)}, u32[]{:S(2)}, u32[]{:S(2)}) collective-permute-start(bf16[512,1024]{0,1:T(8,128)(2,1)} %pad_maximum_fusion.16), channel_id=1, source_target_pairs={{0,1},{1,0},{2,3},{3,2},{4,5},{5,4},{6,7},{7,6},{8,9},{9,8},{10,11... | collective-permute-start | bytes 3145736 | tf_op jit(solution)/shard_map/ppermute | solution.py:539
  128.0 3.4 constant_dynamic-slice_fusion.8
  131.4 39.2 %all-gather.5.cloned.1.call-done = bf16[1024,2176]{1,0:T(8,128)(2,1)} async-done(((bf16[128,2176]{1,0:T(8,128)(2,1)}), bf16[1024,2176]{1,0:T(8,128)(2,1)}) %all-gather.5.cloned.1.call-update) | async-done | bytes 4456464 | tf_op jit(solution)/shard_map/all_gather | solution.py:644
  171.8 1.9 convolution_convert_fusion.6.k_ref
  175.0 3.1 fusion.26.og_ref
  180.9 17.7 %mix_forward.1 = (bf16[1024,512]{1,0:T(8,128)(2,1)S(1)}, f32[1024,512]{1,0:T(8,128)S(1)}, f32[8,2,256,128]{3,2,1,0:T(8,128)S(1)}) custom-call(s32[8]{0:T(128)S(1)} %fusion.45.order, bf16[1024,256]{1,0:T(8,128)(2,1)S(1)} %convolution_convert_fusion.7.q_ref, bf16[1024,256]{1,0:T(8,128)(2,1)S(1)} %convolution_convert_fusion.6.k_ref, ...), custom_call_target="tpu_custom_call" | custom-call | tf_op jit(solution)/shard_map/mix_forward/pallas_call | solution.py:484
  199.2 2.3 constant_dynamic-update-slice_fusion.5
  209.4 2.8 multiply_reduce_fusion.1
  215.9 47.8 %all-gather.7.cloned.1.call-done = bf16[1024,2816]{1,0:T(8,128)(2,1)} async-done(((bf16[128,2816]{1,0:T(8,128)(2,1)}), bf16[1024,2816]{1,0:T(8,128)(2,1)}) %all-gather.7.cloned.1.call-update) | async-done | bytes 5767184 | tf_op jit(solution)/shard_map/all_gather | solution.py:645
  263.7 6.1 fusion.5
  269.9 5.3 fusion.9
  275.2 9.7 %multiply_convert_fusion.1 = (bf16[1024,1408]{1,0:T(8,128)(2,1)}, bf16[1024,1408]{1,0:T(8,128)(2,1)}, bf16[1024,1408]{1,0:T(8,128)(2,1)}) fusion(f32[1024,1408]{1,0:T(8,128)} %fusion.9, f32[1024,1408]{1,0:T(8,128)S(1)} %fusion.5, bf16[1024,1024]{0,1:T(8,128)(2,1)S(1)} %copy-done.42, bf16[1408,1024]{1,0:T(8,128)(2,1)S(1)} %bitcast.80), kind=kOutput, calls=%fused_computation.2 | convolution fusion | flops 2974416896 | bytes 25165824 | tf_op jit(solution)/shard_map/dot_general | solution.py:44
  284.9 5.4 fusion.3
  290.3 5.0 fusion.18
  295.3 5.7 convolution_convert_fusion
  303.0 2.8 fusion.54
  306.5 3.3 multiply_reduce_fusion
  309.9 3.9 fusion.53
  313.8 3.3 fusion.22.dg_ref
  317.8 15.9 %mix_backward.1 = (bf16[1024,1536]{1,0:T(8,128)(2,1)}, bf16[1024,256]{1,0:T(8,128)(2,1)S(1)}, f32[1,256]{1,0:T(1,128)S(1)}, f32[1,256]{1,0:T(1,128)S(1)}) custom-call(s32[8]{0:T(128)S(1)} %fusion.45.order, bf16[1024,256]{1,0:T(8,128)(2,1)S(1)} %copy-done.17, bf16[1024,256]{1,0:T(8,128)(2,1)S(1)} %copy-done.15, bf16[1024,512]{1,0:T(8,128)(2,1)S(1)} %copy-done.3, ...), custom_call_target="tpu_custom_call" | custom-call | tf_op jit(solution)/shard_map/mix_backward/pallas_call | solution.py:513
  340.7 5.6 convolution_convert_fusion.1
  346.3 3.6 convolution_convert_fusion.2
  350.0 2.8 pad_maximum_fusion
  354.4 2.6 convert_element_type.83
  358.6 3.6 fusion.59
  368.3 3.6 convolution_convert_fusion.3
  371.9 2.6 pad_maximum_fusion.1
  374.6 6.5 fusion.1
  383.1 2.5 copy-done.21
  385.6 2.3 fusion.13
  392.9 62.3 %all-reduce.4.cloned.1.call-done = f32[1024,16]{0,1:T(8,128)} async-done(((f32[1024,16]{0,1:T(8,128)}), f32[1024,16]{0,1:T(8,128)}) %all-reduce.4.cloned.1.call-update) | async-done | bytes 65552 | tf_op jit(solution)/shard_map/psum | solution.py:759
  456.9 3.2 multiply_reduce_fusion.3
  464.5 3.7 collective-permute-start.22
  469.3 65.8 %all-reduce.1 = (f32[1024]{0:T(1024)}, f32[512,16]{0,1:T(8,128)S(1)}, f32[512]{0:T(512)}, f32[256]{0:T(256)}, f32[1024]{0:T(1024)}) all-reduce(f32[1024]{0:T(1024)S(1)} %get-tuple-element.46, f32[512,16]{0,1:T(8,128)S(1)} %pad_maximum_fusion.24, ...), channel_id=1, replica_groups=mesh['shard'=8,'x'=2,'core'=2] {'shard','x','core'}, use_global_device_ids=true, to_apply=%region_5.6 | all-reduce | flops 11008 | bytes 88064 | tf_op jit(solution)/shard_map/psum | solution.py:759
  538.8 12.5 %reduce-scatter.8.cloned.1.call-done = bf16[176,1024]{1,0:T(8,128)(2,1)} async-done(((bf16[1408,1024]{1,0:T(8,128)(2,1)}), bf16[176,1024]{1,0:T(8,128)(2,1)}) %reduce-scatter.8.cloned.1.call-update) | async-done | bytes 360464 | tf_op jit(solution)/shard_map/reduce_scatter | solution.py:708
  552.7 111.2 %reduce-scatter.6.cloned.1.call-done = bf16[128,2816]{1,0:T(8,128)(2,1)} async-done(((bf16[1024,2816]{1,0:T(8,128)(2,1)}), bf16[128,2816]{1,0:T(8,128)(2,1)}) %reduce-scatter.6.cloned.1.call-update) | async-done | bytes 720912 | tf_op jit(solution)/shard_map/reduce_scatter | solution.py:712
  666.9 1.9 convert_add_fusion.3
  668.8 13.1 %collective-permute-done.27 = bf16[128,2816]{1,0:T(8,128)(2,1)S(1)} collective-permute-done((bf16[128,2816]{1,0:T(8,128)(2,1)}, bf16[128,2816]{1,0:T(8,128)(2,1)S(1)}, u32[]{:S(2)}, u32[]{:S(2)}) %collective-permute-start.27) | collective-permute-done | bytes 720928 | tf_op jit(solution)/shard_map/ppermute | solution.py:543
  683.6 71.7 %reduce-scatter.4.cloned.1.call-done = bf16[128,2048]{1,0:T(8,128)(2,1)} async-done(((bf16[1024,2048]{1,0:T(8,128)(2,1)}), bf16[128,2048]{1,0:T(8,128)(2,1)}) %reduce-scatter.4.cloned.1.call-update) | async-done | bytes 524304 | tf_op jit(solution)/shard_map/reduce_scatter | solution.py:735
  762.0 7.4 collective-permute-done.25
  (350 shorter events, 103.1 us)
Async XLA Ops:
  7.2 120.8 %all-gather.9.cloned.1.call-start = ((), (), s32[]{:S(2)}) async-start(), calls=%async_computation.9 | async-start | bytes 3244032 | tf_op jit(solution)/shard_map/all_gather | solution.py:648
  9.1 161.6 %all-gather.5.cloned.1.call-start = ((), (), s32[]{:S(2)}) async-start(), calls=%async_computation.3 | async-start | bytes 5013504 | tf_op jit(solution)/shard_map/all_gather | solution.py:644
  14.6 249.1 %all-gather.7.cloned.1.call-start = ((), (), s32[]{:S(2)}) async-start(), calls=%async_computation.4 | async-start | bytes 6488064 | tf_op jit(solution)/shard_map/all_gather | solution.py:645
  15.6 439.6 %all-reduce.4.cloned.1.call-start = ((), (), s32[]{:S(2)}) async-start(), calls=%async_computation.6 | async-start | bytes 131072 | tf_op jit(solution)/shard_map/psum | solution.py:759
  17.5 8.4 %collective-permute-start = (bf16[128,1024]{0,1:T(8,128)(2,1)S(1)}, bf16[128,1024]{0,1:T(8,128)(2,1)S(1)}, u32[]{:S(2)}, u32[]{:S(2)}) collective-permute-start(bf16[128,1024]{0,1:T(8,128)(2,1)S(1)} %bitcast.93), channel_id=1, source_target_pairs={{0,0},{1,16},{2,2},{3,18},{4,4},{5,20},{6,6},{7,22},{8,8},{9,24},{... | collective-permute-start | bytes 786440 | tf_op jit(solution)/shard_map/ppermute | solution.py:602
  18.4 15.3 %collective-permute-start.1 = (bf16[128,1024]{0,1:T(8,128)(2,1)S(1)}, bf16[128,1024]{0,1:T(8,128)(2,1)S(1)}, u32[]{:S(2)}, u32[]{:S(2)}) collective-permute-start(bf16[128,1024]{0,1:T(8,128)(2,1)S(1)} %bitcast.94), channel_id=1, source_target_pairs={{0,4},{1,20},{2,6},{3,22},{4,8},{5,24},{6,10},{7,26},{8,12},{9,28}... | collective-permute-start | bytes 786440 | tf_op jit(solution)/shard_map/ppermute | solution.py:602
  21.6 17.1 %collective-permute-start.2 = (bf16[128,1024]{0,1:T(8,128)(2,1)S(1)}, bf16[128,1024]{0,1:T(8,128)(2,1)S(1)}, u32[]{:S(2)}, u32[]{:S(2)}) collective-permute-start(bf16[128,1024]{0,1:T(8,128)(2,1)S(1)} %bitcast.95), channel_id=1, source_target_pairs={{0,8},{1,24},{2,10},{3,26},{4,12},{5,28},{6,14},{7,30},{8,0},{9,16... | collective-permute-start | bytes 786440 | tf_op jit(solution)/shard_map/ppermute | solution.py:602
  24.4 64.1 %copy-start.78 = (bf16[1024]{0:T(1024)(128)(2,1)S(1)}, bf16[1024]{0:T(1024)(128)(2,1)}, u32[]{:S(2)}) copy-start(bf16[1024]{0:T(1024)(128)(2,1)} %param.20) | copy-start | bytes 6148
  24.4 64.0 %copy-start.83 = (bf16[256]{0:T(256)(128)(2,1)S(1)}, bf16[256]{0:T(256)(128)(2,1)}, u32[]{:S(2)}) copy-start(bf16[256]{0:T(256)(128)(2,1)} %param.28) | copy-start | bytes 1540
  24.4 64.0 %copy-start.79 = (bf16[1024]{0:T(1024)(128)(2,1)S(1)}, bf16[1024]{0:T(1024)(128)(2,1)}, u32[]{:S(2)}) copy-start(bf16[1024]{0:T(1024)(128)(2,1)} %param.30) | copy-start | bytes 6148
  24.4 64.1 %copy-start.80 = (bf16[512]{0:T(512)(128)(2,1)S(1)}, bf16[512]{0:T(512)(128)(2,1)}, u32[]{:S(2)}) copy-start(bf16[512]{0:T(512)(128)(2,1)} %param.27) | copy-start | bytes 3076
  24.4 20.8 %collective-permute-start.3 = (bf16[128,1024]{0,1:T(8,128)(2,1)S(1)}, bf16[128,1024]{0,1:T(8,128)(2,1)S(1)}, u32[]{:S(2)}, u32[]{:S(2)}) collective-permute-start(bf16[128,1024]{0,1:T(8,128)(2,1)S(1)} %bitcast.96), channel_id=1, source_target_pairs={{0,12},{1,28},{2,14},{3,30},{4,0},{5,16},{6,2},{7,18},{8,4},{9,20}... | collective-permute-start | bytes 786440 | tf_op jit(solution)/shard_map/ppermute | solution.py:602
  33.7 49.2 %copy-start.63 = (bf16[128,1024]{0,1:T(8,128)(2,1)}, bf16[128,1024]{0,1:T(8,128)(2,1)S(1)}, u32[]{:S(2)}) copy-start(bf16[128,1024]{0,1:T(8,128)(2,1)S(1)} %collective-permute-done.1) | copy-start | bytes 786436
  38.7 45.9 %copy-start.65 = (bf16[128,1024]{0,1:T(8,128)(2,1)}, bf16[128,1024]{0,1:T(8,128)(2,1)S(1)}, u32[]{:S(2)}) copy-start(bf16[128,1024]{0,1:T(8,128)(2,1)S(1)} %collective-permute-done.2) | copy-start | bytes 786436
  45.3 80.6 %collective-permute-start.4 = (bf16[512,1024]{0,1:T(8,128)(2,1)S(1)}, bf16[512,1024]{0,1:T(8,128)(2,1)S(1)}, u32[]{:S(2)}, u32[]{:S(2)}) collective-permute-start(bf16[512,1024]{0,1:T(8,128)(2,1)S(1)} %pad_maximum_fusion.14), channel_id=1, source_target_pairs={{0,1},{1,0},{2,3},{3,2},{4,5},{5,4},{6,7},{7,6},{8,9},{9,8},{10,11... | collective-permute-start | bytes 3145736 | tf_op jit(solution)/shard_map/ppermute | solution.py:539
  79.4 9.7 %collective-permute-start.13 = (bf16[128,1024]{0,1:T(8,128)(2,1)}, bf16[128,1024]{0,1:T(8,128)(2,1)S(1)}, u32[]{:S(2)}, u32[]{:S(2)}) collective-permute-start(bf16[128,1024]{0,1:T(8,128)(2,1)} %bitcast.89), channel_id=1, source_target_pairs={{0,0},{1,16},{2,2},{3,18},{4,4},{5,20},{6,6},{7,22},{8,8},{9,24},{... | collective-permute-start | bytes 786440 | tf_op jit(solution)/shard_map/ppermute | solution.py:602
  82.8 11.6 %collective-permute-start.14 = (bf16[128,1024]{0,1:T(8,128)(2,1)}, bf16[128,1024]{0,1:T(8,128)(2,1)S(1)}, u32[]{:S(2)}, u32[]{:S(2)}) collective-permute-start(bf16[128,1024]{0,1:T(8,128)(2,1)} %bitcast.90), channel_id=1, source_target_pairs={{0,4},{1,20},{2,6},{3,22},{4,8},{5,24},{6,10},{7,26},{8,12},{9,28}... | collective-permute-start | bytes 786440 | tf_op jit(solution)/shard_map/ppermute | solution.py:602
  84.6 9.8 %collective-permute-start.15 = (bf16[128,1024]{0,1:T(8,128)(2,1)}, bf16[128,1024]{0,1:T(8,128)(2,1)S(1)}, u32[]{:S(2)}, u32[]{:S(2)}) collective-permute-start(bf16[128,1024]{0,1:T(8,128)(2,1)} %bitcast.91), channel_id=1, source_target_pairs={{0,8},{1,24},{2,10},{3,26},{4,12},{5,28},{6,14},{7,30},{8,0},{9,16... | collective-permute-start | bytes 786440 | tf_op jit(solution)/shard_map/ppermute | solution.py:602
  85.8 15.3 %collective-permute-start.16 = (bf16[128,1024]{0,1:T(8,128)(2,1)}, bf16[128,1024]{0,1:T(8,128)(2,1)S(1)}, u32[]{:S(2)}, u32[]{:S(2)}) collective-permute-start(bf16[128,1024]{0,1:T(8,128)(2,1)} %bitcast.92), channel_id=1, source_target_pairs={{0,12},{1,28},{2,14},{3,30},{4,0},{5,16},{6,2},{7,18},{8,4},{9,20}... | collective-permute-start | bytes 786440 | tf_op jit(solution)/shard_map/ppermute | solution.py:602
  88.5 37.3 %copy-start.68 = (bf16[128,1024]{0,1:T(8,128)(2,1)S(1)}, bf16[128,1024]{0,1:T(8,128)(2,1)}, u32[]{:S(2)}) copy-start(bf16[128,1024]{0,1:T(8,128)(2,1)} %copy-done.67) | copy-start | bytes 786436
  102.2 97.0 %collective-permute-start.17 = (bf16[512,1024]{0,1:T(8,128)(2,1)}, bf16[512,1024]{0,1:T(8,128)(2,1)}, u32[]{:S(2)}, u32[]{:S(2)}) collective-permute-start(bf16[512,1024]{0,1:T(8,128)(2,1)} %pad_maximum_fusion.16), channel_id=1, source_target_pairs={{0,1},{1,0},{2,3},{3,2},{4,5},{5,4},{6,7},{7,6},{8,9},{9,8},{10,11... | collective-permute-start | bytes 3145736 | tf_op jit(solution)/shard_map/ppermute | solution.py:539
  128.0 45.7 %copy-start.29 = (bf16[1024,1024]{0,1:T(8,128)(2,1)}, bf16[1024,1024]{0,1:T(8,128)(2,1)S(1)}, u32[]{:S(2)}) copy-start(bf16[1024,1024]{0,1:T(8,128)(2,1)S(1)} %multiply_convert_fusion.4) | copy-start | bytes 6291460
  131.4 70.3 %collective-permute-start.7 = (bf16[4,176,1024]{2,1,0:T(8,128)(2,1)}, bf16[4,176,1024]{2,1,0:T(8,128)(2,1)}, u32[]{:S(2)}, u32[]{:S(2)}) collective-permute-start(bf16[4,176,1024]{2,1,0:T(8,128)(2,1)} %constant_dynamic-slice_fusion.8), channel_id=1, source_target_pairs={{0,1},{1,0},{2,3},{3,2},{4,5},{5,4},{6,7},{7,6},{8,9},{9,8},{10,11... | collective-permute-start | bytes 4325384 | tf_op jit(solution)/shard_map/ppermute | solution.py:539
  198.7 7.1 collective-permute-start.5
  201.6 4.7 collective-permute-start.6
  295.3 7.8 collective-permute-start.18
  302.3 32.2 %collective-permute-start.29 = (bf16[4,176,1024]{2,1,0:T(8,128)(2,1)}, bf16[4,176,1024]{2,1,0:T(8,128)(2,1)}, u32[]{:S(2)}, u32[]{:S(2)}) collective-permute-start(bf16[4,176,1024]{2,1,0:T(8,128)(2,1)} %dynamic-slice_bitcast_fusion), channel_id=1, source_target_pairs={{0,1},{1,0},{2,3},{3,2},{4,5},{5,4},{6,7},{7,6},{8,9},{9,8},{10,11... | collective-permute-start | bytes 4325384 | tf_op jit(solution)/shard_map/ppermute | solution.py:539
  333.9 2.2 collective-permute-start.20
  337.3 214.0 %reduce-scatter.8.cloned.1.call-start = ((), (), s32[]{:S(2)}) async-start(), calls=%async_computation.8 | async-start | bytes 3244032 | tf_op jit(solution)/shard_map/reduce_scatter | solution.py:708
  339.2 324.8 %reduce-scatter.6.cloned.1.call-start = ((), (), s32[]{:S(2)}) async-start(), calls=%async_computation.7 | async-start | bytes 6488064 | tf_op jit(solution)/shard_map/reduce_scatter | solution.py:712
  352.8 402.5 %reduce-scatter.4.cloned.1.call-start = ((), (), s32[]{:S(2)}) async-start(), calls=%async_computation.5 | async-start | bytes 4718592 | tf_op jit(solution)/shard_map/reduce_scatter | solution.py:735
  365.3 17.8 %collective-permute-start.8 = (f32[512,1024]{0,1:T(8,128)}, f32[512,1024]{0,1:T(8,128)}, u32[]{:S(2)}, u32[]{:S(2)}) collective-permute-start(f32[512,1024]{0,1:T(8,128)} %slice.220), channel_id=1, source_target_pairs={{0,1},{1,0},{2,3},{3,2},{4,5},{5,4},{6,7},{7,6},{8,9},{9,8},{10,11... | collective-permute-start | bytes 6291464 | tf_op jit(solution)/shard_map/ppermute | solution.py:539
  382.7 74.2 %collective-permute-start.19 = (f32[512,1024]{0,1:T(8,128)}, f32[512,1024]{0,1:T(8,128)S(1)}, u32[]{:S(2)}, u32[]{:S(2)}) collective-permute-start(f32[512,1024]{0,1:T(8,128)} %slice.230), channel_id=1, source_target_pairs={{0,1},{1,0},{2,3},{3,2},{4,5},{5,4},{6,7},{7,6},{8,9},{9,8},{10,11... | collective-permute-start | bytes 6291464 | tf_op jit(solution)/shard_map/ppermute | solution.py:539
  388.9 67.7 %collective-permute-start.9 = (bf16[128,1024]{0,1:T(8,128)(2,1)}, bf16[128,1024]{0,1:T(8,128)(2,1)S(1)}, u32[]{:S(2)}, u32[]{:S(2)}) collective-permute-start(bf16[128,1024]{0,1:T(8,128)(2,1)} %get-tuple-element.99), channel_id=1, source_target_pairs={{0,0},{16,1},{2,2},{18,3},{4,4},{20,5},{6,6},{22,7},{8,8},{24,9},{... | collective-permute-start | bytes 786440 | tf_op jit(solution)/shard_map/ppermute | solution.py:614
  390.5 66.1 %collective-permute-start.10 = (bf16[128,1024]{0,1:T(8,128)(2,1)}, bf16[128,1024]{0,1:T(8,128)(2,1)S(1)}, u32[]{:S(2)}, u32[]{:S(2)}) collective-permute-start(bf16[128,1024]{0,1:T(8,128)(2,1)} %get-tuple-element.98), channel_id=1, source_target_pairs={{4,0},{20,1},{6,2},{22,3},{8,4},{24,5},{10,6},{26,7},{12,8},{28,9}... | collective-permute-start | bytes 786440 | tf_op jit(solution)/shard_map/ppermute | solution.py:614
  390.6 66.0 %collective-permute-start.11 = (bf16[128,1024]{0,1:T(8,128)(2,1)}, bf16[128,1024]{0,1:T(8,128)(2,1)S(1)}, u32[]{:S(2)}, u32[]{:S(2)}) collective-permute-start(bf16[128,1024]{0,1:T(8,128)(2,1)} %get-tuple-element.97), channel_id=1, source_target_pairs={{8,0},{24,1},{10,2},{26,3},{12,4},{28,5},{14,6},{30,7},{0,8},{16,9... | collective-permute-start | bytes 786440 | tf_op jit(solution)/shard_map/ppermute | solution.py:614
  392.5 64.2 %collective-permute-start.12 = (bf16[128,1024]{0,1:T(8,128)(2,1)S(1)}, bf16[128,1024]{0,1:T(8,128)(2,1)S(1)}, u32[]{:S(2)}, u32[]{:S(2)}) collective-permute-start(bf16[128,1024]{0,1:T(8,128)(2,1)S(1)} %get-tuple-element.96), channel_id=1, source_target_pairs={{12,0},{28,1},{14,2},{30,3},{0,4},{16,5},{2,6},{18,7},{4,8},{20,9}... | collective-permute-start | bytes 786440 | tf_op jit(solution)/shard_map/ppermute | solution.py:614
  462.4 73.4 %collective-permute-start.21 = (bf16[128,1024]{0,1:T(8,128)(2,1)S(1)}, bf16[128,1024]{0,1:T(8,128)(2,1)S(1)}, u32[]{:S(2)}, u32[]{:S(2)}) collective-permute-start(bf16[128,1024]{0,1:T(8,128)(2,1)S(1)} %get-tuple-element.91), channel_id=1, source_target_pairs={{0,0},{16,1},{2,2},{18,3},{4,4},{20,5},{6,6},{22,7},{8,8},{24,9},{... | collective-permute-start | bytes 786440 | tf_op jit(solution)/shard_map/ppermute | solution.py:614
  464.5 72.0 %collective-permute-start.22 = (bf16[128,1024]{0,1:T(8,128)(2,1)S(1)}, bf16[128,1024]{0,1:T(8,128)(2,1)S(1)}, u32[]{:S(2)}, u32[]{:S(2)}) collective-permute-start(bf16[128,1024]{0,1:T(8,128)(2,1)S(1)} %get-tuple-element.90), channel_id=1, source_target_pairs={{4,0},{20,1},{6,2},{22,3},{8,4},{24,5},{10,6},{26,7},{12,8},{28,9}... | collective-permute-start | bytes 786440 | tf_op jit(solution)/shard_map/ppermute | solution.py:614
  468.2 69.1 %collective-permute-start.23 = (bf16[128,1024]{0,1:T(8,128)(2,1)S(1)}, bf16[128,1024]{0,1:T(8,128)(2,1)S(1)}, u32[]{:S(2)}, u32[]{:S(2)}) collective-permute-start(bf16[128,1024]{0,1:T(8,128)(2,1)S(1)} %get-tuple-element.89), channel_id=1, source_target_pairs={{8,0},{24,1},{10,2},{26,3},{12,4},{28,5},{14,6},{30,7},{0,8},{16,9... | collective-permute-start | bytes 786440 | tf_op jit(solution)/shard_map/ppermute | solution.py:614
  468.2 69.8 %collective-permute-start.24 = (bf16[128,1024]{0,1:T(8,128)(2,1)S(1)}, bf16[128,1024]{0,1:T(8,128)(2,1)S(1)}, u32[]{:S(2)}, u32[]{:S(2)}) collective-permute-start(bf16[128,1024]{0,1:T(8,128)(2,1)S(1)} %get-tuple-element.88), channel_id=1, source_target_pairs={{12,0},{28,1},{14,2},{30,3},{0,4},{16,5},{2,6},{18,7},{4,8},{20,9}... | collective-permute-start | bytes 786440 | tf_op jit(solution)/shard_map/ppermute | solution.py:614
  551.2 115.7 %collective-permute-start.30 = (bf16[176,1024]{1,0:T(8,128)(2,1)}, bf16[176,1024]{1,0:T(8,128)(2,1)S(1)}, u32[]{:S(2)}, u32[]{:S(2)}) collective-permute-start(bf16[176,1024]{1,0:T(8,128)(2,1)} %reduce-scatter.8.cloned.1.call-done), channel_id=1, source_target_pairs={{0,2},{2,0},{1,3},{3,1},{4,6},{6,4},{5,7},{7,5},{8,10},{10,8},{9,1... | collective-permute-start | bytes 1081352 | tf_op jit(solution)/shard_map/ppermute | solution.py:543
  664.0 17.9 %collective-permute-start.27 = (bf16[128,2816]{1,0:T(8,128)(2,1)}, bf16[128,2816]{1,0:T(8,128)(2,1)S(1)}, u32[]{:S(2)}, u32[]{:S(2)}) collective-permute-start(bf16[128,2816]{1,0:T(8,128)(2,1)} %reduce-scatter.6.cloned.1.call-done), channel_id=1, source_target_pairs={{0,2},{2,0},{1,3},{3,1},{4,6},{6,4},{5,7},{7,5},{8,10},{10,8},{9,1... | collective-permute-start | bytes 2162696 | tf_op jit(solution)/shard_map/ppermute | solution.py:543
  668.8 90.6 %collective-permute-start.31 = (f32[176,1024]{1,0:T(8,128)}, f32[176,1024]{1,0:T(8,128)}, u32[]{:S(2)}, u32[]{:S(2)}) collective-permute-start(f32[176,1024]{1,0:T(8,128)} %convert_add_fusion.3), channel_id=1, source_target_pairs={{0,1},{1,0},{2,3},{3,2},{4,5},{5,4},{6,7},{7,6},{8,9},{9,8},{10,11... | collective-permute-start | bytes 2162696 | tf_op jit(solution)/shard_map/ppermute | solution.py:539
  682.1 88.5 %collective-permute-start.28 = (f32[128,2816]{1,0:T(8,128)S(1)}, f32[128,2816]{1,0:T(8,128)}, u32[]{:S(2)}, u32[]{:S(2)}) collective-permute-start(f32[128,2816]{1,0:T(8,128)S(1)} %convert_add_fusion.1), channel_id=1, source_target_pairs={{0,1},{1,0},{2,3},{3,2},{4,5},{5,4},{6,7},{7,6},{8,9},{9,8},{10,11... | collective-permute-start | bytes 4325384 | tf_op jit(solution)/shard_map/ppermute | solution.py:539
  683.6 75.8 %copy-start.48 = (bf16[176,1024]{1,0:T(8,128)(2,1)S(1)}, bf16[176,1024]{1,0:T(8,128)(2,1)}, u32[]{:S(2)}) copy-start(bf16[176,1024]{1,0:T(8,128)(2,1)} %reduce-scatter.8.cloned.1.call-done) | copy-start | bytes 1081348
  755.3 14.0 %collective-permute-start.25 = (bf16[128,2048]{1,0:T(8,128)(2,1)}, bf16[128,2048]{1,0:T(8,128)(2,1)}, u32[]{:S(2)}, u32[]{:S(2)}) collective-permute-start(bf16[128,2048]{1,0:T(8,128)(2,1)} %reduce-scatter.4.cloned.1.call-done), channel_id=1, source_target_pairs={{0,2},{2,0},{1,3},{3,1},{4,6},{6,4},{5,7},{7,5},{8,10},{10,8},{9,1... | collective-permute-start | bytes 1572872 | tf_op jit(solution)/shard_map/ppermute | solution.py:543
  770.5 4.0 collective-permute-start.26
  (78 other events, 551.8 us)
Sparse Core Ops, SparseCore 0:
  10.8 71.5 all-gather.8
  85.1 85.4 all-gather.4
  172.8 90.8 all-gather.6
  337.4 117.8 all-reduce.3
  458.7 92.5 reduce-scatter.7
  554.7 109.2 reduce-scatter.5
  667.6 87.6 reduce-scatter.3

commit v2 on v1

--- a/solution.py
+++ b/solution.py
@@ -543,6 +543,67 @@
     return lax.ppermute(a, "x", [(0, 1), (1, 0)])
 
 
+def ring_order(shards):
+    return list(range(0, shards, 2)) + list(range(shards - 1, 0, -2))
+
+
+class Ring:
+    def __init__(self):
+        self.shards, self.xs = lax.axis_size("shard"), lax.axis_size("x")
+        self.core = lax.axis_index("core")
+        cycle = ring_order(self.shards)
+        spot = [cycle.index(s) for s in range(self.shards)]
+        self.cycle = jnp.asarray(cycle, jnp.int32)
+        self.spot = jnp.asarray(spot, jnp.int32)[lax.axis_index("shard")]
+        self.sign = 1 - 2 * self.core
+        self.pairs = []
+        for s in range(self.shards):
+            for x in range(self.xs):
+                for c in range(2):
+                    step = 1 if c == 0 else -1
+                    to = cycle[(spot[s] + step) % self.shards]
+                    self.pairs.append(
+                        (device_of(s, x, c, self.xs), device_of(to, x, c, self.xs))
+                    )
+
+    def behind(self, hops):
+        return self.cycle[(self.spot - self.sign * hops) % self.shards]
+
+    def send(self, a):
+        return lax.ppermute(a, AXES, self.pairs)
+
+    def gather(self, piece):
+        whole = jnp.zeros((self.shards,) + piece.shape, piece.dtype)
+        pieces = [piece]
+        for _ in range(self.shards - 1):
+            pieces.append(self.send(pieces[-1]))
+        for hops, a in enumerate(pieces):
+            whole = lax.dynamic_update_index_in_dim(whole, a, self.behind(hops), 0)
+        return whole, pieces
+
+    def scatter(self, blocks):
+        def own(hops):
+            return lax.dynamic_index_in_dim(blocks, self.behind(hops), 0, False)
+
+        moving = own(1)
+        for hops in range(2, self.shards + 1):
+            arrived = self.send(moving)
+            moving = (arrived.astype(F32) + own(hops).astype(F32)).astype(BF16)
+        return moving
+
+
+def tree_sum(a):
+    shards = lax.axis_size("shard")
+    a = a + core_swap(a)
+    if lax.axis_size("x") == 2:
+        a = a + x_swap(a)
+    step = 1
+    while step < shards:
+        a = a + lax.ppermute(a, "shard", [(s, s ^ step) for s in range(shards)])
+        step *= 2
+    return a
+
+
 def by_core(mine, other, axis):
     first = lax.axis_index("core") == 0
     return jnp.concatenate(
@@ -641,12 +702,17 @@
     )
     wide = 2 * ck + 2 * cv
     own = rows_in(tokens)
-    attn_full = lax.all_gather(packed, "shard", axis=0, tiled=True)
-    ffn_cols = lax.all_gather(
-        jnp.concatenate([core_half(w_gate, 1), core_half(w_up, 1)], 1), "shard", axis=0, tiled=True
-    )
-    down_rows = lax.all_gather(core_half(w_down, 0), "shard", axis=0)
-    own_grad = rows_in(out_grad)
+    ring = Ring()
+    attn_full, attn_pieces = ring.gather(packed)
+    attn_full = attn_full.reshape(width, -1)
+    cols_piece = jnp.concatenate([core_half(w_gate, 1), core_half(w_up, 1)], 1)
+    cols_piece, down_piece, grad_in, _ = lax.optimization_barrier(
+        (cols_piece, core_half(w_down, 0), out_grad, attn_pieces[-2])
+    )
+    ffn_cols, _ = ring.gather(cols_piece)
+    ffn_cols = ffn_cols.reshape(width, -1)
+    down_rows, _ = ring.gather(down_piece)
+    own_grad = rows_in(grad_in)
 
     x_low = jnp.concatenate([own, core_swap(own)], 0)
     inputs = x_low.astype(F32)
@@ -705,13 +771,9 @@
     mine_dg = lax.dynamic_index_in_dim(down_grad, core, 1, False)
     other_dg = core_swap(lax.dynamic_index_in_dim(down_grad, 1 - core, 1, False))
     down_grad = by_core(mine_dg, other_dg, 0)
-    down_own = lax.psum_scatter(
-        down_grad.reshape(-1, width), "shard", scatter_dimension=0, tiled=True
-    )
-    gateup_grad = jnp.concatenate([outer_sum(ffn_in, d_gate), outer_sum(ffn_in, d_up)], 1)
-    gateup_own = lax.psum_scatter(
-        gateup_grad.astype(BF16), "shard", scatter_dimension=0, tiled=True
-    )
+    down_own = ring.scatter(down_grad)
+    gate_own = ring.scatter(outer_sum(ffn_in, d_gate).astype(BF16).reshape(shards, -1, ff_half))
+    up_own = ring.scatter(outer_sum(ffn_in, d_up).astype(BF16).reshape(shards, -1, ff_half))
 
     dn_part = times_transpose(d_gate, w_gate_half) + times_transpose(d_up, w_up_half)
     dn_ffn = dn_part + swap_rows(core_swap(dn_part))
@@ -727,17 +789,13 @@
         order, queries, keys, values, logits, out_gate, mixed, d_gated, states, gain,
         sums, masks, upper
     )
-    rank_out_grad = outer_sum(d_logits, rank_rows)
+    rank_out_grad = outer_sum(rank_rows, d_logits)
     rank_part = product(d_logits, rank_out)
     d_rank = (rank_part + swap_rows(core_swap(rank_part))).astype(BF16)
-    rank_in_grad = outer_sum(normed[:half_rows], d_rank[:half_rows])
+    rank_in_grad = outer_sum(d_rank[:half_rows], normed[:half_rows])
     qkvo_grad = outer_sum(normed, d_all)
-    attn_own = lax.psum_scatter(
-        jnp.concatenate([qkvo_grad, out_w_grad], 1).astype(BF16),
-        "shard",
-        scatter_dimension=0,
-        tiled=True,
-    )
+    attn_own = ring.scatter(qkvo_grad.astype(BF16).reshape(shards, -1, wide))
+    wout_own = ring.scatter(out_w_grad.astype(BF16).reshape(shards, -1, cv))
     dn_attn = times_transpose(d_all, w_qkvo)
     dn_own = (
         dn_attn[:half_rows]
@@ -754,25 +812,37 @@
     attn_gain_grad = jnp.sum(dn_own * own_in * own_r, axis=0)
 
     first = (core == 0).astype(F32)
-    bias_both = jnp.concatenate([bias_part[0] * first, bias_part[0] * (1.0 - first)], 0)
-    rank_out_both = jnp.concatenate([rank_out_grad * first, rank_out_grad * (1.0 - first)], 0)
-    small = lax.psum(
-        (attn_gain_grad, bias_both, hgain_part[0], ffn_gain_grad, rank_in_grad, rank_out_both),
-        AXES,
-    )
+
+    def spread(a):
+        return jnp.concatenate([a * first, a * (1.0 - first)], 1)
+
+    rank_out_both = spread(rank_out_grad)
+    lanes = 128
+
+    def flat(a):
+        return a.reshape(-1, lanes)
+
+    parts = (
+        attn_gain_grad[None], spread(bias_part), hgain_part, ffn_gain_grad[None],
+        rank_in_grad, rank_out_both,
+    )
+    small = tree_sum(jnp.concatenate([flat(a) for a in parts], 0))
+    pieces, at = [], 0
+    for a in parts:
+        size = a.size // lanes
+        pieces.append(small[at : at + size].reshape(a.shape))
+        at += size
     rin_rows, rout_rows = w_rank_in.shape[0], w_rank_out.shape[0]
-    rank_in_own = lax.dynamic_slice_in_dim(small[4], place * rin_rows, rin_rows, 0)
-    rank_out_own = lax.dynamic_slice_in_dim(small[5], place * rout_rows, rout_rows, 0)
-
-    def settle(a):
-        total = a.astype(F32)
+    rank_in_own = lax.dynamic_slice_in_dim(pieces[4], place * rin_rows, rin_rows, 1).T
+    rank_out_own = lax.dynamic_slice_in_dim(pieces[5].T, place * rout_rows, rout_rows, 0)
+
+    def settle(moving):
+        total = moving.astype(F32)
         if xs == 2:
-            total = total + x_swap(a).astype(F32)
+            total = total + x_swap(moving).astype(F32)
         return total, core_swap(total)
 
     attn_mine, attn_other = settle(attn_own)
-    gu_mine, gu_other = settle(gateup_own)
-    down_mine, down_other = settle(down_own)
 
     def columns(mine, other, start, size):
         return by_core(mine[:, start : start + size], other[:, start : start + size], 1)
@@ -780,20 +850,20 @@
     return (
         block_out,
         tokens_grad,
-        small[0],
+        pieces[0][0],
         columns(attn_mine, attn_other, 0, ck),
         columns(attn_mine, attn_other, ck, ck),
         columns(attn_mine, attn_other, 2 * ck, cv),
         columns(attn_mine, attn_other, 2 * ck + cv, cv),
         rank_in_own,
         rank_out_own,
-        small[1],
-        small[2],
-        columns(attn_mine, attn_other, wide, cv),
-        small[3],
-        columns(gu_mine, gu_other, 0, ff_half),
-        columns(gu_mine, gu_other, ff_half, ff_half),
-        by_core(down_mine, down_other, 0),
+        pieces[1][0],
+        pieces[2][0],
+        by_core(*settle(wout_own), 1),
+        pieces[3][0],
+        by_core(*settle(gate_own), 1),
+        by_core(*settle(up_own), 1),
+        by_core(*settle(down_own), 0),
     )
 
 

time: 794 us -> 636 us (0.80)
  waiting for transfers between devices: 397 us -> 210 us
  blocking collectives: 65.8 us -> 0 us
  starting transfers between devices: 84.1 us -> 137 us
  matrix products: 79.9 us -> 93.3 us
  between operations: 15.9 us -> 27.8 us
  local copies, waits for them, and re-layouts: 64.6 us -> 75.3 us
    reduce_scatter x3 -> x0, waiting for transfers between devices: 195 us -> none  [the longest x1 111 us: body(): lax.psum_scatter(gateup_grad.astype(BF16), 'shard', scatter_dimension=0,...]
    ppermute x0 -> x59, waiting for transfers between devices: none -> 192 us  [the longest x56 186 us: send(): return lax.ppermute(a, AXES, self.pairs)]
    all_gather x3 -> x0, waiting for transfers between devices: 87.1 us -> none  [the longest x1 47.8 us: body(): lax.all_gather(jnp.concatenate([core_half(w_gate, 1), core_half(w_up, 1)]...]
    ppermute x0 -> x59, starting transfers between devices: none -> 83.6 us  [the longest x56 71.2 us: send(): return lax.ppermute(a, AXES, self.pairs)]
    psum x1 -> x0, blocking collectives: 65.8 us -> none  [body(): lax.psum((attn_gain_grad, bias_both, hgain_part[0], ffn_gain_grad, rank_i...]
    psum x1 -> x0, waiting for transfers between devices: 62.3 us -> none  [body(): lax.psum((attn_gain_grad, bias_both, hgain_part[0], ffn_gain_grad, rank_i...]
    ppermute x13 -> x16, starting transfers between devices: 58.4 us -> 19.5 us  [core_swap(): return lax.ppermute(a, 'core', [(0, 1), (1, 0)])]
    ppermute x8, waiting for transfers between devices: 31.3 us -> 5.01 us  [rows_in(): lax.ppermute(lax.dynamic_index_in_dim(a, (step + piece) % seqs, 0, False)...]
  transfers between devices with their start and end apart: 39 -> 97, of which waited for: 13 -> 45; matrix products, arithmetic and copies ran while one was open for 17% -> 25% of each run, Pallas kernels for 4% -> 5%
where the time goes in v2:
time: 636 us; the launch traced here: 628 us
  waiting for transfers between devices  210 us (33%)
  starting transfers between devices  137 us (22%)
  matrix products  93.3 us (15%)
  local copies, waits for them, and re-layouts  75.3 us (12%)
  other arithmetic  50.8 us (8%)
  Pallas kernels  33.1 us (5%)
  between operations  27.8 us (4%)
    ppermute x56, waiting for transfers between devices, send(): return lax.ppermute(a, AXES, self.pairs)  186 us
    ppermute x56, starting transfers between devices, send(): return lax.ppermute(a, AXES, self.pairs)  71.2 us
    dot_general x10, matrix products, product(): return jnp.dot(left_side, right_side, preferred_element_type=jnp.float32)  38 us
    dot_general x7, matrix products, times_transpose(): lax.dot_general(left_side, right_side, (((1,), (1,)), ((), ())), preferre...  30.1 us
    dot_general x7, matrix products, outer_sum(): lax.dot_general(left_side, right_side, (((0,), (0,)), ((), ())), preferre...  25.2 us
    unnamed x158, local copies, waits for them, and re-layouts  21.4 us
    ppermute x16, starting transfers between devices, core_swap(): return lax.ppermute(a, 'core', [(0, 1), (1, 0)])  19.5 us
    dynamic_update_slice x24, local copies, waits for them, and re-layouts, gather(): whole = lax.dynamic_update_index_in_dim(whole, a, self.behind(hops), 0)  18.7 us
  transfers between devices with their start and end apart: 97, of which 45 were waited for; matrix products, arithmetic and copies ran while one was open for 25% of the time, Pallas kernels for 5%

profile of v2, /device:TPU:0, one launch (start us, length us, event | category | flops | bytes accessed | tf_op | source)
XLA Modules:
  0.0 627.8 jit_solution(19665562939236445)
XLA Ops:
  50.9 4.9 collective-permute-start.4
  61.9 7.8 %collective-permute-done.6 = bf16[128,2176]{1,0:T(8,128)(2,1)S(1)} collective-permute-done((bf16[128,2176]{1,0:T(8,128)(2,1)}, bf16[128,2176]{1,0:T(8,128)(2,1)S(1)}, u32[]{:S(2)}, u32[]{:S(2)}) %collective-permute-start.6) | collective-permute-done | bytes 557088 | tf_op jit(solution)/shard_map/ppermute | solution.py:573
  80.1 8.7 %collective-permute-done.8 = bf16[128,2176]{1,0:T(8,128)(2,1)S(1)} collective-permute-done((bf16[128,2176]{1,0:T(8,128)(2,1)S(1)}, bf16[128,2176]{1,0:T(8,128)(2,1)S(1)}, u32[]{:S(2)}, u32[]{:S(2)}) %collective-permute-start.8) | collective-permute-done | bytes 557088 | tf_op jit(solution)/shard_map/ppermute | solution.py:573
  89.6 8.7 %collective-permute-done.9 = bf16[128,2176]{1,0:T(8,128)(2,1)S(1)} collective-permute-done((bf16[128,2176]{1,0:T(8,128)(2,1)S(1)}, bf16[128,2176]{1,0:T(8,128)(2,1)S(1)}, u32[]{:S(2)}, u32[]{:S(2)}) %collective-permute-start.9) | collective-permute-done | bytes 557088 | tf_op jit(solution)/shard_map/ppermute | solution.py:573
  99.1 8.7 %collective-permute-done.10 = bf16[128,2176]{1,0:T(8,128)(2,1)S(1)} collective-permute-done((bf16[128,2176]{1,0:T(8,128)(2,1)S(1)}, bf16[128,2176]{1,0:T(8,128)(2,1)S(1)}, u32[]{:S(2)}, u32[]{:S(2)}) %collective-permute-start.10) | collective-permute-done | bytes 557088 | tf_op jit(solution)/shard_map/ppermute | solution.py:573
  113.3 3.7 collective-permute-start.34
  130.3 3.7 collective-permute-done.36
  137.5 6.5 %collective-permute-start.38 = (bf16[512,1024]{0,1:T(8,128)(2,1)}, bf16[512,1024]{0,1:T(8,128)(2,1)S(1)}, u32[]{:S(2)}, u32[]{:S(2)}) collective-permute-start(bf16[512,1024]{0,1:T(8,128)(2,1)} %pad_maximum_fusion.13), channel_id=1, source_target_pairs={{0,1},{1,0},{2,3},{3,2},{4,5},{5,4},{6,7},{7,6},{8,9},{9,8},{10,11... | collective-permute-start | bytes 3145736 | tf_op jit(solution)/shard_map/ppermute | solution.py:539
  147.2 7.3 %collective-permute-start.22 = (bf16[176,1024]{1,0:T(8,128)(2,1)S(1)}, bf16[176,1024]{1,0:T(8,128)(2,1)S(1)}, u32[]{:S(2)}, u32[]{:S(2)}) collective-permute-start(bf16[176,1024]{1,0:T(8,128)(2,1)S(1)} %collective-permute-done.21), channel_id=1, source_target_pairs={{0,8},{1,5},{2,10},{3,7},{4,0},{5,13},{6,2},{7,15},{8,16},{9,1},{1... | collective-permute-start | bytes 1081352 | tf_op jit(solution)/shard_map/ppermute | solution.py:573
  168.4 17.5 %mix_forward.1 = (bf16[1024,512]{1,0:T(8,128)(2,1)S(1)}, f32[1024,512]{1,0:T(8,128)S(1)}, f32[8,2,256,128]{3,2,1,0:T(8,128)S(1)}) custom-call(s32[8]{0:T(128)S(1)} %fusion.88.order, bf16[1024,256]{1,0:T(8,128)(2,1)S(1)} %convolution_convert_fusion.7.q_ref, bf16[1024,256]{1,0:T(8,128)(2,1)S(1)} %convolution_convert_fusion.6.k_ref, ...), custom_call_target="tpu_custom_call" | custom-call | tf_op jit(solution)/shard_map/mix_forward/pallas_call | solution.py:484
  189.9 12.0 %collective-permute-done.23 = bf16[176,1024]{1,0:T(8,128)(2,1)S(1)} collective-permute-done((bf16[176,1024]{1,0:T(8,128)(2,1)S(1)}, bf16[176,1024]{1,0:T(8,128)(2,1)S(1)}, u32[]{:S(2)}, u32[]{:S(2)}) %collective-permute-start.23) | collective-permute-done | bytes 360480 | tf_op jit(solution)/shard_map/ppermute | solution.py:573
  204.3 5.0 collective-permute-done.24
  215.0 5.9 collective-permute-done.25
  222.7 5.6 collective-permute-done.26
  228.4 11.5 %collective-permute-done.27 = bf16[176,1024]{1,0:T(8,128)(2,1)S(1)} collective-permute-done((bf16[176,1024]{1,0:T(8,128)(2,1)S(1)}, bf16[176,1024]{1,0:T(8,128)(2,1)S(1)}, u32[]{:S(2)}, u32[]{:S(2)}) %collective-permute-start.27) | collective-permute-done | bytes 360480 | tf_op jit(solution)/shard_map/ppermute | solution.py:573
  242.1 9.4 %collective-permute-done.18 = bf16[128,2816]{1,0:T(8,128)(2,1)S(1)} collective-permute-done((bf16[128,2816]{1,0:T(8,128)(2,1)S(1)}, bf16[128,2816]{1,0:T(8,128)(2,1)S(1)}, u32[]{:S(2)}, u32[]{:S(2)}) %collective-permute-start.18) | collective-permute-done | bytes 720928 | tf_op jit(solution)/shard_map/ppermute | solution.py:573
  252.9 9.9 %collective-permute-done.19 = bf16[128,2816]{1,0:T(8,128)(2,1)S(1)} collective-permute-done((bf16[128,2816]{1,0:T(8,128)(2,1)S(1)}, bf16[128,2816]{1,0:T(8,128)(2,1)S(1)}, u32[]{:S(2)}, u32[]{:S(2)}) %collective-permute-start.19) | collective-permute-done | bytes 720928 | tf_op jit(solution)/shard_map/ppermute | solution.py:573
  263.2 5.3 fusion.104
  269.5 5.0 collective-permute-done.20
  275.4 7.2 %fusion.5 = f32[1024,1408]{1,0:T(8,128)} fusion(bf16[1024,1024]{0,1:T(8,128)(2,1)S(1)} %multiply_convert_fusion.3, bf16[1024,2816]{1,0:T(8,128)(2,1)} %bitcast.33), kind=kOutput, calls=%fused_computation.38 | convolution fusion | flops 2952790016 | bytes 10747904 | tf_op jit(solution)/shard_map/dot_general | solution.py:40
  282.6 11.2 %multiply_convert_fusion.1 = (bf16[1024,1408]{1,0:T(8,128)(2,1)}, bf16[1024,1408]{1,0:T(8,128)(2,1)}, bf16[1024,1408]{1,0:T(8,128)(2,1)S(1)}) fusion(f32[1024,1408]{1,0:T(8,128)} %fusion.104, f32[1024,1408]{1,0:T(8,128)} %fusion.5, bf16[1024,1024]{0,1:T(8,128)(2,1)S(1)} %multiply_convert_fusion.3, bf16[1024,2816]{1,0:T(8,128)(2,1)} %bitcast.33), kind=kOutput, calls=%fused_computation.1 | convolution fusion | flops 2974416896 | bytes 25165824 | tf_op jit(solution)/shard_map/dot_general | solution.py:40
  293.8 6.5 %convolution_convert_fusion.1 = bf16[1024,1408]{1,0:T(8,128)(2,1)S(1)} fusion(bf16[1024,1024]{0,1:T(8,128)(2,1)S(1)} %multiply_convert_fusion.3, bf16[1024,1408]{1,0:T(8,128)(2,1)} %get-tuple-element.59), kind=kOutput, calls=%fused_computation.29 | convolution fusion | flops 2954231808 | bytes 7864320 | tf_op jit(solution)/shard_map/dot_general | solution.py:50
  300.4 7.9 %fusion.3 = f32[1024,1024]{0,1:T(8,128)} fusion(bf16[1024,1408]{1,0:T(8,128)(2,1)S(1)} %copy-done.65, bf16[1024,2816]{1,0:T(8,128)(2,1)} %bitcast.33), kind=kOutput, calls=%fused_computation.36 | convolution fusion | flops 2952790016 | bytes 9961472 | tf_op jit(solution)/shard_map/dot_general | solution.py:44
  308.3 3.7 convolution_convert_fusion
  312.0 6.4 %fusion.103 = f32[1024,1024]{0,1:T(8,128)S(1)} fusion(bf16[1024,1408]{1,0:T(8,128)(2,1)} %copy-done.64, bf16[1408,1024]{1,0:T(8,128)(2,1)S(1)} %bitcast.278), kind=kOutput, calls=%fused_computation.326 | convolution fusion | flops 2952790016 | bytes 9961472 | tf_op jit(solution)/shard_map/dot_general | solution.py:40
  321.6 5.6 convolution_convert_fusion.2
  328.8 6.2 fusion.18
  342.0 4.0 collective-permute-done.79
  394.1 6.1 collective-permute-done.90
  403.4 4.5 collective-permute-done.91
  409.8 6.0 collective-permute-done.92
  417.5 6.0 collective-permute-done.93
  427.7 3.5 collective-permute-done.94
  435.3 3.9 fusion.96
  445.9 15.6 %mix_backward.1 = (bf16[1024,1536]{1,0:T(8,128)(2,1)}, bf16[1024,256]{1,0:T(8,128)(2,1)S(1)}, f32[1,256]{1,0:T(1,128)S(1)}, f32[1,256]{1,0:T(1,128)S(1)}) custom-call(s32[8]{0:T(128)S(1)} %fusion.88.order, bf16[1024,256]{1,0:T(8,128)(2,1)S(1)} %convolution_convert_fusion.7.q_ref, bf16[1024,256]{1,0:T(8,128)(2,1)S(1)} %convolution_convert_fusion.6.k_ref, ...), custom_call_target="tpu_custom_call" | custom-call | tf_op jit(solution)/shard_map/mix_backward/pallas_call | solution.py:513
  461.5 5.5 convolution_convert_fusion.3
  473.0 6.4 %fusion.1 = f32[1024,1024]{0,1:T(8,128)S(1)} fusion(bf16[1024,1536]{1,0:T(8,128)(2,1)} %get-tuple-element.32, bf16[1024,2176]{1,0:T(8,128)(2,1)} %bitcast.21), kind=kOutput, calls=%fused_computation.32 | convolution fusion | flops 3221225472 | bytes 10485760 | tf_op jit(solution)/shard_map/dot_general | solution.py:44
  499.1 6.3 collective-permute-done.61
  505.4 5.8 collective-permute-start.96
  512.2 4.7 collective-permute-start.62
  533.5 4.1 collective-permute-done.65
  552.2 5.5 collective-permute-done.54
  571.1 4.7 collective-permute-start.44
  577.4 10.6 %collective-permute-done.44 = bf16[128,1024]{0,1:T(8,128)(2,1)S(1)} collective-permute-done((bf16[128,1024]{0,1:T(8,128)(2,1)S(1)}, bf16[128,1024]{0,1:T(8,128)(2,1)S(1)}, u32[]{:S(2)}, u32[]{:S(2)}) %collective-permute-start.44) | collective-permute-done | bytes 262176 | tf_op jit(solution)/shard_map/ppermute | solution.py:675
  589.4 6.3 %collective-permute-start.57 = (bf16[128,1536]{1,0:T(8,128)(2,1)S(1)}, bf16[128,1536]{1,0:T(8,128)(2,1)S(1)}, u32[]{:S(2)}, u32[]{:S(2)}) collective-permute-start(bf16[128,1536]{1,0:T(8,128)(2,1)S(1)} %fusion.31), channel_id=1, source_target_pairs={{0,8},{1,5},{2,10},{3,7},{4,0},{5,13},{6,2},{7,15},{8,16},{9,1},{1... | collective-permute-start | bytes 1179656 | tf_op jit(solution)/shard_map/ppermute | solution.py:573
  595.8 5.2 collective-permute-done.57
  603.3 6.9 %collective-permute-start.49 = (f32[214,128]{1,0:T(8,128)S(1)}, f32[214,128]{1,0:T(8,128)S(1)}, u32[]{:S(2)}, u32[]{:S(2)}) collective-permute-start(f32[214,128]{1,0:T(8,128)S(1)} %add.633), channel_id=1, source_target_pairs={{0,8},{4,12},{8,0},{12,4},{16,24},{20,28},{24,16},{28,20},{1,9},{5... | collective-permute-start | bytes 328712 | tf_op jit(solution)/shard_map/ppermute | solution.py:602
  612.9 4.0 collective-permute-start.50
  (502 shorter events, 272.7 us)
Async XLA Ops:
  6.3 53.6 %collective-permute-start.5 = (bf16[128,2176]{1,0:T(8,128)(2,1)}, bf16[128,2176]{1,0:T(8,128)(2,1)}, u32[]{:S(2)}, u32[]{:S(2)}) collective-permute-start(bf16[128,2176]{1,0:T(8,128)(2,1)} %concatenate.76), channel_id=1, source_target_pairs={{0,8},{1,5},{2,10},{3,7},{4,0},{5,13},{6,2},{7,15},{8,16},{9,1},{1... | collective-permute-start | bytes 1671176 | tf_op jit(solution)/shard_map/ppermute | solution.py:573
  9.6 40.3 %collective-permute-start = (bf16[128,1024]{0,1:T(8,128)(2,1)S(1)}, bf16[128,1024]{0,1:T(8,128)(2,1)S(1)}, u32[]{:S(2)}, u32[]{:S(2)}) collective-permute-start(bf16[128,1024]{0,1:T(8,128)(2,1)S(1)} %bitcast.308), channel_id=1, source_target_pairs={{0,0},{1,16},{2,2},{3,18},{4,4},{5,20},{6,6},{7,22},{8,8},{9,24},{... | collective-permute-start | bytes 786440 | tf_op jit(solution)/shard_map/ppermute | solution.py:663
  10.4 39.5 %collective-permute-start.1 = (bf16[128,1024]{0,1:T(8,128)(2,1)S(1)}, bf16[128,1024]{0,1:T(8,128)(2,1)S(1)}, u32[]{:S(2)}, u32[]{:S(2)}) collective-permute-start(bf16[128,1024]{0,1:T(8,128)(2,1)S(1)} %bitcast.309), channel_id=1, source_target_pairs={{0,4},{1,20},{2,6},{3,22},{4,8},{5,24},{6,10},{7,26},{8,12},{9,28}... | collective-permute-start | bytes 786440 | tf_op jit(solution)/shard_map/ppermute | solution.py:663
  11.3 38.6 %collective-permute-start.2 = (bf16[128,1024]{0,1:T(8,128)(2,1)}, bf16[128,1024]{0,1:T(8,128)(2,1)S(1)}, u32[]{:S(2)}, u32[]{:S(2)}) collective-permute-start(bf16[128,1024]{0,1:T(8,128)(2,1)} %bitcast.2), channel_id=1, source_target_pairs={{0,8},{1,24},{2,10},{3,26},{4,12},{5,28},{6,14},{7,30},{8,0},{9,16... | collective-permute-start | bytes 786440 | tf_op jit(solution)/shard_map/ppermute | solution.py:663
  14.1 35.8 %collective-permute-start.3 = (bf16[128,1024]{0,1:T(8,128)(2,1)}, bf16[128,1024]{0,1:T(8,128)(2,1)S(1)}, u32[]{:S(2)}, u32[]{:S(2)}) collective-permute-start(bf16[128,1024]{0,1:T(8,128)(2,1)} %bitcast.3), channel_id=1, source_target_pairs={{0,12},{1,28},{2,14},{3,30},{4,0},{5,16},{6,2},{7,18},{8,4},{9,20}... | collective-permute-start | bytes 786440 | tf_op jit(solution)/shard_map/ppermute | solution.py:663
  50.9 19.7 %collective-permute-start.4 = (bf16[512,1024]{0,1:T(8,128)(2,1)S(1)}, bf16[512,1024]{0,1:T(8,128)(2,1)S(1)}, u32[]{:S(2)}, u32[]{:S(2)}) collective-permute-start(bf16[512,1024]{0,1:T(8,128)(2,1)S(1)} %pad_maximum_fusion.11), channel_id=1, source_target_pairs={{0,1},{1,0},{2,3},{3,2},{4,5},{5,4},{6,7},{7,6},{8,9},{9,8},{10,11... | collective-permute-start | bytes 3145736 | tf_op jit(solution)/shard_map/ppermute | solution.py:539
  107.8 78.7 %collective-permute-start.14 = (bf16[128,2816]{1,0:T(8,128)(2,1)S(1)}, bf16[128,2816]{1,0:T(8,128)(2,1)}, u32[]{:S(2)}, u32[]{:S(2)}) collective-permute-start(bf16[128,2816]{1,0:T(8,128)(2,1)S(1)} %pad_maximum_fusion.14), channel_id=1, source_target_pairs={{0,8},{1,5},{2,10},{3,7},{4,0},{5,13},{6,2},{7,15},{8,16},{9,1},{1... | collective-permute-start | bytes 2162696 | tf_op jit(solution)/shard_map/ppermute | solution.py:573
  113.3 14.6 %collective-permute-start.34 = (bf16[128,1024]{0,1:T(8,128)(2,1)}, bf16[128,1024]{0,1:T(8,128)(2,1)}, u32[]{:S(2)}, u32[]{:S(2)}) collective-permute-start(bf16[128,1024]{0,1:T(8,128)(2,1)} %bitcast.313), channel_id=1, source_target_pairs={{0,0},{1,16},{2,2},{3,18},{4,4},{5,20},{6,6},{7,22},{8,8},{9,24},{... | collective-permute-start | bytes 786440 | tf_op jit(solution)/shard_map/ppermute | solution.py:663
  122.6 11.4 %collective-permute-start.36 = (bf16[128,1024]{0,1:T(8,128)(2,1)}, bf16[128,1024]{0,1:T(8,128)(2,1)}, u32[]{:S(2)}, u32[]{:S(2)}) collective-permute-start(bf16[128,1024]{0,1:T(8,128)(2,1)} %bitcast.310), channel_id=1, source_target_pairs={{0,8},{1,24},{2,10},{3,26},{4,12},{5,28},{6,14},{7,30},{8,0},{9,16... | collective-permute-start | bytes 786440 | tf_op jit(solution)/shard_map/ppermute | solution.py:663
  123.4 11.9 %collective-permute-start.37 = (bf16[128,1024]{0,1:T(8,128)(2,1)}, bf16[128,1024]{0,1:T(8,128)(2,1)S(1)}, u32[]{:S(2)}, u32[]{:S(2)}) collective-permute-start(bf16[128,1024]{0,1:T(8,128)(2,1)} %bitcast.312), channel_id=1, source_target_pairs={{0,12},{1,28},{2,14},{3,30},{4,0},{5,16},{6,2},{7,18},{8,4},{9,20}... | collective-permute-start | bytes 786440 | tf_op jit(solution)/shard_map/ppermute | solution.py:663
  127.9 19.3 %collective-permute-start.21 = (bf16[176,1024]{1,0:T(8,128)(2,1)S(1)}, bf16[176,1024]{1,0:T(8,128)(2,1)S(1)}, u32[]{:S(2)}, u32[]{:S(2)}) collective-permute-start(bf16[176,1024]{1,0:T(8,128)(2,1)S(1)} %copy-done.30), channel_id=1, source_target_pairs={{0,8},{1,5},{2,10},{3,7},{4,0},{5,13},{6,2},{7,15},{8,16},{9,1},{1... | collective-permute-start | bytes 1081352 | tf_op jit(solution)/shard_map/ppermute | solution.py:573
  128.8 25.8 %collective-permute-start.11 = (bf16[128,2176]{1,0:T(8,128)(2,1)S(1)}, bf16[128,2176]{1,0:T(8,128)(2,1)S(1)}, u32[]{:S(2)}, u32[]{:S(2)}) collective-permute-start(bf16[128,2176]{1,0:T(8,128)(2,1)S(1)} %copy-done.46), channel_id=1, source_target_pairs={{0,8},{1,5},{2,10},{3,7},{4,0},{5,13},{6,2},{7,15},{8,16},{9,1},{1... | collective-permute-start | bytes 1671176 | tf_op jit(solution)/shard_map/ppermute | solution.py:573
  137.5 64.5 %collective-permute-start.38 = (bf16[512,1024]{0,1:T(8,128)(2,1)}, bf16[512,1024]{0,1:T(8,128)(2,1)S(1)}, u32[]{:S(2)}, u32[]{:S(2)}) collective-permute-start(bf16[512,1024]{0,1:T(8,128)(2,1)} %pad_maximum_fusion.13), channel_id=1, source_target_pairs={{0,1},{1,0},{2,3},{3,2},{4,5},{5,4},{6,7},{7,6},{8,9},{9,8},{10,11... | collective-permute-start | bytes 3145736 | tf_op jit(solution)/shard_map/ppermute | solution.py:539
  147.2 39.3 %collective-permute-start.22 = (bf16[176,1024]{1,0:T(8,128)(2,1)S(1)}, bf16[176,1024]{1,0:T(8,128)(2,1)S(1)}, u32[]{:S(2)}, u32[]{:S(2)}) collective-permute-start(bf16[176,1024]{1,0:T(8,128)(2,1)S(1)} %collective-permute-done.21), channel_id=1, source_target_pairs={{0,8},{1,5},{2,10},{3,7},{4,0},{5,13},{6,2},{7,15},{8,16},{9,1},{1... | collective-permute-start | bytes 1081352 | tf_op jit(solution)/shard_map/ppermute | solution.py:573
  185.9 23.4 %collective-permute-start.12 = (bf16[1024,512]{1,0:T(8,128)(2,1)S(1)}, bf16[1024,512]{1,0:T(8,128)(2,1)S(1)}, u32[]{:S(2)}, u32[]{:S(2)}) collective-permute-start(bf16[1024,512]{1,0:T(8,128)(2,1)S(1)} %get-tuple-element.26), channel_id=1, source_target_pairs={{0,1},{1,0},{2,3},{3,2},{4,5},{5,4},{6,7},{7,6},{8,9},{9,8},{10,11... | collective-permute-start | bytes 3145736 | tf_op jit(solution)/shard_map/ppermute | solution.py:539
  186.0 23.9 %collective-permute-start.13 = (bf16[1024,512]{1,0:T(8,128)(2,1)S(1)}, bf16[1024,512]{1,0:T(8,128)(2,1)S(1)}, u32[]{:S(2)}, u32[]{:S(2)}) collective-permute-start(bf16[1024,512]{1,0:T(8,128)(2,1)S(1)} %slice.215), channel_id=1, source_target_pairs={{0,1},{1,0},{2,3},{3,2},{4,5},{5,4},{6,7},{7,6},{8,9},{9,8},{10,11... | collective-permute-start | bytes 3145736 | tf_op jit(solution)/shard_map/ppermute | solution.py:539
  186.5 15.6 %collective-permute-start.15 = (bf16[128,2816]{1,0:T(8,128)(2,1)}, bf16[128,2816]{1,0:T(8,128)(2,1)S(1)}, u32[]{:S(2)}, u32[]{:S(2)}) collective-permute-start(bf16[128,2816]{1,0:T(8,128)(2,1)} %collective-permute-done.14), channel_id=1, source_target_pairs={{0,8},{1,5},{2,10},{3,7},{4,0},{5,13},{6,2},{7,15},{8,16},{9,1},{1... | collective-permute-start | bytes 2162696 | tf_op jit(solution)/shard_map/ppermute | solution.py:573
  186.6 15.3 %collective-permute-start.23 = (bf16[176,1024]{1,0:T(8,128)(2,1)S(1)}, bf16[176,1024]{1,0:T(8,128)(2,1)S(1)}, u32[]{:S(2)}, u32[]{:S(2)}) collective-permute-start(bf16[176,1024]{1,0:T(8,128)(2,1)S(1)} %collective-permute-done.22), channel_id=1, source_target_pairs={{0,8},{1,5},{2,10},{3,7},{4,0},{5,13},{6,2},{7,15},{8,16},{9,1},{1... | collective-permute-start | bytes 1081352 | tf_op jit(solution)/shard_map/ppermute | solution.py:573
  202.1 19.2 %collective-permute-start.16 = (bf16[128,2816]{1,0:T(8,128)(2,1)S(1)}, bf16[128,2816]{1,0:T(8,128)(2,1)S(1)}, u32[]{:S(2)}, u32[]{:S(2)}) collective-permute-start(bf16[128,2816]{1,0:T(8,128)(2,1)S(1)} %collective-permute-done.15), channel_id=1, source_target_pairs={{0,8},{1,5},{2,10},{3,7},{4,0},{5,13},{6,2},{7,15},{8,16},{9,1},{1... | collective-permute-start | bytes 2162696 | tf_op jit(solution)/shard_map/ppermute | solution.py:573
  209.3 11.6 %collective-permute-start.25 = (bf16[176,1024]{1,0:T(8,128)(2,1)S(1)}, bf16[176,1024]{1,0:T(8,128)(2,1)S(1)}, u32[]{:S(2)}, u32[]{:S(2)}) collective-permute-start(bf16[176,1024]{1,0:T(8,128)(2,1)S(1)} %collective-permute-done.24), channel_id=1, source_target_pairs={{0,8},{1,5},{2,10},{3,7},{4,0},{5,13},{6,2},{7,15},{8,16},{9,1},{1... | collective-permute-start | bytes 1081352 | tf_op jit(solution)/shard_map/ppermute | solution.py:573
  221.3 18.8 %collective-permute-start.17 = (bf16[128,2816]{1,0:T(8,128)(2,1)S(1)}, bf16[128,2816]{1,0:T(8,128)(2,1)S(1)}, u32[]{:S(2)}, u32[]{:S(2)}) collective-permute-start(bf16[128,2816]{1,0:T(8,128)(2,1)S(1)} %collective-permute-done.16), channel_id=1, source_target_pairs={{0,8},{1,5},{2,10},{3,7},{4,0},{5,13},{6,2},{7,15},{8,16},{9,1},{1... | collective-permute-start | bytes 2162696 | tf_op jit(solution)/shard_map/ppermute | solution.py:573
  228.3 11.6 %collective-permute-start.27 = (bf16[176,1024]{1,0:T(8,128)(2,1)S(1)}, bf16[176,1024]{1,0:T(8,128)(2,1)S(1)}, u32[]{:S(2)}, u32[]{:S(2)}) collective-permute-start(bf16[176,1024]{1,0:T(8,128)(2,1)S(1)} %collective-permute-done.26), channel_id=1, source_target_pairs={{0,8},{1,5},{2,10},{3,7},{4,0},{5,13},{6,2},{7,15},{8,16},{9,1},{1... | collective-permute-start | bytes 1081352 | tf_op jit(solution)/shard_map/ppermute | solution.py:573
  240.1 12.4 %collective-permute-start.28 = (bf16[4,176,1024]{2,1,0:T(8,128)(2,1)S(1)}, bf16[4,176,1024]{2,1,0:T(8,128)(2,1)S(1)}, u32[]{:S(2)}, u32[]{:S(2)}) collective-permute-start(bf16[4,176,1024]{2,1,0:T(8,128)(2,1)S(1)} %constant_dynamic-slice_fusion.8), channel_id=1, source_target_pairs={{0,1},{1,0},{2,3},{3,2},{4,5},{5,4},{6,7},{7,6},{8,9},{9,8},{10,11... | collective-permute-start | bytes 4325384 | tf_op jit(solution)/shard_map/ppermute | solution.py:539
  262.8 11.7 %collective-permute-start.20 = (bf16[128,2816]{1,0:T(8,128)(2,1)S(1)}, bf16[128,2816]{1,0:T(8,128)(2,1)S(1)}, u32[]{:S(2)}, u32[]{:S(2)}) collective-permute-start(bf16[128,2816]{1,0:T(8,128)(2,1)S(1)} %collective-permute-done.19), channel_id=1, source_target_pairs={{0,8},{1,5},{2,10},{3,7},{4,0},{5,13},{6,2},{7,15},{8,16},{9,1},{1... | collective-permute-start | bytes 2162696 | tf_op jit(solution)/shard_map/ppermute | solution.py:573
  318.6 48.2 %collective-permute-start.87 = (bf16[4,176,1024]{2,1,0:T(8,128)(2,1)S(1)}, bf16[4,176,1024]{2,1,0:T(8,128)(2,1)}, u32[]{:S(2)}, u32[]{:S(2)}) collective-permute-start(bf16[4,176,1024]{2,1,0:T(8,128)(2,1)S(1)} %dynamic-slice_bitcast_fusion), channel_id=1, source_target_pairs={{0,1},{1,0},{2,3},{3,2},{4,5},{5,4},{6,7},{7,6},{8,9},{9,8},{10,11... | collective-permute-start | bytes 4325384 | tf_op jit(solution)/shard_map/ppermute | solution.py:539
  318.8 18.5 %collective-permute-start.78 = (bf16[128,1408]{1,0:T(8,128)(2,1)S(1)}, bf16[128,1408]{1,0:T(8,128)(2,1)}, u32[]{:S(2)}, u32[]{:S(2)}) collective-permute-start(bf16[128,1408]{1,0:T(8,128)(2,1)S(1)} %dynamic-slice_bitcast_fusion.2), channel_id=1, source_target_pairs={{0,8},{1,5},{2,10},{3,7},{4,0},{5,13},{6,2},{7,15},{8,16},{9,1},{1... | collective-permute-start | bytes 1081352 | tf_op jit(solution)/shard_map/ppermute | solution.py:573
  335.0 98.7 %collective-permute-start.39 = (f32[1024,1024]{0,1:T(8,128)S(1)}, f32[1024,1024]{0,1:T(8,128)S(1)}, u32[]{:S(2)}, u32[]{:S(2)}) collective-permute-start(f32[1024,1024]{0,1:T(8,128)S(1)} %fusion.18), channel_id=1, source_target_pairs={{0,1},{1,0},{2,3},{3,2},{4,5},{5,4},{6,7},{7,6},{8,9},{9,8},{10,11... | collective-permute-start | bytes 12582920 | tf_op jit(solution)/shard_map/ppermute | solution.py:539
  337.3 143.7 %collective-permute-start.29 = (f32[512,1024]{0,1:T(8,128)}, f32[512,1024]{0,1:T(8,128)}, u32[]{:S(2)}, u32[]{:S(2)}) collective-permute-start(f32[512,1024]{0,1:T(8,128)} %slice.220), channel_id=1, source_target_pairs={{0,1},{1,0},{2,3},{3,2},{4,5},{5,4},{6,7},{7,6},{8,9},{9,8},{10,11... | collective-permute-start | bytes 6291464 | tf_op jit(solution)/shard_map/ppermute | solution.py:539
  380.9 11.5 %collective-permute-start.84 = (bf16[128,1408]{1,0:T(8,128)(2,1)S(1)}, bf16[128,1408]{1,0:T(8,128)(2,1)S(1)}, u32[]{:S(2)}, u32[]{:S(2)}) collective-permute-start(bf16[128,1408]{1,0:T(8,128)(2,1)S(1)} %fusion.45), channel_id=1, source_target_pairs={{0,8},{1,5},{2,10},{3,7},{4,0},{5,13},{6,2},{7,15},{8,16},{9,1},{1... | collective-permute-start | bytes 1081352 | tf_op jit(solution)/shard_map/ppermute | solution.py:573
  384.8 16.9 %collective-permute-start.75 = (bf16[128,1408]{1,0:T(8,128)(2,1)S(1)}, bf16[128,1408]{1,0:T(8,128)(2,1)S(1)}, u32[]{:S(2)}, u32[]{:S(2)}) collective-permute-start(bf16[128,1408]{1,0:T(8,128)(2,1)S(1)} %fusion.52), channel_id=1, source_target_pairs={{0,8},{1,5},{2,10},{3,7},{4,0},{5,13},{6,2},{7,15},{8,16},{9,1},{1... | collective-permute-start | bytes 1081352 | tf_op jit(solution)/shard_map/ppermute | solution.py:573
  392.5 17.1 %collective-permute-start.85 = (bf16[128,1408]{1,0:T(8,128)(2,1)S(1)}, bf16[128,1408]{1,0:T(8,128)(2,1)S(1)}, u32[]{:S(2)}, u32[]{:S(2)}) collective-permute-start(bf16[128,1408]{1,0:T(8,128)(2,1)S(1)} %fusion.44), channel_id=1, source_target_pairs={{0,2},{2,0},{1,3},{3,1},{4,6},{6,4},{5,7},{7,5},{8,10},{10,8},{9,1... | collective-permute-start | bytes 1081352 | tf_op jit(solution)/shard_map/ppermute | solution.py:543
  401.8 15.5 %collective-permute-start.76 = (bf16[128,1408]{1,0:T(8,128)(2,1)S(1)}, bf16[128,1408]{1,0:T(8,128)(2,1)S(1)}, u32[]{:S(2)}, u32[]{:S(2)}) collective-permute-start(bf16[128,1408]{1,0:T(8,128)(2,1)S(1)} %fusion.51), channel_id=1, source_target_pairs={{0,2},{2,0},{1,3},{3,1},{4,6},{6,4},{5,7},{7,5},{8,10},{10,8},{9,1... | collective-permute-start | bytes 1081352 | tf_op jit(solution)/shard_map/ppermute | solution.py:543
  409.7 15.3 %collective-permute-start.86 = (f32[128,1408]{1,0:T(8,128)S(1)}, f32[128,1408]{1,0:T(8,128)S(1)}, u32[]{:S(2)}, u32[]{:S(2)}) collective-permute-start(f32[128,1408]{1,0:T(8,128)S(1)} %convert_add_fusion.31), channel_id=1, source_target_pairs={{0,1},{1,0},{2,3},{3,2},{4,5},{5,4},{6,7},{7,6},{8,9},{9,8},{10,11... | collective-permute-start | bytes 2162696 | tf_op jit(solution)/shard_map/ppermute | solution.py:539
  432.2 57.7 %collective-permute-start.95 = (bf16[176,1024]{1,0:T(8,128)(2,1)}, bf16[176,1024]{1,0:T(8,128)(2,1)}, u32[]{:S(2)}, u32[]{:S(2)}) collective-permute-start(bf16[176,1024]{1,0:T(8,128)(2,1)} %fusion.37), channel_id=1, source_target_pairs={{0,2},{2,0},{1,3},{3,1},{4,6},{6,4},{5,7},{7,5},{8,10},{10,8},{9,1... | collective-permute-start | bytes 1081352 | tf_op jit(solution)/shard_map/ppermute | solution.py:543
  444.6 46.6 %collective-permute-start.60 = (bf16[128,512]{1,0:T(8,128)(2,1)}, bf16[128,512]{1,0:T(8,128)(2,1)}, u32[]{:S(2)}, u32[]{:S(2)}) collective-permute-start(bf16[128,512]{1,0:T(8,128)(2,1)} %dynamic-slice_bitcast_fusion.4), channel_id=1, source_target_pairs={{0,8},{1,5},{2,10},{3,7},{4,0},{5,13},{6,2},{7,15},{8,16},{9,1},{1... | collective-permute-start | bytes 393224 | tf_op jit(solution)/shard_map/ppermute | solution.py:573
  469.4 57.6 %collective-permute-start.51 = (bf16[128,1536]{1,0:T(8,128)(2,1)}, bf16[128,1536]{1,0:T(8,128)(2,1)}, u32[]{:S(2)}, u32[]{:S(2)}) collective-permute-start(bf16[128,1536]{1,0:T(8,128)(2,1)} %dynamic-slice_bitcast_fusion.1), channel_id=1, source_target_pairs={{0,8},{1,5},{2,10},{3,7},{4,0},{5,13},{6,2},{7,15},{8,16},{9,1},{1... | collective-permute-start | bytes 1179656 | tf_op jit(solution)/shard_map/ppermute | solution.py:573
  472.9 14.2 %collective-permute-start.41 = (f32[1024,16]{0,1:T(8,128)S(1)}, f32[1024,16]{0,1:T(8,128)S(1)}, u32[]{:S(2)}, u32[]{:S(2)}) collective-permute-start(f32[1024,16]{0,1:T(8,128)S(1)} %fusion.78), channel_id=1, source_target_pairs={{0,1},{1,0},{2,3},{3,2},{4,5},{5,4},{6,7},{7,6},{8,9},{9,8},{10,11... | collective-permute-start | bytes 196616 | tf_op jit(solution)/shard_map/ppermute | solution.py:539
  480.9 78.0 %collective-permute-start.40 = (f32[512,1024]{0,1:T(8,128)}, f32[512,1024]{0,1:T(8,128)}, u32[]{:S(2)}, u32[]{:S(2)}) collective-permute-start(f32[512,1024]{0,1:T(8,128)} %slice.230), channel_id=1, source_target_pairs={{0,1},{1,0},{2,3},{3,2},{4,5},{5,4},{6,7},{7,6},{8,9},{9,8},{10,11... | collective-permute-start | bytes 6291464 | tf_op jit(solution)/shard_map/ppermute | solution.py:539
  491.1 21.0 %collective-permute-start.32 = (bf16[128,1024]{0,1:T(8,128)(2,1)}, bf16[128,1024]{0,1:T(8,128)(2,1)S(1)}, u32[]{:S(2)}, u32[]{:S(2)}) collective-permute-start(bf16[128,1024]{0,1:T(8,128)(2,1)} %get-tuple-element.96), channel_id=1, source_target_pairs={{8,0},{24,1},{10,2},{26,3},{12,4},{28,5},{14,6},{30,7},{0,8},{16,9... | collective-permute-start | bytes 786440 | tf_op jit(solution)/shard_map/ppermute | solution.py:675
  494.4 22.5 %collective-permute-start.33 = (bf16[128,1024]{0,1:T(8,128)(2,1)}, bf16[128,1024]{0,1:T(8,128)(2,1)S(1)}, u32[]{:S(2)}, u32[]{:S(2)}) collective-permute-start(bf16[128,1024]{0,1:T(8,128)(2,1)} %get-tuple-element.95), channel_id=1, source_target_pairs={{12,0},{28,1},{14,2},{30,3},{0,4},{16,5},{2,6},{18,7},{4,8},{20,9}... | collective-permute-start | bytes 786440 | tf_op jit(solution)/shard_map/ppermute | solution.py:675
  505.4 38.7 %collective-permute-start.96 = (f32[176,1024]{1,0:T(8,128)S(1)}, f32[176,1024]{1,0:T(8,128)}, u32[]{:S(2)}, u32[]{:S(2)}) collective-permute-start(f32[176,1024]{1,0:T(8,128)S(1)} %convert_add_fusion.30), channel_id=1, source_target_pairs={{0,1},{1,0},{2,3},{3,2},{4,5},{5,4},{6,7},{7,6},{8,9},{9,8},{10,11... | collective-permute-start | bytes 2162696 | tf_op jit(solution)/shard_map/ppermute | solution.py:539
  565.9 11.5 %collective-permute-start.43 = (bf16[128,1024]{0,1:T(8,128)(2,1)S(1)}, bf16[128,1024]{0,1:T(8,128)(2,1)S(1)}, u32[]{:S(2)}, u32[]{:S(2)}) collective-permute-start(bf16[128,1024]{0,1:T(8,128)(2,1)S(1)} %get-tuple-element.89), channel_id=1, source_target_pairs={{4,0},{20,1},{6,2},{22,3},{8,4},{24,5},{10,6},{26,7},{12,8},{28,9}... | collective-permute-start | bytes 786440 | tf_op jit(solution)/shard_map/ppermute | solution.py:675
  570.6 17.7 %collective-permute-start.56 = (bf16[128,1536]{1,0:T(8,128)(2,1)S(1)}, bf16[128,1536]{1,0:T(8,128)(2,1)S(1)}, u32[]{:S(2)}, u32[]{:S(2)}) collective-permute-start(bf16[128,1536]{1,0:T(8,128)(2,1)S(1)} %fusion.32), channel_id=1, source_target_pairs={{0,8},{1,5},{2,10},{3,7},{4,0},{5,13},{6,2},{7,15},{8,16},{9,1},{1... | collective-permute-start | bytes 1179656 | tf_op jit(solution)/shard_map/ppermute | solution.py:573
  571.1 16.9 %collective-permute-start.44 = (bf16[128,1024]{0,1:T(8,128)(2,1)S(1)}, bf16[128,1024]{0,1:T(8,128)(2,1)S(1)}, u32[]{:S(2)}, u32[]{:S(2)}) collective-permute-start(bf16[128,1024]{0,1:T(8,128)(2,1)S(1)} %get-tuple-element.88), channel_id=1, source_target_pairs={{8,0},{24,1},{10,2},{26,3},{12,4},{28,5},{14,6},{30,7},{0,8},{16,9... | collective-permute-start | bytes 786440 | tf_op jit(solution)/shard_map/ppermute | solution.py:675
  575.8 12.5 %collective-permute-start.45 = (bf16[128,1024]{0,1:T(8,128)(2,1)S(1)}, bf16[128,1024]{0,1:T(8,128)(2,1)S(1)}, u32[]{:S(2)}, u32[]{:S(2)}) collective-permute-start(bf16[128,1024]{0,1:T(8,128)(2,1)S(1)} %get-tuple-element.87), channel_id=1, source_target_pairs={{12,0},{28,1},{14,2},{30,3},{0,4},{16,5},{2,6},{18,7},{4,8},{20,9}... | collective-permute-start | bytes 786440 | tf_op jit(solution)/shard_map/ppermute | solution.py:675
  575.8 27.4 %collective-permute-start.48 = (f32[214,128]{1,0:T(8,128)S(1)}, f32[214,128]{1,0:T(8,128)S(1)}, u32[]{:S(2)}, u32[]{:S(2)}) collective-permute-start(f32[214,128]{1,0:T(8,128)S(1)} %add.632), channel_id=1, source_target_pairs={{0,4},{4,0},{8,12},{12,8},{16,20},{20,16},{24,28},{28,24},{1,5},{5... | collective-permute-start | bytes 328712 | tf_op jit(solution)/shard_map/ppermute | solution.py:602
  589.4 11.6 %collective-permute-start.57 = (bf16[128,1536]{1,0:T(8,128)(2,1)S(1)}, bf16[128,1536]{1,0:T(8,128)(2,1)S(1)}, u32[]{:S(2)}, u32[]{:S(2)}) collective-permute-start(bf16[128,1536]{1,0:T(8,128)(2,1)S(1)} %fusion.31), channel_id=1, source_target_pairs={{0,8},{1,5},{2,10},{3,7},{4,0},{5,13},{6,2},{7,15},{8,16},{9,1},{1... | collective-permute-start | bytes 1179656 | tf_op jit(solution)/shard_map/ppermute | solution.py:573
  602.1 18.7 %collective-permute-start.58 = (bf16[128,1536]{1,0:T(8,128)(2,1)S(1)}, bf16[128,1536]{1,0:T(8,128)(2,1)S(1)}, u32[]{:S(2)}, u32[]{:S(2)}) collective-permute-start(bf16[128,1536]{1,0:T(8,128)(2,1)S(1)} %fusion.30), channel_id=1, source_target_pairs={{0,2},{2,0},{1,3},{3,1},{4,6},{6,4},{5,7},{7,5},{8,10},{10,8},{9,1... | collective-permute-start | bytes 1179656 | tf_op jit(solution)/shard_map/ppermute | solution.py:543
  (115 other events, 1404.8 us)

commit v3 on v2

--- a/solution.py
+++ b/solution.py
@@ -494,7 +494,8 @@
         ),
         out_shape=[jax.ShapeDtypeStruct((rows, cv), BF16), jax.ShapeDtypeStruct((rows, cv), F32),
                    jax.ShapeDtypeStruct((steps, PAIR, DV, DK), F32)],
-        compiler_params=pltpu.CompilerParams(vmem_limit_bytes=40 * 1024 * 1024),
+        compiler_params=pltpu.CompilerParams(vmem_limit_bytes=58 * 1024 * 1024),
+        cost_estimate=pl.CostEstimate(flops=1000, bytes_accessed=1000, transcendentals=0),
         name="mix_forward",
     )(order, q, k, v, logits, og, gain, sums, masks)
 
@@ -526,9 +527,180 @@
         ),
         out_shape=[jax.ShapeDtypeStruct((rows, 2 * ck + 2 * cv), BF16), jax.ShapeDtypeStruct((rows, ck), BF16),
                    jax.ShapeDtypeStruct((1, DV), F32), jax.ShapeDtypeStruct((1, ck), F32)],
-        compiler_params=pltpu.CompilerParams(vmem_limit_bytes=40 * 1024 * 1024),
+        compiler_params=pltpu.CompilerParams(vmem_limit_bytes=58 * 1024 * 1024),
+        cost_estimate=pl.CostEstimate(flops=1000, bytes_accessed=1000, transcendentals=0),
         name="mix_backward",
     )(order, q, k, v, logits, og, mixed, d_gated, states, gain, sums, masks, upper)
+
+
+FREE = pl.CostEstimate(flops=1000, bytes_accessed=1000, transcendentals=0)
+ROOMY = pltpu.CompilerParams(vmem_limit_bytes=58 * 1024 * 1024)
+
+
+def held(a):
+    return pl.BlockSpec(a.shape, lambda *g: (0,) * a.ndim, pipeline_mode=pl.Buffered(1))
+
+
+def tiles(rows, width):
+    return pl.BlockSpec((rows, width), lambda g: (g, 0))
+
+
+def attn_in_kernel(x_ref, gain_ref, w_ref, rank_ref, bias_ref, n_ref, q_ref, k_ref, v_ref, og_ref, rr_ref, lg_ref):
+    ck, cv = q_ref.shape[1], v_ref.shape[1]
+    x = x_ref[...].astype(F32)
+    r = lax.rsqrt(jnp.mean(x * x, axis=1, keepdims=True) + EPSILON)
+    n = (x * r * gain_ref[...]).astype(BF16)
+    n_ref[...] = n
+    q_ref[...] = dot_nn(n, w_ref[:, :ck]).astype(BF16)
+    k_ref[...] = dot_nn(n, w_ref[:, ck : 2 * ck]).astype(BF16)
+    v_ref[...] = dot_nn(n, w_ref[:, 2 * ck : 2 * ck + cv]).astype(BF16)
+    og_ref[...] = dot_nn(n, w_ref[:, 2 * ck + cv : 2 * ck + 2 * cv])
+    rank = dot_nn(n, w_ref[:, 2 * ck + 3 * cv :]).astype(BF16)
+    rr_ref[...] = rank
+    lg_ref[...] = dot_nt(rank, rank_ref[...]) + bias_ref[...]
+
+
+def attn_in(x, gain, w, rank, bias):
+    rows, ck, cv, step = x.shape[0], PAIR * DK, PAIR * DV, 256
+    shapes = [(x.shape[1], BF16), (ck, BF16), (ck, BF16), (cv, BF16), (cv, F32), (128, BF16), (ck, F32)]
+    return pl.pallas_call(
+        attn_in_kernel,
+        grid=(rows // step,),
+        in_specs=[tiles(step, x.shape[1]), held(gain), held(w), held(rank), held(bias)],
+        out_specs=[tiles(step, c) for c, _ in shapes],
+        out_shape=[jax.ShapeDtypeStruct((rows, c), t) for c, t in shapes],
+        compiler_params=ROOMY,
+        cost_estimate=FREE,
+        name="attn_in",
+    )(x, gain, w, rank, bias)
+
+
+def attn_out_kernel(x_ref, g_ref, w_ref, gain_ref, res_ref, n_ref, r_ref):
+    res = x_ref[...].astype(F32) + dot_nn(g_ref[...], w_ref[...])
+    r = lax.rsqrt(jnp.mean(res * res, axis=1, keepdims=True) + EPSILON)
+    res_ref[...] = res
+    n_ref[...] = (res * r * gain_ref[...]).astype(BF16)
+    r_ref[...] = r
+
+
+def attn_out(x, gated, w, gain):
+    rows, width = x.shape
+    step = 256
+    return pl.pallas_call(
+        attn_out_kernel,
+        grid=(rows // step,),
+        in_specs=[tiles(step, width), tiles(step, gated.shape[1]), held(w), held(gain)],
+        out_specs=[tiles(step, width), tiles(step, width), tiles(step, 1)],
+        out_shape=[jax.ShapeDtypeStruct((rows, width), F32), jax.ShapeDtypeStruct((rows, width), BF16),
+                   jax.ShapeDtypeStruct((rows, 1), F32)],
+        compiler_params=ROOMY,
+        cost_estimate=FREE,
+        name="attn_out",
+    )(x, gated, w, gain)
+
+
+def ffn_kernel(plane, n_ref, dy_ref, near_ref, far_ref, down_ref, hid_ref, near_d_ref, far_d_ref, block_ref, dn_ref):
+    straight = plane[0] == 0
+    n = n_ref[...]
+    near = dot_nn(n, near_ref[...])
+    far = dot_nn(n, far_ref[...])
+    gate, up = jnp.where(straight, near, far), jnp.where(straight, far, near)
+    sig = sigmoid(gate)
+    act = gate * sig
+    hidden = (act * up).astype(BF16)
+    hid_ref[...] = hidden
+    d_hidden = dot_nt(dy_ref[...], down_ref[...])
+    d_gate = d_hidden * up * (sig + act * (1.0 - sig))
+    d_up = d_hidden * act
+    d_near = jnp.where(straight, d_gate, d_up).astype(BF16)
+    d_far = jnp.where(straight, d_up, d_gate).astype(BF16)
+    near_d_ref[...] = d_near
+    far_d_ref[...] = d_far
+    block_ref[...] = dot_nn(hidden, down_ref[...])
+    dn_ref[...] = dot_nt(d_near, near_ref[...]) + dot_nt(d_far, far_ref[...])
+
+
+def ffn(plane, n, dy, near, far, down):
+    rows, width = n.shape
+    ff, step = near.shape[1], 256
+
+    def row(width):
+        return pl.BlockSpec((step, width), lambda g, p: (g, 0))
+
+    return pl.pallas_call(
+        ffn_kernel,
+        grid_spec=pltpu.PrefetchScalarGridSpec(
+            num_scalar_prefetch=1,
+            grid=(rows // step,),
+            in_specs=[row(width), row(width), held(near), held(far), held(down)],
+            out_specs=[row(ff), row(ff), row(ff), row(width), row(width)],
+        ),
+        out_shape=[jax.ShapeDtypeStruct((rows, ff), BF16)] * 3
+        + [jax.ShapeDtypeStruct((rows, width), F32)] * 2,
+        compiler_params=ROOMY,
+        cost_estimate=FREE,
+        name="ffn",
+    )(plane, n, dy, near, far, down)
+
+
+def branch_kernel(dn_ref, sw_ref, dy_ref, res_ref, r_ref, gain_ref, w_ref, d_ref, low_ref, dg_ref, fg_ref):
+    step = pl.program_id(0)
+
+    @pl.when(step == 0)
+    def _():
+        fg_ref[...] = jnp.zeros_like(fg_ref)
+
+    dn = dn_ref[...] + sw_ref[...]
+    res, r = res_ref[...], r_ref[...]
+    n = res * r
+
+    @pl.when(step < pl.num_programs(0) // 2)
+    def _():
+        fg_ref[...] += jnp.sum(dn * n, axis=0, keepdims=True)
+
+    u = gain_ref[...] * dn
+    d = dy_ref[...].astype(F32) + r * (u - n * jnp.mean(u * n, axis=1, keepdims=True))
+    low = d.astype(BF16)
+    d_ref[...] = d
+    low_ref[...] = low
+    dg_ref[...] = dot_nt(low, w_ref[...])
+
+
+def branch(dn, swapped, dy, res, r, gain, w):
+    rows, width = dn.shape
+    step = 256
+    count = rows // step
+    other = pl.BlockSpec((step, width), lambda g: ((g + count // 2) % count, 0))
+    full = tiles(step, width)
+    return pl.pallas_call(
+        branch_kernel,
+        grid=(count,),
+        in_specs=[full, other, full, full, tiles(step, 1), held(gain), held(w)],
+        out_specs=[full, full, tiles(step, w.shape[0]), pl.BlockSpec((1, width), lambda g: (0, 0))],
+        out_shape=[jax.ShapeDtypeStruct((rows, width), F32), jax.ShapeDtypeStruct((rows, width), BF16),
+                   jax.ShapeDtypeStruct((rows, w.shape[0]), F32), jax.ShapeDtypeStruct((1, width), F32)],
+        compiler_params=ROOMY,
+        cost_estimate=FREE,
+        name="branch",
+    )(dn, swapped, dy, res, r, gain, w)
+
+
+def outer_kernel(n_ref, d_ref, g_ref):
+    g_ref[...] = dot_tn(n_ref[...], d_ref[...]).astype(BF16)
+
+
+def outer(n, d, step=256):
+    rows, width = n.shape
+    return pl.pallas_call(
+        outer_kernel,
+        grid=(width // step,),
+        in_specs=[pl.BlockSpec((rows, step), lambda i: (0, i)), held(d)],
+        out_specs=tiles(step, d.shape[1]),
+        out_shape=jax.ShapeDtypeStruct((width, d.shape[1]), BF16),
+        compiler_params=ROOMY,
+        cost_estimate=FREE,
+        name="outer",
+    )(n, d)
 
 
 def device_of(shard, x, core, xs):
@@ -572,36 +744,66 @@
     def send(self, a):
         return lax.ppermute(a, AXES, self.pairs)
 
-    def gather(self, piece):
+    def gather(self, piece, early=None):
         whole = jnp.zeros((self.shards,) + piece.shape, piece.dtype)
         pieces = [piece]
-        for _ in range(self.shards - 1):
+        for hops in range(self.shards - 1):
+            if hops == 1 and early is not None:
+                pieces[-1], early = lax.optimization_barrier((pieces[-1], early))
             pieces.append(self.send(pieces[-1]))
         for hops, a in enumerate(pieces):
             whole = lax.dynamic_update_index_in_dim(whole, a, self.behind(hops), 0)
-        return whole, pieces
-
-    def scatter(self, blocks):
-        def own(hops):
-            return lax.dynamic_index_in_dim(blocks, self.behind(hops), 0, False)
-
-        moving = own(1)
-        for hops in range(2, self.shards + 1):
-            arrived = self.send(moving)
-            moving = (arrived.astype(F32) + own(hops).astype(F32)).astype(BF16)
-        return moving
-
-
-def tree_sum(a):
+        return whole, pieces, early
+
+    def own(self, blocks, hops):
+        return lax.dynamic_index_in_dim(blocks, self.behind(hops), 0, False)
+
+
+class Gather:
+    def __init__(self, ring, piece):
+        self.ring, self.hops, self.last = ring, 0, piece
+        self.whole = jnp.zeros((ring.shards,) + piece.shape, piece.dtype)
+        self.keep(piece)
+
+    def keep(self, piece):
+        self.whole = lax.dynamic_update_index_in_dim(
+            self.whole, piece, self.ring.behind(self.hops), 0
+        )
+
+    def take(self, arrived, *deps):
+        self.hops += 1
+        self.last = after(arrived, *deps)
+        self.keep(self.last)
+
+
+class Scatter:
+    def __init__(self, ring, blocks):
+        self.ring, self.blocks, self.hops = ring, blocks, 1
+        self.moving = ring.own(blocks, 1)
+
+    def hop(self, *deps):
+        self.hops += 1
+        arrived = self.ring.send(self.moving)
+        mine = after(self.ring.own(self.blocks, self.hops), *deps)
+        self.moving = (arrived.astype(F32) + mine.astype(F32)).astype(BF16)
+        return self.moving
+
+
+def after(a, *deps):
+    return lax.optimization_barrier((a,) + deps)[0] if deps else a
+
+
+def tree_steps():
     shards = lax.axis_size("shard")
-    a = a + core_swap(a)
+    steps = [core_swap]
     if lax.axis_size("x") == 2:
-        a = a + x_swap(a)
+        steps.append(x_swap)
     step = 1
     while step < shards:
-        a = a + lax.ppermute(a, "shard", [(s, s ^ step) for s in range(shards)])
+        pairs = [(s, s ^ step) for s in range(shards)]
+        steps.append(lambda a, pairs=pairs: lax.ppermute(a, "shard", pairs))
         step *= 2
-    return a
+    return steps
 
 
 def by_core(mine, other, axis):
@@ -703,45 +905,49 @@
     wide = 2 * ck + 2 * cv
     own = rows_in(tokens)
     ring = Ring()
-    attn_full, attn_pieces = ring.gather(packed)
+    attn_full, attn_pieces, own = ring.gather(packed, own)
     attn_full = attn_full.reshape(width, -1)
-    cols_piece = jnp.concatenate([core_half(w_gate, 1), core_half(w_up, 1)], 1)
-    cols_piece, down_piece, grad_in, _ = lax.optimization_barrier(
-        (cols_piece, core_half(w_down, 0), out_grad, attn_pieces[-2])
-    )
-    ffn_cols, _ = ring.gather(cols_piece)
-    ffn_cols = ffn_cols.reshape(width, -1)
-    down_rows, _ = ring.gather(down_piece)
-    own_grad = rows_in(grad_in)
-
+    plane = lax.axis_index("x") == 0
+    gate_piece, up_piece = core_half(w_gate, 1), core_half(w_up, 1)
+    near_ring = Gather(ring, after(jnp.where(plane, gate_piece, up_piece), attn_pieces[6]))
+    far_ring = Gather(ring, jnp.where(plane, up_piece, gate_piece))
+    down_ring = Gather(ring, after(core_half(w_down, 0), attn_pieces[6]))
+    own_grad = rows_in(after(out_grad, attn_pieces[7]))
+
+    def ffn_hop(*deps):
+        down_ring.take(ring.send(down_ring.last), *deps)
+        near_ring.take(ring.send(near_ring.last), *deps)
+        far_ring.take(x_swap(near_ring.last))
+
+    ffn_hop()
     x_low = jnp.concatenate([own, core_swap(own)], 0)
-    inputs = x_low.astype(F32)
-    r_in = lax.rsqrt(jnp.mean(inputs * inputs, axis=1, keepdims=True) + EPSILON)
     attn_row = attn_gain.astype(F32)
-    normed = (inputs * r_in * attn_row).astype(BF16)
-
-    w_qkvo = attn_full[:, :wide]
-    rank_in = attn_full[:, wide + cv : wide + cv + 16]
     rank_out = attn_full[:, wide + cv + 16 : wide + cv + 32]
     rank_out = rank_out.reshape(shards, -1, 16)[:, : w_rank_out.shape[0]].reshape(-1, 16)
-    rank_out = core_half(rank_out, 0)
-    queries = product(normed, w_qkvo[:, :ck]).astype(BF16)
-    keys = product(normed, w_qkvo[:, ck : 2 * ck]).astype(BF16)
-    values = product(normed, w_qkvo[:, 2 * ck : 2 * ck + cv]).astype(BF16)
-    out_gate = product(normed, w_qkvo[:, 2 * ck + cv :])
-    rank_rows = product(normed, rank_in).astype(BF16)
-    logits = times_transpose(rank_rows, rank_out) + core_half(fgate_bias, 0).astype(F32)
+    rank_out = jnp.pad(core_half(rank_out, 0), ((0, 0), (0, 112)))
+    bias = core_half(fgate_bias, 0).astype(F32)[None]
+    normed, queries, keys, values, out_gate, rank_rows, logits = attn_in(
+        x_low, attn_row[None], attn_full, rank_out, bias
+    )
     gain = head_gain.astype(F32)[None]
+    ffn_hop(queries)
+    queries = after(queries, near_ring.last)
     gated, mixed, states = mix_forward(
         order, queries, keys, values, logits, out_gate, gain, sums, masks
     )
+    ffn_hop(gated)
+    gated = after(gated, near_ring.last)
     gated_full = by_core(gated, swap_rows(core_swap(gated)), 1)
     out_mine = attn_full[:, wide : wide + cv]
     w_out_full = by_core(out_mine, core_swap(out_mine), 1)
-    residual = inputs + product(gated_full, w_out_full)
-    r_ffn = lax.rsqrt(jnp.mean(residual * residual, axis=1, keepdims=True) + EPSILON)
     ffn_row = ffn_gain.astype(F32)
-    ffn_in = (residual * r_ffn * ffn_row).astype(BF16)
+    residual, ffn_in, r_ffn = attn_out(x_low, gated_full, w_out_full, ffn_row[None])
+    ffn_hop(ffn_in)
+    for _ in range(4, shards - 1):
+        ffn_hop()
+    cols_near = near_ring.whole.reshape(width, -1)
+    cols_far = far_ring.whole.reshape(width, -1)
+    down_rows = down_ring.whole
 
     ff_half = w_gate.shape[1] // 2
     group = shards // 2
@@ -749,67 +955,74 @@
     send_down = lax.dynamic_slice_in_dim(down_rows, (1 - core) * group, group, 0)
     other_down = core_swap(send_down)
     w_down_half = by_core(mine_down, other_down, 1).reshape(ff_half, width)
-    w_gate_half, w_up_half = ffn_cols[:, :ff_half], ffn_cols[:, ff_half:]
 
     dy = jnp.concatenate([own_grad, core_swap(own_grad)], 0)
-    gate = product(ffn_in, w_gate_half)
-    up = product(ffn_in, w_up_half)
-    sig = sigmoid(gate)
-    act = gate * sig
-    hidden = (act * up).astype(BF16)
-    d_hidden = times_transpose(dy, w_down_half)
-    d_gate = (d_hidden * up * (sig * (1.0 + gate * (1.0 - sig)))).astype(BF16)
-    d_up = (d_hidden * act).astype(BF16)
+    turn = lax.axis_index("x")[None].astype(jnp.int32)
+    hidden, d_near, d_far, block_part, dn_part = ffn(
+        turn, ffn_in, dy, cols_near, cols_far, w_down_half
+    )
     half_rows = x_low.shape[0] // 2
-    block_part = product(hidden, w_down_half)
+    dn_swapped = core_swap(dn_part)
+    block_swapped = core_swap(block_part[half_rows:])
+    far_part = outer(ffn_in, d_far)
+    grad_far = x_swap(far_part)
+    grad_near = outer(after(ffn_in, far_part), d_near)
+    hidden = after(hidden, grad_near)
+    down_grad = outer(hidden, dy, 128).reshape(group, 2, -1, width)
+    mine_dg = lax.dynamic_index_in_dim(down_grad, core, 1, False)
+    other_dg = core_swap(lax.dynamic_index_in_dim(down_grad, 1 - core, 1, False))
+    down = Scatter(ring, by_core(mine_dg, other_dg, 0))
+
+    d_residual, d_branch, d_gated, ffn_gain_grad = branch(
+        dn_part, after(dn_swapped, down.moving), dy, residual, r_ffn, ffn_row[None],
+        core_half(w_out_full, 0)
+    )
+    ffn_gain_grad = ffn_gain_grad[0]
+    down.hop(d_gated)
     block_own = (
-        residual[:half_rows] + block_part[:half_rows] + core_swap(block_part[half_rows:])
+        residual[:half_rows] + block_part[:half_rows] + after(block_swapped, d_gated)
     ).astype(BF16)
     block_out = rows_out(block_own)
-
-    down_grad = outer_sum(hidden, dy).astype(BF16).reshape(group, 2, -1, width)
-    mine_dg = lax.dynamic_index_in_dim(down_grad, core, 1, False)
-    other_dg = core_swap(lax.dynamic_index_in_dim(down_grad, 1 - core, 1, False))
-    down_grad = by_core(mine_dg, other_dg, 0)
-    down_own = ring.scatter(down_grad)
-    gate_own = ring.scatter(outer_sum(ffn_in, d_gate).astype(BF16).reshape(shards, -1, ff_half))
-    up_own = ring.scatter(outer_sum(ffn_in, d_up).astype(BF16).reshape(shards, -1, ff_half))
-
-    dn_part = times_transpose(d_gate, w_gate_half) + times_transpose(d_up, w_up_half)
-    dn_ffn = dn_part + swap_rows(core_swap(dn_part))
-    u = ffn_row * dn_ffn
-    d_residual = dy.astype(F32) + r_ffn * (
-        u - residual * (r_ffn * r_ffn) * jnp.mean(u * residual, axis=1, keepdims=True)
-    )
-    ffn_gain_grad = jnp.sum((dn_ffn * residual * r_ffn)[:half_rows], axis=0)
-    d_branch = d_residual.astype(BF16)
+    d_all, d_logits, hgain_part, bias_part = mix_backward(
+        order, queries, keys, values, logits, out_gate, mixed, after(d_gated, down.moving),
+        states, gain, sums, masks, upper
+    )
+    down.hop(d_all)
+    d_all = after(d_all, down.moving)
     out_w_grad = outer_sum(gated_full, core_half(d_branch, 1))
-    d_gated = times_transpose(d_branch, core_half(w_out_full, 0))
-    d_all, d_logits, hgain_part, bias_part = mix_backward(
-        order, queries, keys, values, logits, out_gate, mixed, d_gated, states, gain,
-        sums, masks, upper
-    )
-    rank_out_grad = outer_sum(rank_rows, d_logits)
-    rank_part = product(d_logits, rank_out)
-    d_rank = (rank_part + swap_rows(core_swap(rank_part))).astype(BF16)
+    qkvo_grad = outer_sum(normed, d_all)
+    near_total = after(grad_near, d_all).astype(F32) + grad_far.astype(F32)
+    last_grad = jnp.concatenate(
+        [qkvo_grad.astype(BF16), out_w_grad.astype(BF16), near_total.astype(BF16)], 1
+    )
+    attn = Scatter(ring, last_grad.reshape(shards, -1, wide + cv + ff_half))
+    down.hop(attn.moving)
+    rank_out_grad = outer_sum(rank_rows[:, :16], d_logits)
+    rank_part = product(d_logits, rank_out[:, :16])
+    rank_swapped = core_swap(rank_part)
+    dn_attn = times_transpose(after(d_all, down.moving), attn_full[:, :wide])
+    dn_attn_swapped = core_swap(dn_attn[half_rows:])
+    attn.hop(dn_attn)
+    down.hop(dn_attn, attn.moving)
+    dn_attn_swapped = after(dn_attn_swapped, down.moving)
+    d_rank = (rank_part + swap_rows(rank_swapped)).astype(BF16)
     rank_in_grad = outer_sum(d_rank[:half_rows], normed[:half_rows])
-    qkvo_grad = outer_sum(normed, d_all)
-    attn_own = ring.scatter(qkvo_grad.astype(BF16).reshape(shards, -1, wide))
-    wout_own = ring.scatter(out_w_grad.astype(BF16).reshape(shards, -1, cv))
-    dn_attn = times_transpose(d_all, w_qkvo)
     dn_own = (
         dn_attn[:half_rows]
-        + core_swap(dn_attn[half_rows:])
-        + times_transpose(d_rank[:half_rows], rank_in)
-    )
-    own_in, own_r = inputs[:half_rows], r_in[:half_rows]
+        + dn_attn_swapped
+        + times_transpose(d_rank[:half_rows], attn_full[:, wide + cv : wide + cv + 16])
+    )
+    own_in = x_low[:half_rows].astype(F32)
+    own_r = lax.rsqrt(jnp.mean(own_in * own_in, axis=1, keepdims=True) + EPSILON)
     u = attn_row * dn_own
     tok_grad = (
         d_residual[:half_rows]
         + own_r * (u - own_in * (own_r * own_r) * jnp.mean(u * own_in, axis=1, keepdims=True))
     ).astype(BF16)
-    tokens_grad = rows_out(tok_grad)
     attn_gain_grad = jnp.sum(dn_own * own_in * own_r, axis=0)
+    attn.hop(tok_grad)
+    down.hop(tok_grad, attn.moving)
+    tokens_grad = rows_out(after(tok_grad, down.moving))
 
     first = (core == 0).astype(F32)
 
@@ -826,7 +1039,25 @@
         attn_gain_grad[None], spread(bias_part), hgain_part, ffn_gain_grad[None],
         rank_in_grad, rank_out_both,
     )
-    small = tree_sum(jnp.concatenate([flat(a) for a in parts], 0))
+    small = jnp.concatenate([flat(a) for a in parts], 0)
+    steps = tree_steps()
+    for count in range(3, shards):
+        if count < 3 + len(steps):
+            small = small + steps[count - 3](small)
+        attn.hop(small)
+        if down.hops < shards:
+            down.hop(attn.moving)
+            small = after(small, down.moving)
+        else:
+            small = after(small, attn.moving)
+    for step in steps[shards - 3 :]:
+        small = small + step(small)
+    last_own, down_own = attn.moving, down.moving
+    last_far = x_swap(last_own)
+    split_at = wide + cv
+    near_own, far_own = last_own[:, split_at:], last_far[:, split_at:]
+    gate_own = jnp.where(plane, near_own, far_own)
+    up_own = jnp.where(plane, far_own, near_own)
     pieces, at = [], 0
     for a in parts:
         size = a.size // lanes
@@ -842,7 +1073,8 @@
             total = total + x_swap(moving).astype(F32)
         return total, core_swap(total)
 
-    attn_mine, attn_other = settle(attn_own)
+    attn_mine = last_own[:, :split_at].astype(F32) + last_far[:, :split_at].astype(F32)
+    attn_other = core_swap(attn_mine)
 
     def columns(mine, other, start, size):
         return by_core(mine[:, start : start + size], other[:, start : start + size], 1)
@@ -859,10 +1091,10 @@
         rank_out_own,
         pieces[1][0],
         pieces[2][0],
-        by_core(*settle(wout_own), 1),
+        columns(attn_mine, attn_other, wide, cv),
         pieces[3][0],
-        by_core(*settle(gate_own), 1),
-        by_core(*settle(up_own), 1),
+        by_core(gate_own, core_swap(gate_own), 1).astype(F32),
+        by_core(up_own, core_swap(up_own), 1).astype(F32),
         by_core(*settle(down_own), 0),
     )
 

time: 636 us -> 560 us (0.88)
  Pallas kernels: 33.1 us -> 118 us
  waiting for transfers between devices: 210 us -> 131 us
  matrix products: 93.3 us -> 18.5 us
  starting transfers between devices: 137 us -> 128 us
  local copies, waits for them, and re-layouts: 75.3 us -> 82.9 us
  other arithmetic: 50.8 us -> 43.4 us
    ppermute x56 -> x35, waiting for transfers between devices: 186 us -> 82.2 us  [send(): return lax.ppermute(a, AXES, self.pairs)]
    pallas_call x0 -> x7, Pallas kernels: none -> 78.9 us  [the longest x1 26.4 us: ffn(): pl.pallas_call(ffn_kernel, grid_spec=pltpu.PrefetchScalarGridSpec(num_sca...]
    dot_general x10 -> x1, matrix products: 38 us -> 1.26 us  [product(): return jnp.dot(left_side, right_side, preferred_element_type=jnp.float32)]
    ppermute x6 -> x11, waiting for transfers between devices: 2.84 us -> 34.2 us  [x_swap(): return lax.ppermute(a, 'x', [(0, 1), (1, 0)])]
    dot_general x7 -> x2, matrix products: 30.1 us -> 7.35 us  [times_transpose(): lax.dot_general(left_side, right_side, (((1,), (1,)), ((), ())), preferre...]
    dynamic_update_slice x0 -> x23, local copies, waits for them, and re-layouts: none -> 22.7 us  [keep(): lax.dynamic_update_index_in_dim(self.whole, piece, self.ring.behind(self....]
    dot_general x7 -> x4, matrix products: 25.2 us -> 9.89 us  [outer_sum(): lax.dot_general(left_side, right_side, (((0,), (0,)), ((), ())), preferre...]
    ppermute x8, waiting for transfers between devices: 10.9 us -> 0.02 us  [rows_out(): lax.ppermute(a[step * tok_dev:(step + 1) * tok_dev], AXES, [(t, s) for s,...]
  transfers between devices with their start and end apart: 97 -> 80, of which waited for: 45 -> 28; matrix products, arithmetic and copies ran while one was open for 25% -> 23% of each run, Pallas kernels for 5% -> 17%
where the time goes in v3:
time: 560 us; the launch traced here: 549 us
  waiting for transfers between devices  131 us (23%)
  starting transfers between devices  128 us (23%)
  Pallas kernels  118 us (21%)
  local copies, waits for them, and re-layouts  82.9 us (15%)
  other arithmetic  43.4 us (8%)
  between operations  27 us (5%)
  matrix products  18.5 us (3%)
    ppermute x35, waiting for transfers between devices, send(): return lax.ppermute(a, AXES, self.pairs)  82.2 us
    ppermute x35, starting transfers between devices, send(): return lax.ppermute(a, AXES, self.pairs)  67.8 us
    ppermute x11, waiting for transfers between devices, x_swap(): return lax.ppermute(a, 'x', [(0, 1), (1, 0)])  34.2 us
    pallas_call x1, Pallas kernels, ffn(): pl.pallas_call(ffn_kernel, grid_spec=pltpu.PrefetchScalarGridSpec(num_sca...  26.4 us
    pallas_call x3, Pallas kernels, outer(): pl.pallas_call(outer_kernel, grid=(width // step,), in_specs=[pl.BlockSpe...  25.1 us
    dynamic_update_slice x23, local copies, waits for them, and re-layouts, keep(): lax.dynamic_update_index_in_dim(self.whole, piece, self.ring.behind(self....  22.7 us
    pallas_call x1, Pallas kernels, mix_forward(): pl.pallas_call(mix_forward_kernel, grid_spec=pltpu.PrefetchScalarGridSpec...  20.5 us
    pallas_call x1, Pallas kernels, mix_backward(): pl.pallas_call(mix_backward_kernel, grid_spec=pltpu.PrefetchScalarGridSpe...  18.1 us
  transfers between devices with their start and end apart: 80, of which 28 were waited for; matrix products, arithmetic and copies ran while one was open for 23% of the time, Pallas kernels for 17%

profile of v3, /device:TPU:0, one launch (start us, length us, event | category | flops | bytes accessed | tf_op | source)
XLA Modules:
  0.0 549.2 jit_solution(18201348193855550149)
XLA Ops:
  5.6 3.1 collective-permute-start
  11.3 2.9 collective-permute-start.4
  26.3 2.7 broadcast_in_dim.135
  51.5 3.6 collective-permute-start.5
  57.1 3.7 collective-permute-done.6
  63.7 6.6 %collective-permute-done.7 = bf16[128,2176]{1,0:T(8,128)(2,1)S(1)} collective-permute-done((bf16[128,2176]{1,0:T(8,128)(2,1)S(1)}, bf16[128,2176]{1,0:T(8,128)(2,1)S(1)}, u32[]{:S(2)}, u32[]{:S(2)}) %collective-permute-start.7) | collective-permute-done | bytes 557088 | tf_op jit(solution)/shard_map/ppermute | solution.py:745
  70.3 2.7 collective-permute-start.8
  73.9 6.2 %collective-permute-done.8 = bf16[128,2176]{1,0:T(8,128)(2,1)S(1)} collective-permute-done((bf16[128,2176]{1,0:T(8,128)(2,1)S(1)}, bf16[128,2176]{1,0:T(8,128)(2,1)S(1)}, u32[]{:S(2)}, u32[]{:S(2)}) %collective-permute-start.8) | collective-permute-done | bytes 557088 | tf_op jit(solution)/shard_map/ppermute | solution.py:745
  83.4 6.2 %collective-permute-done.9 = bf16[128,2176]{1,0:T(8,128)(2,1)S(1)} collective-permute-done((bf16[128,2176]{1,0:T(8,128)(2,1)S(1)}, bf16[128,2176]{1,0:T(8,128)(2,1)S(1)}, u32[]{:S(2)}, u32[]{:S(2)}) %collective-permute-start.9) | collective-permute-done | bytes 557088 | tf_op jit(solution)/shard_map/ppermute | solution.py:745
  89.6 2.5 collective-permute-start.10
  92.9 6.2 %collective-permute-done.10 = bf16[128,2176]{1,0:T(8,128)(2,1)S(1)} collective-permute-done((bf16[128,2176]{1,0:T(8,128)(2,1)S(1)}, bf16[128,2176]{1,0:T(8,128)(2,1)S(1)}, u32[]{:S(2)}, u32[]{:S(2)}) %collective-permute-start.10) | collective-permute-done | bytes 557088 | tf_op jit(solution)/shard_map/ppermute | solution.py:745
  121.1 3.2 collective-permute-start.20
  125.0 9.0 %attn_in.1 = (bf16[1024,1024]{1,0:T(8,128)(2,1)}, bf16[1024,256]{1,0:T(8,128)(2,1)}, bf16[1024,256]{1,0:T(8,128)(2,1)}, bf16[1024,512]{1,0:T(8,128)(2,1)}, f32[1...) custom-call(bf16[1024,1024]{1,0:T(8,128)(2,1)} %copy-done.3, f32[1,1024]{1,0:T(1,128)} %bitcast.194, ...), custom_call_target="tpu_custom_call" | custom-call | flops 1000 | bytes 1000 | tf_op jit(solution)/shard_map/attn_in/pallas_call | solution.py:566
  139.0 20.5 %mix_forward.1 = (bf16[1024,512]{1,0:T(8,128)(2,1)}, f32[1024,512]{1,0:T(8,128)}, f32[8,2,256,128]{3,2,1,0:T(8,128)}) custom-call(s32[8]{0:T(128)} %fusion.39.order, bf16[1024,256]{1,0:T(8,128)(2,1)} %get-tuple-element.89.q_ref, bf16[1024,256]{1,0:T(8,128)(2,1)} %get-tuple-element.90.k_ref, bf16[1024,512]{1,0:T(8,128)(2,1)} %get-tuple-element.91.v_ref, ...), custom_call_target="tpu_custom_call" | custom-call | flops 1000 | bytes 1000 | tf_op jit(solution)/shard_map/mix_forward/pallas_call | solution.py:484
  159.5 6.3 %collective-permute-start.16 = (bf16[1024,512]{1,0:T(8,128)(2,1)S(1)}, bf16[1024,512]{1,0:T(8,128)(2,1)S(1)}, u32[]{:S(2)}, u32[]{:S(2)}) collective-permute-start(bf16[1024,512]{1,0:T(8,128)(2,1)S(1)} %slice.190), channel_id=1, source_target_pairs={{0,1},{1,0},{2,3},{3,2},{4,5},{5,4},{6,7},{7,6},{8,9},{9,8},{10,11... | collective-permute-start | bytes 3145736 | tf_op jit(solution)/shard_map/ppermute | solution.py:711
  171.4 4.1 collective-permute-done.14
  176.1 3.2 collective-permute-done.35
  193.0 7.4 %attn_out.1 = (f32[1024,1024]{1,0:T(8,128)}, bf16[1024,1024]{1,0:T(8,128)(2,1)}, f32[1024,1]{1,0:T(8,128)}) custom-call(bf16[1024,1024]{1,0:T(8,128)(2,1)} %copy-done.3, bf16[1024,1024]{1,0:T(8,128)(2,1)} %pad_maximum_fusion.3.g_ref, bf16[1024,1024]{1,0:T(8,128)(2,1)} %pad_maximum_fusion.2.w_ref, f32[1,1024]{1,0:T(1,128)} %bitcast.195), custom_call_target="tpu_custom_call" | custom-call | flops 1000 | bytes 1000 | tf_op jit(solution)/shard_map/attn_out/pallas_call | solution.py:589
  223.9 5.4 collective-permute-done.39
  235.5 7.8 %collective-permute-done.32 = bf16[128,1408]{1,0:T(8,128)(2,1)S(1)} collective-permute-done((bf16[128,1408]{1,0:T(8,128)(2,1)S(1)}, bf16[128,1408]{1,0:T(8,128)(2,1)S(1)}, u32[]{:S(2)}, u32[]{:S(2)}) %collective-permute-start.32) | collective-permute-done | bytes 360480 | tf_op jit(solution)/shard_map/ppermute | solution.py:715
  247.7 26.4 %ffn.1 = (bf16[1024,1408]{1,0:T(8,128)(2,1)}, bf16[1024,1408]{1,0:T(8,128)(2,1)}, bf16[1024,1408]{1,0:T(8,128)(2,1)}, f32[1024,1024]{1,0:T(8,128)}, f32[1024,1024]{1,0:T(8,128)}) custom-call(s32[1]{0:T(128)} %bitcast.28.plane, bf16[1024,1024]{1,0:T(8,128)(2,1)} %get-tuple-element.109.n_ref, bf16[1024,1024]{1,0:T(8,128)(2,1)} %copy-done.2, ...), custom_call_target="tpu_custom_call" | custom-call | flops 1000 | bytes 1000 | tf_op jit(solution)/shard_map/ffn/pallas_call | solution.py:630
  274.1 7.3 %outer.3 = bf16[1024,1408]{1,0:T(8,128)(2,1)} custom-call(bf16[1024,1024]{1,0:T(8,128)(2,1)} %get-tuple-element.109.n_ref, bf16[1024,1408]{1,0:T(8,128)(2,1)} %get-tuple-element.108.d_ref), custom_call_target="tpu_custom_call" | custom-call | flops 1000 | bytes 1000 | tf_op jit(solution)/shard_map/outer/pallas_call | solution.py:694
  281.4 7.3 %outer.4 = bf16[1024,1408]{1,0:T(8,128)(2,1)} custom-call(bf16[1024,1024]{1,0:T(8,128)(2,1)} %get-tuple-element.109.n_ref, bf16[1024,1408]{1,0:T(8,128)(2,1)} %get-tuple-element.110.d_ref), custom_call_target="tpu_custom_call" | custom-call | flops 1000 | bytes 1000 | tf_op jit(solution)/shard_map/outer/pallas_call | solution.py:694
  288.7 10.6 %outer.5 = bf16[1408,1024]{1,0:T(8,128)(2,1)} custom-call(bf16[1024,1408]{1,0:T(8,128)(2,1)} %get-tuple-element.111.n_ref, bf16[1024,1024]{1,0:T(8,128)(2,1)} %copy-done.2), custom_call_target="tpu_custom_call" | custom-call | flops 1000 | bytes 1000 | tf_op jit(solution)/shard_map/outer/pallas_call | solution.py:694
  299.2 2.6 dynamic-slice_bitcast_fusion
  302.3 3.1 slice.147
  316.0 11.0 %branch.1 = (f32[1024,1024]{1,0:T(8,128)}, bf16[1024,1024]{1,0:T(8,128)(2,1)}, f32[1024,512]{1,0:T(8,128)}, f32[1,1024]{1,0:T(1,128)}) custom-call(f32[1024,1024]{1,0:T(8,128)} %get-tuple-element.106.dn_ref, f32[1024,1024]{1,0:T(8,128)} %collective-permute-done.42.sw_ref, bf16[1024,1024]{1,0:T(8,128)(2,1)} %copy-done.2, ...), custom_call_target="tpu_custom_call" | custom-call | flops 1000 | bytes 1000 | tf_op jit(solution)/shard_map/branch/pallas_call | solution.py:675
  329.7 18.1 %mix_backward.1 = (bf16[1024,1536]{1,0:T(8,128)(2,1)}, bf16[1024,256]{1,0:T(8,128)(2,1)}, f32[1,256]{1,0:T(1,128)}, f32[1,256]{1,0:T(1,128)}) custom-call(s32[8]{0:T(128)} %fusion.39.order, bf16[1024,256]{1,0:T(8,128)(2,1)} %get-tuple-element.89.q_ref, bf16[1024,256]{1,0:T(8,128)(2,1)} %get-tuple-element.90.k_ref, ...), custom_call_target="tpu_custom_call" | custom-call | flops 1000 | bytes 1000 | tf_op jit(solution)/shard_map/mix_backward/pallas_call | solution.py:514
  351.1 3.6 add_convert_fusion.1
  364.5 6.1 %convolution_convert_fusion = bf16[1024,1536]{1,0:T(8,128)(2,1)S(1)} fusion(bf16[1024,1024]{1,0:T(8,128)(2,1)} %get-tuple-element.124, bf16[1024,1536]{1,0:T(8,128)(2,1)} %get-tuple-element.128), kind=kOutput, calls=%fused_computation.18 | convolution fusion | flops 3222798336 | bytes 8388608 | tf_op jit(solution)/shard_map/dot_general | solution.py:50
  370.7 8.1 %collective-permute-done.51 = bf16[1024,1408]{1,0:T(8,128)(2,1)} collective-permute-done((bf16[1024,1408]{1,0:T(8,128)(2,1)}, bf16[1024,1408]{1,0:T(8,128)(2,1)}, u32[]{:S(2)}, u32[]{:S(2)}) %collective-permute-start.51) | collective-permute-done | bytes 2883616 | tf_op jit(solution)/shard_map/ppermute | solution.py:715
  380.1 2.5 add_convert_fusion
  387.7 5.3 fusion
  401.3 5.2 collective-permute-done.53
  410.3 5.7 %collective-permute-done.57 = bf16[128,3456]{1,0:T(8,128)(2,1)S(1)} collective-permute-done((bf16[128,3456]{1,0:T(8,128)(2,1)S(1)}, bf16[128,3456]{1,0:T(8,128)(2,1)S(1)}, u32[]{:S(2)}, u32[]{:S(2)}) %collective-permute-start.57) | collective-permute-done | bytes 884768 | tf_op jit(solution)/shard_map/ppermute | solution.py:745
  423.6 10.7 %collective-permute-done.56 = bf16[176,1024]{1,0:T(8,128)(2,1)} collective-permute-done((bf16[176,1024]{1,0:T(8,128)(2,1)}, bf16[176,1024]{1,0:T(8,128)(2,1)}, u32[]{:S(2)}, u32[]{:S(2)}) %collective-permute-start.56) | collective-permute-done | bytes 360480 | tf_op jit(solution)/shard_map/ppermute | solution.py:745
  449.4 6.2 %collective-permute-done.67 = bf16[128,3456]{1,0:T(8,128)(2,1)S(1)} collective-permute-done((bf16[128,3456]{1,0:T(8,128)(2,1)S(1)}, bf16[128,3456]{1,0:T(8,128)(2,1)S(1)}, u32[]{:S(2)}, u32[]{:S(2)}) %collective-permute-start.67) | collective-permute-done | bytes 884768 | tf_op jit(solution)/shard_map/ppermute | solution.py:745
  455.7 5.1 collective-permute-start.66
  461.0 7.0 %collective-permute-start.69 = (bf16[128,3456]{1,0:T(8,128)(2,1)S(1)}, bf16[128,3456]{1,0:T(8,128)(2,1)S(1)}, u32[]{:S(2)}, u32[]{:S(2)}) collective-permute-start(bf16[128,3456]{1,0:T(8,128)(2,1)S(1)} %add_convert_fusion.5), channel_id=1, source_target_pairs={{0,8},{1,5},{2,10},{3,7},{4,0},{5,13},{6,2},{7,15},{8,16},{9,1},{1... | collective-permute-start | bytes 2654216 | tf_op jit(solution)/shard_map/ppermute | solution.py:745
  468.0 4.2 collective-permute-done.66
  472.4 7.0 %collective-permute-done.68 = f32[214,128]{1,0:T(8,128)S(1)} collective-permute-done((f32[214,128]{1,0:T(8,128)S(1)}, f32[214,128]{1,0:T(8,128)S(1)}, u32[]{:S(2)}, u32[]{:S(2)}) %collective-permute-start.68) | collective-permute-done | bytes 109600 | tf_op jit(solution)/shard_map/ppermute | solution.py:804
  481.9 6.6 %collective-permute-start.71 = (bf16[128,3456]{1,0:T(8,128)(2,1)S(1)}, bf16[128,3456]{1,0:T(8,128)(2,1)S(1)}, u32[]{:S(2)}, u32[]{:S(2)}) collective-permute-start(bf16[128,3456]{1,0:T(8,128)(2,1)S(1)} %add_convert_fusion.4), channel_id=1, source_target_pairs={{0,8},{1,5},{2,10},{3,7},{4,0},{5,13},{6,2},{7,15},{8,16},{9,1},{1... | collective-permute-start | bytes 2654216 | tf_op jit(solution)/shard_map/ppermute | solution.py:745
  490.0 5.4 collective-permute-start.70
  495.4 2.8 collective-permute-done.78
  501.8 2.5 collective-permute-start.73
  505.6 5.1 collective-permute-start.72
  512.0 5.3 collective-permute-done.72
  522.5 15.5 %collective-permute-done.74 = bf16[128,3456]{1,0:T(8,128)(2,1)S(1)} collective-permute-done((bf16[128,3456]{1,0:T(8,128)(2,1)S(1)}, bf16[128,3456]{1,0:T(8,128)(2,1)S(1)}, u32[]{:S(2)}, u32[]{:S(2)}) %collective-permute-start.74) | collective-permute-done | bytes 884768 | tf_op jit(solution)/shard_map/ppermute | solution.py:715
  (386 shorter events, 202.8 us)
Async XLA Ops:
  5.6 45.4 %collective-permute-start = (bf16[128,2176]{1,0:T(8,128)(2,1)S(1)}, bf16[128,2176]{1,0:T(8,128)(2,1)}, u32[]{:S(2)}, u32[]{:S(2)}) collective-permute-start(bf16[128,2176]{1,0:T(8,128)(2,1)S(1)} %concatenate.70), channel_id=1, source_target_pairs={{0,8},{1,5},{2,10},{3,7},{4,0},{5,13},{6,2},{7,15},{8,16},{9,1},{1... | collective-permute-start | bytes 1671176 | tf_op jit(solution)/shard_map/ppermute | solution.py:745
  9.6 39.4 %collective-permute-start.1 = (bf16[128,1024]{1,0:T(8,128)(2,1)}, bf16[128,1024]{1,0:T(8,128)(2,1)S(1)}, u32[]{:S(2)}, u32[]{:S(2)}) collective-permute-start(bf16[128,1024]{1,0:T(8,128)(2,1)} %get-tuple-element.206), channel_id=1, source_target_pairs={{0,0},{1,16},{2,2},{3,18},{4,4},{5,20},{6,6},{7,22},{8,8},{9,24},{... | collective-permute-start | bytes 786440 | tf_op jit(solution)/shard_map/ppermute | solution.py:865
  11.2 37.8 %collective-permute-start.2 = (bf16[128,1024]{1,0:T(8,128)(2,1)}, bf16[128,1024]{1,0:T(8,128)(2,1)}, u32[]{:S(2)}, u32[]{:S(2)}) collective-permute-start(bf16[128,1024]{1,0:T(8,128)(2,1)} %get-tuple-element.207), channel_id=1, source_target_pairs={{0,4},{1,20},{2,6},{3,22},{4,8},{5,24},{6,10},{7,26},{8,12},{9,28}... | collective-permute-start | bytes 786440 | tf_op jit(solution)/shard_map/ppermute | solution.py:865
  11.3 37.7 %collective-permute-start.4 = (bf16[128,1024]{1,0:T(8,128)(2,1)}, bf16[128,1024]{1,0:T(8,128)(2,1)}, u32[]{:S(2)}, u32[]{:S(2)}) collective-permute-start(bf16[128,1024]{1,0:T(8,128)(2,1)} %get-tuple-element.208), channel_id=1, source_target_pairs={{0,12},{1,28},{2,14},{3,30},{4,0},{5,16},{6,2},{7,18},{8,4},{9,20}... | collective-permute-start | bytes 786440 | tf_op jit(solution)/shard_map/ppermute | solution.py:865
  14.1 35.6 %collective-permute-start.3 = (bf16[128,1024]{1,0:T(8,128)(2,1)}, bf16[128,1024]{1,0:T(8,128)(2,1)}, u32[]{:S(2)}, u32[]{:S(2)}) collective-permute-start(bf16[128,1024]{1,0:T(8,128)(2,1)} %get-tuple-element.209), channel_id=1, source_target_pairs={{0,8},{1,24},{2,10},{3,26},{4,12},{5,28},{6,14},{7,30},{8,0},{9,16... | collective-permute-start | bytes 786440 | tf_op jit(solution)/shard_map/ppermute | solution.py:865
  99.1 13.5 %collective-permute-start.12 = (bf16[128,1408]{1,0:T(8,128)(2,1)S(1)}, bf16[128,1408]{1,0:T(8,128)(2,1)}, u32[]{:S(2)}, u32[]{:S(2)}) collective-permute-start(bf16[128,1408]{1,0:T(8,128)(2,1)S(1)} %broadcast_select_fusion.14), channel_id=1, source_target_pairs={{0,8},{1,5},{2,10},{3,7},{4,0},{5,13},{6,2},{7,15},{8,16},{9,1},{1... | collective-permute-start | bytes 1081352 | tf_op jit(solution)/shard_map/ppermute | solution.py:745
  101.6 12.5 %collective-permute-start.33 = (bf16[176,1024]{1,0:T(8,128)(2,1)S(1)}, bf16[176,1024]{1,0:T(8,128)(2,1)S(1)}, u32[]{:S(2)}, u32[]{:S(2)}) collective-permute-start(bf16[176,1024]{1,0:T(8,128)(2,1)S(1)} %constant_dynamic-slice_fusion.5), channel_id=1, source_target_pairs={{0,8},{1,5},{2,10},{3,7},{4,0},{5,13},{6,2},{7,15},{8,16},{9,1},{1... | collective-permute-start | bytes 1081352 | tf_op jit(solution)/shard_map/ppermute | solution.py:745
  112.6 23.0 %collective-permute-start.26 = (bf16[128,1408]{1,0:T(8,128)(2,1)}, bf16[128,1408]{1,0:T(8,128)(2,1)}, u32[]{:S(2)}, u32[]{:S(2)}) collective-permute-start(bf16[128,1408]{1,0:T(8,128)(2,1)} %collective-permute-done.12), channel_id=1, source_target_pairs={{0,2},{2,0},{1,3},{3,1},{4,6},{6,4},{5,7},{7,5},{8,10},{10,8},{9,1... | collective-permute-start | bytes 1081352 | tf_op jit(solution)/shard_map/ppermute | solution.py:715
  114.1 20.0 %collective-permute-start.13 = (bf16[128,1408]{1,0:T(8,128)(2,1)}, bf16[128,1408]{1,0:T(8,128)(2,1)S(1)}, u32[]{:S(2)}, u32[]{:S(2)}) collective-permute-start(bf16[128,1408]{1,0:T(8,128)(2,1)} %collective-permute-done.12), channel_id=1, source_target_pairs={{0,8},{1,5},{2,10},{3,7},{4,0},{5,13},{6,2},{7,15},{8,16},{9,1},{1... | collective-permute-start | bytes 1081352 | tf_op jit(solution)/shard_map/ppermute | solution.py:745
  114.1 45.4 %collective-permute-start.34 = (bf16[176,1024]{1,0:T(8,128)(2,1)S(1)}, bf16[176,1024]{1,0:T(8,128)(2,1)S(1)}, u32[]{:S(2)}, u32[]{:S(2)}) collective-permute-start(bf16[176,1024]{1,0:T(8,128)(2,1)S(1)} %collective-permute-done.33), channel_id=1, source_target_pairs={{0,8},{1,5},{2,10},{3,7},{4,0},{5,13},{6,2},{7,15},{8,16},{9,1},{1... | collective-permute-start | bytes 1081352 | tf_op jit(solution)/shard_map/ppermute | solution.py:745
  121.1 45.4 %collective-permute-start.20 = (bf16[128,1024]{1,0:T(8,128)(2,1)S(1)}, bf16[128,1024]{1,0:T(8,128)(2,1)S(1)}, u32[]{:S(2)}, u32[]{:S(2)}) collective-permute-start(bf16[128,1024]{1,0:T(8,128)(2,1)S(1)} %get-tuple-element.200), channel_id=1, source_target_pairs={{0,12},{1,28},{2,14},{3,30},{4,0},{5,16},{6,2},{7,18},{8,4},{9,20}... | collective-permute-start | bytes 786440 | tf_op jit(solution)/shard_map/ppermute | solution.py:865
  124.3 43.7 %collective-permute-start.19 = (bf16[128,1024]{1,0:T(8,128)(2,1)}, bf16[128,1024]{1,0:T(8,128)(2,1)S(1)}, u32[]{:S(2)}, u32[]{:S(2)}) collective-permute-start(bf16[128,1024]{1,0:T(8,128)(2,1)} %get-tuple-element.201), channel_id=1, source_target_pairs={{0,8},{1,24},{2,10},{3,26},{4,12},{5,28},{6,14},{7,30},{8,0},{9,16... | collective-permute-start | bytes 786440 | tf_op jit(solution)/shard_map/ppermute | solution.py:865
  134.1 35.5 %collective-permute-start.18 = (bf16[128,1024]{1,0:T(8,128)(2,1)}, bf16[128,1024]{1,0:T(8,128)(2,1)S(1)}, u32[]{:S(2)}, u32[]{:S(2)}) collective-permute-start(bf16[128,1024]{1,0:T(8,128)(2,1)} %get-tuple-element.202), channel_id=1, source_target_pairs={{0,4},{1,20},{2,6},{3,22},{4,8},{5,24},{6,10},{7,26},{8,12},{9,28}... | collective-permute-start | bytes 786440 | tf_op jit(solution)/shard_map/ppermute | solution.py:865
  135.6 35.6 %collective-permute-start.17 = (bf16[128,1024]{1,0:T(8,128)(2,1)}, bf16[128,1024]{1,0:T(8,128)(2,1)S(1)}, u32[]{:S(2)}, u32[]{:S(2)}) collective-permute-start(bf16[128,1024]{1,0:T(8,128)(2,1)} %get-tuple-element.203), channel_id=1, source_target_pairs={{0,0},{1,16},{2,2},{3,18},{4,4},{5,20},{6,6},{7,22},{8,8},{9,24},{... | collective-permute-start | bytes 786440 | tf_op jit(solution)/shard_map/ppermute | solution.py:865
  159.5 27.1 %collective-permute-start.16 = (bf16[1024,512]{1,0:T(8,128)(2,1)S(1)}, bf16[1024,512]{1,0:T(8,128)(2,1)S(1)}, u32[]{:S(2)}, u32[]{:S(2)}) collective-permute-start(bf16[1024,512]{1,0:T(8,128)(2,1)S(1)} %slice.190), channel_id=1, source_target_pairs={{0,1},{1,0},{2,3},{3,2},{4,5},{5,4},{6,7},{7,6},{8,9},{9,8},{10,11... | collective-permute-start | bytes 3145736 | tf_op jit(solution)/shard_map/ppermute | solution.py:711
  166.5 16.1 %collective-permute-start.27 = (bf16[128,1408]{1,0:T(8,128)(2,1)S(1)}, bf16[128,1408]{1,0:T(8,128)(2,1)S(1)}, u32[]{:S(2)}, u32[]{:S(2)}) collective-permute-start(bf16[128,1408]{1,0:T(8,128)(2,1)S(1)} %collective-permute-done.13), channel_id=1, source_target_pairs={{0,2},{2,0},{1,3},{3,1},{4,6},{6,4},{5,7},{7,5},{8,10},{10,8},{9,1... | collective-permute-start | bytes 1081352 | tf_op jit(solution)/shard_map/ppermute | solution.py:715
  171.2 18.4 %collective-permute-start.21 = (bf16[512,1024]{1,0:T(8,128)(2,1)S(1)}, bf16[512,1024]{1,0:T(8,128)(2,1)S(1)}, u32[]{:S(2)}, u32[]{:S(2)}) collective-permute-start(bf16[512,1024]{1,0:T(8,128)(2,1)S(1)} %pad_maximum_fusion.7), channel_id=1, source_target_pairs={{0,1},{1,0},{2,3},{3,2},{4,5},{5,4},{6,7},{7,6},{8,9},{9,8},{10,11... | collective-permute-start | bytes 3145736 | tf_op jit(solution)/shard_map/ppermute | solution.py:711
  179.3 21.0 %collective-permute-start.22 = (bf16[128,1408]{1,0:T(8,128)(2,1)}, bf16[128,1408]{1,0:T(8,128)(2,1)}, u32[]{:S(2)}, u32[]{:S(2)}) collective-permute-start(bf16[128,1408]{1,0:T(8,128)(2,1)} %collective-permute-done.14), channel_id=1, source_target_pairs={{0,8},{1,5},{2,10},{3,7},{4,0},{5,13},{6,2},{7,15},{8,16},{9,1},{1... | collective-permute-start | bytes 1081352 | tf_op jit(solution)/shard_map/ppermute | solution.py:745
  182.6 19.6 %collective-permute-start.36 = (bf16[176,1024]{1,0:T(8,128)(2,1)S(1)}, bf16[176,1024]{1,0:T(8,128)(2,1)}, u32[]{:S(2)}, u32[]{:S(2)}) collective-permute-start(bf16[176,1024]{1,0:T(8,128)(2,1)S(1)} %collective-permute-done.35), channel_id=1, source_target_pairs={{0,8},{1,5},{2,10},{3,7},{4,0},{5,13},{6,2},{7,15},{8,16},{9,1},{1... | collective-permute-start | bytes 1081352 | tf_op jit(solution)/shard_map/ppermute | solution.py:745
  200.4 15.1 %collective-permute-start.29 = (bf16[128,1408]{1,0:T(8,128)(2,1)}, bf16[128,1408]{1,0:T(8,128)(2,1)S(1)}, u32[]{:S(2)}, u32[]{:S(2)}) collective-permute-start(bf16[128,1408]{1,0:T(8,128)(2,1)} %collective-permute-done.22), channel_id=1, source_target_pairs={{0,2},{2,0},{1,3},{3,1},{4,6},{6,4},{5,7},{7,5},{8,10},{10,8},{9,1... | collective-permute-start | bytes 1081352 | tf_op jit(solution)/shard_map/ppermute | solution.py:715
  208.6 23.1 %collective-permute-start.30 = (bf16[128,1408]{1,0:T(8,128)(2,1)S(1)}, bf16[128,1408]{1,0:T(8,128)(2,1)S(1)}, u32[]{:S(2)}, u32[]{:S(2)}) collective-permute-start(bf16[128,1408]{1,0:T(8,128)(2,1)S(1)} %collective-permute-done.23), channel_id=1, source_target_pairs={{0,2},{2,0},{1,3},{3,1},{4,6},{6,4},{5,7},{7,5},{8,10},{10,8},{9,1... | collective-permute-start | bytes 1081352 | tf_op jit(solution)/shard_map/ppermute | solution.py:715
  217.5 17.2 %collective-permute-start.31 = (bf16[128,1408]{1,0:T(8,128)(2,1)S(1)}, bf16[128,1408]{1,0:T(8,128)(2,1)S(1)}, u32[]{:S(2)}, u32[]{:S(2)}) collective-permute-start(bf16[128,1408]{1,0:T(8,128)(2,1)S(1)} %collective-permute-done.24), channel_id=1, source_target_pairs={{0,2},{2,0},{1,3},{3,1},{4,6},{6,4},{5,7},{7,5},{8,10},{10,8},{9,1... | collective-permute-start | bytes 1081352 | tf_op jit(solution)/shard_map/ppermute | solution.py:715
  218.1 14.4 %collective-permute-start.25 = (bf16[128,1408]{1,0:T(8,128)(2,1)S(1)}, bf16[128,1408]{1,0:T(8,128)(2,1)S(1)}, u32[]{:S(2)}, u32[]{:S(2)}) collective-permute-start(bf16[128,1408]{1,0:T(8,128)(2,1)S(1)} %collective-permute-done.24), channel_id=1, source_target_pairs={{0,8},{1,5},{2,10},{3,7},{4,0},{5,13},{6,2},{7,15},{8,16},{9,1},{1... | collective-permute-start | bytes 1081352 | tf_op jit(solution)/shard_map/ppermute | solution.py:745
  231.6 12.4 %collective-permute-start.40 = (bf16[4,176,1024]{2,1,0:T(8,128)(2,1)S(1)}, bf16[4,176,1024]{2,1,0:T(8,128)(2,1)S(1)}, u32[]{:S(2)}, u32[]{:S(2)}) collective-permute-start(bf16[4,176,1024]{2,1,0:T(8,128)(2,1)S(1)} %constant_dynamic-slice_fusion.4), channel_id=1, source_target_pairs={{0,1},{1,0},{2,3},{3,2},{4,5},{5,4},{6,7},{7,6},{8,9},{9,8},{10,11... | collective-permute-start | bytes 4325384 | tf_op jit(solution)/shard_map/ppermute | solution.py:711
  274.1 41.9 %collective-permute-start.42 = (f32[1024,1024]{1,0:T(8,128)}, f32[1024,1024]{1,0:T(8,128)}, u32[]{:S(2)}, u32[]{:S(2)}) collective-permute-start(f32[1024,1024]{1,0:T(8,128)} %get-tuple-element.106.dn_ref), channel_id=1, source_target_pairs={{0,1},{1,0},{2,3},{3,2},{4,5},{5,4},{6,7},{7,6},{8,9},{9,8},{10,11... | collective-permute-start | bytes 12582920 | tf_op jit(solution)/shard_map/ppermute | solution.py:711
  305.4 45.6 %collective-permute-start.41 = (f32[512,1024]{1,0:T(8,128)}, f32[512,1024]{1,0:T(8,128)}, u32[]{:S(2)}, u32[]{:S(2)}) collective-permute-start(f32[512,1024]{1,0:T(8,128)} %slice.147), channel_id=1, source_target_pairs={{0,1},{1,0},{2,3},{3,2},{4,5},{5,4},{6,7},{7,6},{8,9},{9,8},{10,11... | collective-permute-start | bytes 6291464 | tf_op jit(solution)/shard_map/ppermute | solution.py:711
  311.5 15.5 %collective-permute-start.48 = (bf16[176,1024]{1,0:T(8,128)(2,1)S(1)}, bf16[176,1024]{1,0:T(8,128)(2,1)S(1)}, u32[]{:S(2)}, u32[]{:S(2)}) collective-permute-start(bf16[176,1024]{1,0:T(8,128)(2,1)S(1)} %get-tuple-element.169), channel_id=1, source_target_pairs={{0,8},{1,5},{2,10},{3,7},{4,0},{5,13},{6,2},{7,15},{8,16},{9,1},{1... | collective-permute-start | bytes 1081352 | tf_op jit(solution)/shard_map/ppermute | solution.py:745
  314.4 64.4 %collective-permute-start.51 = (bf16[1024,1408]{1,0:T(8,128)(2,1)}, bf16[1024,1408]{1,0:T(8,128)(2,1)}, u32[]{:S(2)}, u32[]{:S(2)}) collective-permute-start(bf16[1024,1408]{1,0:T(8,128)(2,1)} %outer.3), channel_id=1, source_target_pairs={{0,2},{2,0},{1,3},{3,1},{4,6},{6,4},{5,7},{7,5},{8,10},{10,8},{9,1... | collective-permute-start | bytes 8650760 | tf_op jit(solution)/shard_map/ppermute | solution.py:715
  327.8 34.9 %collective-permute-start.49 = (bf16[176,1024]{1,0:T(8,128)(2,1)}, bf16[176,1024]{1,0:T(8,128)(2,1)S(1)}, u32[]{:S(2)}, u32[]{:S(2)}) collective-permute-start(bf16[176,1024]{1,0:T(8,128)(2,1)} %add_convert_fusion.15), channel_id=1, source_target_pairs={{0,8},{1,5},{2,10},{3,7},{4,0},{5,13},{6,2},{7,15},{8,16},{9,1},{1... | collective-permute-start | bytes 1081352 | tf_op jit(solution)/shard_map/ppermute | solution.py:745
  355.6 41.8 %collective-permute-start.47 = (bf16[128,1024]{1,0:T(8,128)(2,1)}, bf16[128,1024]{1,0:T(8,128)(2,1)}, u32[]{:S(2)}, u32[]{:S(2)}) collective-permute-start(bf16[128,1024]{1,0:T(8,128)(2,1)} %get-tuple-element.196), channel_id=1, source_target_pairs={{12,0},{28,1},{14,2},{30,3},{0,4},{16,5},{2,6},{18,7},{4,8},{20,9}... | collective-permute-start | bytes 786440 | tf_op jit(solution)/shard_map/ppermute | solution.py:877
  356.0 39.7 %collective-permute-start.46 = (bf16[128,1024]{1,0:T(8,128)(2,1)}, bf16[128,1024]{1,0:T(8,128)(2,1)}, u32[]{:S(2)}, u32[]{:S(2)}) collective-permute-start(bf16[128,1024]{1,0:T(8,128)(2,1)} %get-tuple-element.197), channel_id=1, source_target_pairs={{8,0},{24,1},{10,2},{26,3},{12,4},{28,5},{14,6},{30,7},{0,8},{16,9... | collective-permute-start | bytes 786440 | tf_op jit(solution)/shard_map/ppermute | solution.py:877
  359.8 34.2 %collective-permute-start.45 = (bf16[128,1024]{1,0:T(8,128)(2,1)}, bf16[128,1024]{1,0:T(8,128)(2,1)}, u32[]{:S(2)}, u32[]{:S(2)}) collective-permute-start(bf16[128,1024]{1,0:T(8,128)(2,1)} %get-tuple-element.198), channel_id=1, source_target_pairs={{4,0},{20,1},{6,2},{22,3},{8,4},{24,5},{10,6},{26,7},{12,8},{28,9}... | collective-permute-start | bytes 786440 | tf_op jit(solution)/shard_map/ppermute | solution.py:877
  362.8 30.5 %collective-permute-start.44 = (bf16[128,1024]{1,0:T(8,128)(2,1)}, bf16[128,1024]{1,0:T(8,128)(2,1)S(1)}, u32[]{:S(2)}, u32[]{:S(2)}) collective-permute-start(bf16[128,1024]{1,0:T(8,128)(2,1)} %get-tuple-element.199), channel_id=1, source_target_pairs={{0,0},{16,1},{2,2},{18,3},{4,4},{20,5},{6,6},{22,7},{8,8},{24,9},{... | collective-permute-start | bytes 786440 | tf_op jit(solution)/shard_map/ppermute | solution.py:877
  386.2 14.4 %collective-permute-start.54 = (bf16[128,3456]{1,0:T(8,128)(2,1)S(1)}, bf16[128,3456]{1,0:T(8,128)(2,1)S(1)}, u32[]{:S(2)}, u32[]{:S(2)}) collective-permute-start(bf16[128,3456]{1,0:T(8,128)(2,1)S(1)} %get-tuple-element.161), channel_id=1, source_target_pairs={{0,8},{1,5},{2,10},{3,7},{4,0},{5,13},{6,2},{7,15},{8,16},{9,1},{1... | collective-permute-start | bytes 2654216 | tf_op jit(solution)/shard_map/ppermute | solution.py:745
  393.2 14.1 %collective-permute-start.52 = (f32[512,1024]{1,0:T(8,128)S(1)}, f32[512,1024]{1,0:T(8,128)S(1)}, u32[]{:S(2)}, u32[]{:S(2)}) collective-permute-start(f32[512,1024]{1,0:T(8,128)S(1)} %slice.197), channel_id=1, source_target_pairs={{0,1},{1,0},{2,3},{3,2},{4,5},{5,4},{6,7},{7,6},{8,9},{9,8},{10,11... | collective-permute-start | bytes 6291464 | tf_op jit(solution)/shard_map/ppermute | solution.py:711
  400.8 15.1 %collective-permute-start.57 = (bf16[128,3456]{1,0:T(8,128)(2,1)S(1)}, bf16[128,3456]{1,0:T(8,128)(2,1)S(1)}, u32[]{:S(2)}, u32[]{:S(2)}) collective-permute-start(bf16[128,3456]{1,0:T(8,128)(2,1)S(1)} %add_convert_fusion.8), channel_id=1, source_target_pairs={{0,8},{1,5},{2,10},{3,7},{4,0},{5,13},{6,2},{7,15},{8,16},{9,1},{1... | collective-permute-start | bytes 2654216 | tf_op jit(solution)/shard_map/ppermute | solution.py:745
  417.1 20.0 %collective-permute-start.64 = (bf16[128,3456]{1,0:T(8,128)(2,1)}, bf16[128,3456]{1,0:T(8,128)(2,1)}, u32[]{:S(2)}, u32[]{:S(2)}) collective-permute-start(bf16[128,3456]{1,0:T(8,128)(2,1)} %add_convert_fusion.7), channel_id=1, source_target_pairs={{0,8},{1,5},{2,10},{3,7},{4,0},{5,13},{6,2},{7,15},{8,16},{9,1},{1... | collective-permute-start | bytes 2654216 | tf_op jit(solution)/shard_map/ppermute | solution.py:745
  419.4 14.9 %collective-permute-start.56 = (bf16[176,1024]{1,0:T(8,128)(2,1)}, bf16[176,1024]{1,0:T(8,128)(2,1)}, u32[]{:S(2)}, u32[]{:S(2)}) collective-permute-start(bf16[176,1024]{1,0:T(8,128)(2,1)} %add_convert_fusion.12), channel_id=1, source_target_pairs={{0,8},{1,5},{2,10},{3,7},{4,0},{5,13},{6,2},{7,15},{8,16},{9,1},{1... | collective-permute-start | bytes 1081352 | tf_op jit(solution)/shard_map/ppermute | solution.py:745
  423.5 13.5 %collective-permute-start.62 = (f32[214,128]{1,0:T(8,128)S(1)}, f32[214,128]{1,0:T(8,128)S(1)}, u32[]{:S(2)}, u32[]{:S(2)}) collective-permute-start(f32[214,128]{1,0:T(8,128)S(1)} %concatenate.84), channel_id=1, source_target_pairs={{0,1},{1,0},{2,3},{3,2},{4,5},{5,4},{6,7},{7,6},{8,9},{9,8},{10,11... | collective-permute-start | bytes 328712 | tf_op jit(solution)/shard_map/ppermute | solution.py:711
  438.5 17.2 %collective-permute-start.67 = (bf16[128,3456]{1,0:T(8,128)(2,1)S(1)}, bf16[128,3456]{1,0:T(8,128)(2,1)S(1)}, u32[]{:S(2)}, u32[]{:S(2)}) collective-permute-start(bf16[128,3456]{1,0:T(8,128)(2,1)S(1)} %add_convert_fusion.6), channel_id=1, source_target_pairs={{0,8},{1,5},{2,10},{3,7},{4,0},{5,13},{6,2},{7,15},{8,16},{9,1},{1... | collective-permute-start | bytes 2654216 | tf_op jit(solution)/shard_map/ppermute | solution.py:745
  445.0 43.6 %collective-permute-start.61 = (bf16[128,1024]{1,0:T(8,128)(2,1)S(1)}, bf16[128,1024]{1,0:T(8,128)(2,1)S(1)}, u32[]{:S(2)}, u32[]{:S(2)}) collective-permute-start(bf16[128,1024]{1,0:T(8,128)(2,1)S(1)} %get-tuple-element.192), channel_id=1, source_target_pairs={{12,0},{28,1},{14,2},{30,3},{0,4},{16,5},{2,6},{18,7},{4,8},{20,9}... | collective-permute-start | bytes 786440 | tf_op jit(solution)/shard_map/ppermute | solution.py:877
  445.7 26.7 %collective-permute-start.60 = (bf16[128,1024]{1,0:T(8,128)(2,1)S(1)}, bf16[128,1024]{1,0:T(8,128)(2,1)S(1)}, u32[]{:S(2)}, u32[]{:S(2)}) collective-permute-start(bf16[128,1024]{1,0:T(8,128)(2,1)S(1)} %get-tuple-element.193), channel_id=1, source_target_pairs={{8,0},{24,1},{10,2},{26,3},{12,4},{28,5},{14,6},{30,7},{0,8},{16,9... | collective-permute-start | bytes 786440 | tf_op jit(solution)/shard_map/ppermute | solution.py:877
  446.8 21.1 %collective-permute-start.59 = (bf16[128,1024]{1,0:T(8,128)(2,1)S(1)}, bf16[128,1024]{1,0:T(8,128)(2,1)S(1)}, u32[]{:S(2)}, u32[]{:S(2)}) collective-permute-start(bf16[128,1024]{1,0:T(8,128)(2,1)S(1)} %get-tuple-element.194), channel_id=1, source_target_pairs={{4,0},{20,1},{6,2},{22,3},{8,4},{24,5},{10,6},{26,7},{12,8},{28,9}... | collective-permute-start | bytes 786440 | tf_op jit(solution)/shard_map/ppermute | solution.py:877
  455.7 16.5 %collective-permute-start.66 = (bf16[176,1024]{1,0:T(8,128)(2,1)S(1)}, bf16[176,1024]{1,0:T(8,128)(2,1)S(1)}, u32[]{:S(2)}, u32[]{:S(2)}) collective-permute-start(bf16[176,1024]{1,0:T(8,128)(2,1)S(1)} %add_convert_fusion.10), channel_id=1, source_target_pairs={{0,8},{1,5},{2,10},{3,7},{4,0},{5,13},{6,2},{7,15},{8,16},{9,1},{1... | collective-permute-start | bytes 1081352 | tf_op jit(solution)/shard_map/ppermute | solution.py:745
  461.0 20.7 %collective-permute-start.69 = (bf16[128,3456]{1,0:T(8,128)(2,1)S(1)}, bf16[128,3456]{1,0:T(8,128)(2,1)S(1)}, u32[]{:S(2)}, u32[]{:S(2)}) collective-permute-start(bf16[128,3456]{1,0:T(8,128)(2,1)S(1)} %add_convert_fusion.5), channel_id=1, source_target_pairs={{0,8},{1,5},{2,10},{3,7},{4,0},{5,13},{6,2},{7,15},{8,16},{9,1},{1... | collective-permute-start | bytes 2654216 | tf_op jit(solution)/shard_map/ppermute | solution.py:745
  481.9 19.5 %collective-permute-start.71 = (bf16[128,3456]{1,0:T(8,128)(2,1)S(1)}, bf16[128,3456]{1,0:T(8,128)(2,1)S(1)}, u32[]{:S(2)}, u32[]{:S(2)}) collective-permute-start(bf16[128,3456]{1,0:T(8,128)(2,1)S(1)} %add_convert_fusion.4), channel_id=1, source_target_pairs={{0,8},{1,5},{2,10},{3,7},{4,0},{5,13},{6,2},{7,15},{8,16},{9,1},{1... | collective-permute-start | bytes 2654216 | tf_op jit(solution)/shard_map/ppermute | solution.py:745
  501.8 15.5 %collective-permute-start.73 = (bf16[128,3456]{1,0:T(8,128)(2,1)S(1)}, bf16[128,3456]{1,0:T(8,128)(2,1)S(1)}, u32[]{:S(2)}, u32[]{:S(2)}) collective-permute-start(bf16[128,3456]{1,0:T(8,128)(2,1)S(1)} %add_convert_fusion.3), channel_id=1, source_target_pairs={{0,8},{1,5},{2,10},{3,7},{4,0},{5,13},{6,2},{7,15},{8,16},{9,1},{1... | collective-permute-start | bytes 2654216 | tf_op jit(solution)/shard_map/ppermute | solution.py:745
  517.6 20.4 %collective-permute-start.74 = (bf16[128,3456]{1,0:T(8,128)(2,1)S(1)}, bf16[128,3456]{1,0:T(8,128)(2,1)S(1)}, u32[]{:S(2)}, u32[]{:S(2)}) collective-permute-start(bf16[128,3456]{1,0:T(8,128)(2,1)S(1)} %add_convert_fusion.2), channel_id=1, source_target_pairs={{0,2},{2,0},{1,3},{3,1},{4,6},{6,4},{5,7},{7,5},{8,10},{10,8},{9,1... | collective-permute-start | bytes 2654216 | tf_op jit(solution)/shard_map/ppermute | solution.py:715
  (79 other events, 740.9 us)

commit v4 on v3

--- a/solution.py
+++ b/solution.py
@@ -495,7 +495,7 @@
         out_shape=[jax.ShapeDtypeStruct((rows, cv), BF16), jax.ShapeDtypeStruct((rows, cv), F32),
                    jax.ShapeDtypeStruct((steps, PAIR, DV, DK), F32)],
         compiler_params=pltpu.CompilerParams(vmem_limit_bytes=58 * 1024 * 1024),
-        cost_estimate=pl.CostEstimate(flops=1000, bytes_accessed=1000, transcendentals=0),
+        cost_estimate=pl.CostEstimate(flops=22_000_000_000, bytes_accessed=1000, transcendentals=0),
         name="mix_forward",
     )(order, q, k, v, logits, og, gain, sums, masks)
 
@@ -528,7 +528,7 @@
         out_shape=[jax.ShapeDtypeStruct((rows, 2 * ck + 2 * cv), BF16), jax.ShapeDtypeStruct((rows, ck), BF16),
                    jax.ShapeDtypeStruct((1, DV), F32), jax.ShapeDtypeStruct((1, ck), F32)],
         compiler_params=pltpu.CompilerParams(vmem_limit_bytes=58 * 1024 * 1024),
-        cost_estimate=pl.CostEstimate(flops=1000, bytes_accessed=1000, transcendentals=0),
+        cost_estimate=pl.CostEstimate(flops=6_000_000_000, bytes_accessed=1000, transcendentals=0),
         name="mix_backward",
     )(order, q, k, v, logits, og, mixed, d_gated, states, gain, sums, masks, upper)
 
@@ -703,6 +703,31 @@
     )(n, d)
 
 
+def outer_wide_kernel(n_ref, d_ref, g_ref, turned):
+    @pl.when(pl.program_id(0) == 0)
+    def _():
+        turned[...] = n_ref[...].T
+
+    g_ref[...] = dot_nn(turned[...], d_ref[...]).astype(BF16)
+
+
+def outer_wide(n, d):
+    rows, width = n.shape
+    step = 256
+    column = pl.BlockSpec((rows, step), lambda i: (0, i))
+    return pl.pallas_call(
+        outer_wide_kernel,
+        grid=(d.shape[1] // step,),
+        in_specs=[held(n), column],
+        out_specs=pl.BlockSpec((width, step), lambda i: (0, i)),
+        out_shape=jax.ShapeDtypeStruct((width, d.shape[1]), BF16),
+        scratch_shapes=[pltpu.VMEM((width, rows), BF16)],
+        compiler_params=ROOMY,
+        cost_estimate=FREE,
+        name="outer_wide",
+    )(n, d)
+
+
 def device_of(shard, x, core, xs):
     return (shard * xs + x) * 2 + core
 
@@ -721,71 +746,93 @@
 
 class Ring:
     def __init__(self):
-        self.shards, self.xs = lax.axis_size("shard"), lax.axis_size("x")
-        self.core = lax.axis_index("core")
+        self.shards, xs = lax.axis_size("shard"), lax.axis_size("x")
         cycle = ring_order(self.shards)
         spot = [cycle.index(s) for s in range(self.shards)]
         self.cycle = jnp.asarray(cycle, jnp.int32)
         self.spot = jnp.asarray(spot, jnp.int32)[lax.axis_index("shard")]
-        self.sign = 1 - 2 * self.core
-        self.pairs = []
-        for s in range(self.shards):
-            for x in range(self.xs):
-                for c in range(2):
-                    step = 1 if c == 0 else -1
-                    to = cycle[(spot[s] + step) % self.shards]
-                    self.pairs.append(
-                        (device_of(s, x, c, self.xs), device_of(to, x, c, self.xs))
-                    )
-
-    def behind(self, hops):
-        return self.cycle[(self.spot - self.sign * hops) % self.shards]
+        self.ahead, self.back = (
+            [
+                (
+                    device_of(s, x, c, xs),
+                    device_of(cycle[(spot[s] + step) % self.shards], x, c, xs),
+                )
+                for s in range(self.shards)
+                for x in range(xs)
+                for c in range(2)
+            ]
+            for step in (1, -1)
+        )
+        self.far = self.shards // 2
+        self.near = (self.shards - 1) // 2
+
+    def at(self, offset):
+        return self.cycle[(self.spot + offset) % self.shards]
 
     def send(self, a):
-        return lax.ppermute(a, AXES, self.pairs)
-
-    def gather(self, piece, early=None):
-        whole = jnp.zeros((self.shards,) + piece.shape, piece.dtype)
-        pieces = [piece]
-        for hops in range(self.shards - 1):
-            if hops == 1 and early is not None:
-                pieces[-1], early = lax.optimization_barrier((pieces[-1], early))
-            pieces.append(self.send(pieces[-1]))
-        for hops, a in enumerate(pieces):
-            whole = lax.dynamic_update_index_in_dim(whole, a, self.behind(hops), 0)
-        return whole, pieces, early
-
-    def own(self, blocks, hops):
-        return lax.dynamic_index_in_dim(blocks, self.behind(hops), 0, False)
+        return lax.ppermute(a, AXES, self.ahead)
+
+    def send_back(self, a):
+        return lax.ppermute(a, AXES, self.back)
 
 
 class Gather:
     def __init__(self, ring, piece):
-        self.ring, self.hops, self.last = ring, 0, piece
+        self.ring, self.hops = ring, 0
+        self.ahead = self.back = piece
         self.whole = jnp.zeros((ring.shards,) + piece.shape, piece.dtype)
-        self.keep(piece)
-
-    def keep(self, piece):
+        self.keep(piece, 0)
+
+    def keep(self, piece, offset):
         self.whole = lax.dynamic_update_index_in_dim(
-            self.whole, piece, self.ring.behind(self.hops), 0
+            self.whole, piece, self.ring.at(offset), 0
         )
 
-    def take(self, arrived, *deps):
+    def hop(self, *deps):
         self.hops += 1
-        self.last = after(arrived, *deps)
-        self.keep(self.last)
+        arrived = []
+        if self.hops <= self.ring.far:
+            self.ahead = after(self.ring.send(self.ahead), *deps)
+            self.keep(self.ahead, -self.hops)
+            arrived.append((self.ahead, -self.hops))
+        if self.hops <= self.ring.near:
+            self.back = after(self.ring.send_back(self.back), *deps)
+            self.keep(self.back, self.hops)
+            arrived.append((self.back, self.hops))
+        return arrived
 
 
 class Scatter:
     def __init__(self, ring, blocks):
-        self.ring, self.blocks, self.hops = ring, blocks, 1
-        self.moving = ring.own(blocks, 1)
+        self.ring, self.blocks, self.hops = ring, blocks, 0
+        self.ahead, self.back = self.own(ring.far), self.own(-ring.near)
+        self.moving = self.ahead
+
+    def own(self, offset, *deps):
+        block = lax.dynamic_index_in_dim(self.blocks, self.ring.at(offset), 0, False)
+        return after(block, *deps)
+
+    def add(self, *terms):
+        total = terms[0].astype(F32)
+        for term in terms[1:]:
+            total = total + term.astype(F32)
+        return total.astype(BF16)
 
     def hop(self, *deps):
         self.hops += 1
-        arrived = self.ring.send(self.moving)
-        mine = after(self.ring.own(self.blocks, self.hops), *deps)
-        self.moving = (arrived.astype(F32) + mine.astype(F32)).astype(BF16)
+        far, near = self.ring.far - self.hops, self.ring.near - self.hops
+        arrived = self.ring.send(self.ahead)
+        if near >= 0:
+            arrived_back = self.ring.send_back(self.back)
+            if near > 0:
+                self.back = self.add(arrived_back, self.own(-near, *deps))
+            else:
+                self.back = arrived_back
+        if far > 0:
+            self.ahead = self.add(arrived, self.own(far, *deps))
+        else:
+            self.ahead = self.add(arrived, self.back, self.own(0, *deps))
+        self.moving = self.ahead
         return self.moving
 
 
@@ -881,8 +928,10 @@
             )
             for step in range(seqs)
         ]
-        twice = jnp.stack(back + back, 0)
-        return lax.dynamic_slice_in_dim(twice, (seqs - piece) % seqs, seqs, 0)
+        out = jnp.zeros((seqs,) + back[0].shape, a.dtype)
+        for step, part in enumerate(back):
+            out = lax.dynamic_update_index_in_dim(out, part, (step + piece) % seqs, 0)
+        return out
 
     counter = jnp.arange(shards, dtype=jnp.int32)
     order = ((counter // seqs) ^ core) * seqs + (piece - counter) % seqs
@@ -905,19 +954,26 @@
     wide = 2 * ck + 2 * cv
     own = rows_in(tokens)
     ring = Ring()
-    attn_full, attn_pieces, own = ring.gather(packed, own)
-    attn_full = attn_full.reshape(width, -1)
+    attn_ring = Gather(ring, packed)
+    attn_ring.hop()
+    attn_ring.ahead, attn_ring.back, own = lax.optimization_barrier(
+        (attn_ring.ahead, attn_ring.back, own)
+    )
+    for _ in range(1, ring.far - 1):
+        attn_ring.hop()
+    attn_late = attn_ring.ahead
+    attn_ring.hop()
+    attn_full = attn_ring.whole.reshape(width, -1)
     plane = lax.axis_index("x") == 0
     gate_piece, up_piece = core_half(w_gate, 1), core_half(w_up, 1)
-    near_ring = Gather(ring, after(jnp.where(plane, gate_piece, up_piece), attn_pieces[6]))
+    near_ring = Gather(ring, after(jnp.where(plane, gate_piece, up_piece), attn_late))
     far_ring = Gather(ring, jnp.where(plane, up_piece, gate_piece))
-    down_ring = Gather(ring, after(core_half(w_down, 0), attn_pieces[6]))
-    own_grad = rows_in(after(out_grad, attn_pieces[7]))
+    down_ring = Gather(ring, after(core_half(w_down, 0), attn_late))
 
     def ffn_hop(*deps):
-        down_ring.take(ring.send(down_ring.last), *deps)
-        near_ring.take(ring.send(near_ring.last), *deps)
-        far_ring.take(x_swap(near_ring.last))
+        down_ring.hop(*deps)
+        for piece, offset in near_ring.hop(*deps):
+            far_ring.keep(x_swap(piece), offset)
 
     ffn_hop()
     x_low = jnp.concatenate([own, core_swap(own)], 0)
@@ -930,21 +986,20 @@
         x_low, attn_row[None], attn_full, rank_out, bias
     )
     gain = head_gain.astype(F32)[None]
-    ffn_hop(queries)
-    queries = after(queries, near_ring.last)
+    for _ in range(1, ring.far):
+        ffn_hop()
+    queries = after(queries, near_ring.ahead, down_ring.ahead)
+    own_grad = rows_in(after(out_grad, near_ring.ahead))
     gated, mixed, states = mix_forward(
         order, queries, keys, values, logits, out_gate, gain, sums, masks
     )
-    ffn_hop(gated)
-    gated = after(gated, near_ring.last)
     gated_full = by_core(gated, swap_rows(core_swap(gated)), 1)
     out_mine = attn_full[:, wide : wide + cv]
     w_out_full = by_core(out_mine, core_swap(out_mine), 1)
     ffn_row = ffn_gain.astype(F32)
     residual, ffn_in, r_ffn = attn_out(x_low, gated_full, w_out_full, ffn_row[None])
-    ffn_hop(ffn_in)
-    for _ in range(4, shards - 1):
-        ffn_hop()
+    ffn_in, own_grad = lax.optimization_barrier((ffn_in, own_grad))
+    dy = jnp.concatenate([own_grad, core_swap(own_grad)], 0)
     cols_near = near_ring.whole.reshape(width, -1)
     cols_far = far_ring.whole.reshape(width, -1)
     down_rows = down_ring.whole
@@ -956,7 +1011,6 @@
     other_down = core_swap(send_down)
     w_down_half = by_core(mine_down, other_down, 1).reshape(ff_half, width)
 
-    dy = jnp.concatenate([own_grad, core_swap(own_grad)], 0)
     turn = lax.axis_index("x")[None].astype(jnp.int32)
     hidden, d_near, d_far, block_part, dn_part = ffn(
         turn, ffn_in, dy, cols_near, cols_far, w_down_half
@@ -967,8 +1021,12 @@
     far_part = outer(ffn_in, d_far)
     grad_far = x_swap(far_part)
     grad_near = outer(after(ffn_in, far_part), d_near)
-    hidden = after(hidden, grad_near)
-    down_grad = outer(hidden, dy, 128).reshape(group, 2, -1, width)
+    block_own = (
+        residual[:half_rows] + block_part[:half_rows] + after(block_swapped, far_part)
+    ).astype(BF16)
+    block_out = rows_out(block_own)
+    hidden = after(hidden, grad_near, block_own)
+    down_grad = outer_wide(hidden, dy).reshape(group, 2, -1, width)
     mine_dg = lax.dynamic_index_in_dim(down_grad, core, 1, False)
     other_dg = core_swap(lax.dynamic_index_in_dim(down_grad, 1 - core, 1, False))
     down = Scatter(ring, by_core(mine_dg, other_dg, 0))
@@ -979,21 +1037,18 @@
     )
     ffn_gain_grad = ffn_gain_grad[0]
     down.hop(d_gated)
-    block_own = (
-        residual[:half_rows] + block_part[:half_rows] + after(block_swapped, d_gated)
-    ).astype(BF16)
-    block_out = rows_out(block_own)
     d_all, d_logits, hgain_part, bias_part = mix_backward(
-        order, queries, keys, values, logits, out_gate, mixed, after(d_gated, down.moving),
+        order, queries, keys, values, logits, out_gate, mixed, after(d_gated, down.moving, block_out),
         states, gain, sums, masks, upper
     )
     down.hop(d_all)
     d_all = after(d_all, down.moving)
-    out_w_grad = outer_sum(gated_full, core_half(d_branch, 1))
-    qkvo_grad = outer_sum(normed, d_all)
-    near_total = after(grad_near, d_all).astype(F32) + grad_far.astype(F32)
+    qkvo_grad = outer(normed, d_all)
+    down.hop(qkvo_grad)
+    out_w_grad = outer(after(gated_full, down.moving), core_half(d_branch, 1))
+    near_total = after(grad_near, out_w_grad).astype(F32) + grad_far.astype(F32)
     last_grad = jnp.concatenate(
-        [qkvo_grad.astype(BF16), out_w_grad.astype(BF16), near_total.astype(BF16)], 1
+        [qkvo_grad, out_w_grad, near_total.astype(BF16)], 1
     )
     attn = Scatter(ring, last_grad.reshape(shards, -1, wide + cv + ff_half))
     down.hop(attn.moving)
@@ -1003,7 +1058,6 @@
     dn_attn = times_transpose(after(d_all, down.moving), attn_full[:, :wide])
     dn_attn_swapped = core_swap(dn_attn[half_rows:])
     attn.hop(dn_attn)
-    down.hop(dn_attn, attn.moving)
     dn_attn_swapped = after(dn_attn_swapped, down.moving)
     d_rank = (rank_part + swap_rows(rank_swapped)).astype(BF16)
     rank_in_grad = outer_sum(d_rank[:half_rows], normed[:half_rows])
@@ -1021,8 +1075,6 @@
     ).astype(BF16)
     attn_gain_grad = jnp.sum(dn_own * own_in * own_r, axis=0)
     attn.hop(tok_grad)
-    down.hop(tok_grad, attn.moving)
-    tokens_grad = rows_out(after(tok_grad, down.moving))
 
     first = (core == 0).astype(F32)
 
@@ -1041,19 +1093,20 @@
     )
     small = jnp.concatenate([flat(a) for a in parts], 0)
     steps = tree_steps()
-    for count in range(3, shards):
-        if count < 3 + len(steps):
-            small = small + steps[count - 3](small)
-        attn.hop(small)
-        if down.hops < shards:
-            down.hop(attn.moving)
-            small = after(small, down.moving)
-        else:
-            small = after(small, attn.moving)
-    for step in steps[shards - 3 :]:
+    small = after(small, attn.moving)
+    for step in steps[:2]:
         small = small + step(small)
+    for _ in range(2, ring.far - 1):
+        attn.hop()
+    tokens_grad = rows_out(after(tok_grad, attn.moving))
+    attn.hop(small)
+    small = after(small, attn.moving)
     last_own, down_own = attn.moving, down.moving
     last_far = x_swap(last_own)
+    for step in steps[2:-1]:
+        small = small + step(small)
+    small, last_far = lax.optimization_barrier((small, last_far))
+    small = small + steps[-1](small)
     split_at = wide + cv
     near_own, far_own = last_own[:, split_at:], last_far[:, split_at:]
     gate_own = jnp.where(plane, near_own, far_own)

time: 560 us -> 531 us (0.948)
  starting transfers between devices: 128 us -> 101 us
  local copies, waits for them, and re-layouts: 82.9 us -> 69.4 us
  Pallas kernels: 118 us -> 127 us
  matrix products: 18.5 us -> 10.2 us
  waiting for transfers between devices: 131 us -> 138 us
    ppermute x11, waiting for transfers between devices: 34.2 us -> 7.26 us  [x_swap(): return lax.ppermute(a, 'x', [(0, 1), (1, 0)])]
    ppermute x8, waiting for transfers between devices: 0.02 us -> 24.2 us  [rows_out(): lax.ppermute(a[step * tok_dev:(step + 1) * tok_dev], AXES, [(t, s) for s,...]
    ppermute x35, starting transfers between devices: 67.8 us -> 45.4 us  [the longest x20 31.4 us: send(): return lax.ppermute(a, AXES, self.ahead)]
    ppermute x35, waiting for transfers between devices: 82.2 us -> 98.5 us  [the longest x20 84.4 us: send(): return lax.ppermute(a, AXES, self.ahead)]
    dot_general x4 -> x2, matrix products: 9.89 us -> 1.49 us  [outer_sum(): lax.dot_general(left_side, right_side, (((0,), (0,)), ((), ())), preferre...]
    unnamed x115 -> x74, local copies, waits for them, and re-layouts: 14 us -> 5.62 us
    pallas_call x0 -> x1, Pallas kernels: none -> 7.92 us  [outer_wide(): pl.pallas_call(outer_wide_kernel, grid=(d.shape[1] // step,), in_specs=[h...]
    ppermute x3, waiting for transfers between devices: 13.8 us -> 7.97 us  [tree_steps(): steps.append(lambda a, pairs=pairs: lax.ppermute(a, 'shard', pairs))]
  transfers between devices with their start and end apart: 80 -> 80, of which waited for: 28 -> 22; matrix products, arithmetic and copies ran while one was open for 23% -> 21% of each run, Pallas kernels for 17% -> 19%
where the time goes in v4:
time: 531 us; the launch traced here: 521 us
  waiting for transfers between devices  138 us (26%)
  Pallas kernels  127 us (24%)
  starting transfers between devices  101 us (19%)
  local copies, waits for them, and re-layouts  69.4 us (13%)
  other arithmetic  48.3 us (9%)
  between operations  26.7 us (5%)
  matrix products  10.2 us (2%)
    ppermute x20, waiting for transfers between devices, send(): return lax.ppermute(a, AXES, self.ahead)  84.4 us
    ppermute x20, starting transfers between devices, send(): return lax.ppermute(a, AXES, self.ahead)  31.4 us
    dynamic_update_slice x31, local copies, waits for them, and re-layouts, keep(): lax.dynamic_update_index_in_dim(self.whole, piece, self.ring.at(offset), 0)  30.5 us
    pallas_call x4, Pallas kernels, outer(): pl.pallas_call(outer_kernel, grid=(width // step,), in_specs=[pl.BlockSpe...  26.8 us
    pallas_call x1, Pallas kernels, ffn(): pl.pallas_call(ffn_kernel, grid_spec=pltpu.PrefetchScalarGridSpec(num_sca...  26.4 us
    ppermute x8, waiting for transfers between devices, rows_out(): lax.ppermute(a[step * tok_dev:(step + 1) * tok_dev], AXES, [(t, s) for s,...  24.2 us
    pallas_call x1, Pallas kernels, mix_forward(): pl.pallas_call(mix_forward_kernel, grid_spec=pltpu.PrefetchScalarGridSpec...  20.7 us
    pallas_call x1, Pallas kernels, mix_backward(): pl.pallas_call(mix_backward_kernel, grid_spec=pltpu.PrefetchScalarGridSpe...  18.1 us
  transfers between devices with their start and end apart: 80, of which 22 were waited for; matrix products, arithmetic and copies ran while one was open for 21% of the time, Pallas kernels for 19%

profile of v4, /device:TPU:0, one launch (start us, length us, event | category | flops | bytes accessed | tf_op | source)
XLA Modules:
  0.0 520.5 jit_solution(11166639838411665057)
XLA Ops:
  5.5 3.1 collective-permute-start
  9.6 3.6 collective-permute-start.2
  27.4 2.7 broadcast_in_dim.160
  61.9 9.0 %collective-permute-done.7 = bf16[128,2176]{1,0:T(8,128)(2,1)S(1)} collective-permute-done((bf16[128,2176]{1,0:T(8,128)(2,1)}, bf16[128,2176]{1,0:T(8,128)(2,1)S(1)}, u32[]{:S(2)}, u32[]{:S(2)}) %collective-permute-start.7) | collective-permute-done | bytes 557088 | tf_op jit(solution)/shard_map/ppermute | solution.py:773
  74.6 10.0 %collective-permute-done.9 = bf16[128,2176]{1,0:T(8,128)(2,1)S(1)} collective-permute-done((bf16[128,2176]{1,0:T(8,128)(2,1)S(1)}, bf16[128,2176]{1,0:T(8,128)(2,1)S(1)}, u32[]{:S(2)}, u32[]{:S(2)}) %collective-permute-start.9) | collective-permute-done | bytes 557088 | tf_op jit(solution)/shard_map/ppermute | solution.py:773
  99.1 4.6 collective-permute-done.12
  108.0 7.6 %collective-permute-done.11 = bf16[128,2176]{1,0:T(8,128)(2,1)S(1)} collective-permute-done((bf16[128,2176]{1,0:T(8,128)(2,1)S(1)}, bf16[128,2176]{1,0:T(8,128)(2,1)S(1)}, u32[]{:S(2)}, u32[]{:S(2)}) %collective-permute-start.11) | collective-permute-done | bytes 557088 | tf_op jit(solution)/shard_map/ppermute | solution.py:773
  118.8 9.0 %attn_in.1 = (bf16[1024,1024]{1,0:T(8,128)(2,1)}, bf16[1024,256]{1,0:T(8,128)(2,1)}, bf16[1024,256]{1,0:T(8,128)(2,1)}, bf16[1024,512]{1,0:T(8,128)(2,1)}, f32[1...) custom-call(bf16[1024,1024]{1,0:T(8,128)(2,1)} %copy-done.3, f32[1,1024]{1,0:T(1,128)} %bitcast.186, ...), custom_call_target="tpu_custom_call" | custom-call | flops 1000 | bytes 1000 | tf_op jit(solution)/shard_map/attn_in/pallas_call | solution.py:566
  133.1 3.5 collective-permute-done.28
  144.7 4.2 collective-permute-done.18
  148.9 2.5 collective-permute-start.14
  152.9 7.5 %collective-permute-done.14 = bf16[128,1408]{1,0:T(8,128)(2,1)} collective-permute-done((bf16[128,1408]{1,0:T(8,128)(2,1)}, bf16[128,1408]{1,0:T(8,128)(2,1)}, u32[]{:S(2)}, u32[]{:S(2)}) %collective-permute-start.14) | collective-permute-done | bytes 360480 | tf_op jit(solution)/shard_map/ppermute | solution.py:773
  160.4 2.5 collective-permute-start.19
  168.2 2.2 collective-permute-start.15
  171.2 4.7 collective-permute-done.15
  175.8 20.7 %mix_forward.1 = (bf16[1024,512]{1,0:T(8,128)(2,1)}, f32[1024,512]{1,0:T(8,128)}, f32[8,2,256,128]{3,2,1,0:T(8,128)}) custom-call(s32[8]{0:T(128)} %fusion.38.order, bf16[1024,256]{1,0:T(8,128)(2,1)} %get-tuple-element.83.q_ref, bf16[1024,256]{1,0:T(8,128)(2,1)} %get-tuple-element.84.k_ref, bf16[1024,512]{1,0:T(8,128)(2,1)} %get-tuple-element.85.v_ref, ...), custom_call_target="tpu_custom_call" | custom-call | flops 22000001024 | bytes 1000 | tf_op jit(solution)/shard_map/mix_forward/pallas_call | solution.py:484
  199.0 2.6 constant_dynamic-slice_fusion.3
  203.3 2.2 collective-permute-start.24
  206.3 3.1 collective-permute-start.25
  212.4 5.3 %collective-permute-start.40 = (bf16[4,176,1024]{2,1,0:T(8,128)(2,1)}, bf16[4,176,1024]{2,1,0:T(8,128)(2,1)}, u32[]{:S(2)}, u32[]{:S(2)}) collective-permute-start(bf16[4,176,1024]{2,1,0:T(8,128)(2,1)} %constant_dynamic-slice_fusion.3), channel_id=1, source_target_pairs={{0,1},{1,0},{2,3},{3,2},{4,5},{5,4},{6,7},{7,6},{8,9},{9,8},{10,11... | collective-permute-start | bytes 4325384 | tf_op jit(solution)/shard_map/ppermute | solution.py:736
  222.3 7.4 %attn_out.1 = (f32[1024,1024]{1,0:T(8,128)}, bf16[1024,1024]{1,0:T(8,128)(2,1)}, f32[1024,1]{1,0:T(8,128)}) custom-call(bf16[1024,1024]{1,0:T(8,128)(2,1)} %copy-done.3, bf16[1024,1024]{1,0:T(8,128)(2,1)} %pad_maximum_fusion.3.g_ref.n_ref, bf16[1024,1024]{1,0:T(8,128)(2,1)} %pad_maximum_fusion.2.w_ref, f32[1,1024]{1,0:T(1,128)} %bitcast.187), custom_call_target="tpu_custom_call" | custom-call | flops 1000 | bytes 1000 | tf_op jit(solution)/shard_map/attn_out/pallas_call | solution.py:589
  229.7 7.3 %collective-permute-start.26 = (bf16[512,1024]{1,0:T(8,128)(2,1)}, bf16[512,1024]{1,0:T(8,128)(2,1)S(1)}, u32[]{:S(2)}, u32[]{:S(2)}) collective-permute-start(bf16[512,1024]{1,0:T(8,128)(2,1)} %pad_maximum_fusion.7), channel_id=1, source_target_pairs={{0,1},{1,0},{2,3},{3,2},{4,5},{5,4},{6,7},{7,6},{8,9},{9,8},{10,11... | collective-permute-start | bytes 3145736 | tf_op jit(solution)/shard_map/ppermute | solution.py:736
  244.3 26.4 %ffn.1 = (bf16[1024,1408]{1,0:T(8,128)(2,1)}, bf16[1024,1408]{1,0:T(8,128)(2,1)}, bf16[1024,1408]{1,0:T(8,128)(2,1)}, f32[1024,1024]{1,0:T(8,128)}, f32[1024,1024]{1,0:T(8,128)}) custom-call(s32[1]{0:T(128)} %bitcast.28.plane, bf16[1024,1024]{1,0:T(8,128)(2,1)} %get-tuple-element.99.n_ref, bf16[1024,1024]{1,0:T(8,128)(2,1)} %copy-done.2, ...), custom_call_target="tpu_custom_call" | custom-call | flops 1000 | bytes 1000 | tf_op jit(solution)/shard_map/ffn/pallas_call | solution.py:630
  270.7 3.2 slice.147
  276.1 7.3 %outer.4 = bf16[1024,1408]{1,0:T(8,128)(2,1)} custom-call(bf16[1024,1024]{1,0:T(8,128)(2,1)} %get-tuple-element.99.n_ref, bf16[1024,1408]{1,0:T(8,128)(2,1)} %get-tuple-element.95.d_ref), custom_call_target="tpu_custom_call" | custom-call | flops 1000 | bytes 1000 | tf_op jit(solution)/shard_map/outer/pallas_call | solution.py:694
  283.5 7.3 %outer.5 = bf16[1024,1408]{1,0:T(8,128)(2,1)} custom-call(bf16[1024,1024]{1,0:T(8,128)(2,1)} %get-tuple-element.99.n_ref, bf16[1024,1408]{1,0:T(8,128)(2,1)} %get-tuple-element.100.d_ref), custom_call_target="tpu_custom_call" | custom-call | flops 1000 | bytes 1000 | tf_op jit(solution)/shard_map/outer/pallas_call | solution.py:694
  290.7 3.4 add_convert_fusion.1
  294.1 7.9 %outer_wide.1 = bf16[1408,1024]{1,0:T(8,128)(2,1)} custom-call(bf16[1024,1408]{1,0:T(8,128)(2,1)} %get-tuple-element.101.n_ref, bf16[1024,1024]{1,0:T(8,128)(2,1)} %copy-done.2), custom_call_target="tpu_custom_call" | custom-call | flops 1000 | bytes 1000 | tf_op jit(solution)/shard_map/outer_wide/pallas_call | solution.py:718
  308.2 3.6 collective-permute-done.43
  311.9 6.7 %collective-permute-done.44 = bf16[128,1024]{1,0:T(8,128)(2,1)S(1)} collective-permute-done((bf16[128,1024]{1,0:T(8,128)(2,1)S(1)}, bf16[128,1024]{1,0:T(8,128)(2,1)S(1)}, u32[]{:S(2)}, u32[]{:S(2)}) %collective-permute-start.44) | collective-permute-done | bytes 262176 | tf_op jit(solution)/shard_map/ppermute | solution.py:924
  320.0 4.6 collective-permute-done.45
  325.7 11.0 %branch.1 = (f32[1024,1024]{1,0:T(8,128)}, bf16[1024,1024]{1,0:T(8,128)(2,1)}, f32[1024,512]{1,0:T(8,128)}, f32[1,1024]{1,0:T(1,128)}) custom-call(f32[1024,1024]{1,0:T(8,128)} %get-tuple-element.97.dn_ref, f32[1024,1024]{1,0:T(8,128)} %collective-permute-done.46.sw_ref, bf16[1024,1024]{1,0:T(8,128)(2,1)} %copy-done.2, ...), custom_call_target="tpu_custom_call" | custom-call | flops 1000 | bytes 1000 | tf_op jit(solution)/shard_map/branch/pallas_call | solution.py:675
  339.1 7.2 %collective-permute-start.49 = (bf16[176,1024]{1,0:T(8,128)(2,1)}, bf16[176,1024]{1,0:T(8,128)(2,1)}, u32[]{:S(2)}, u32[]{:S(2)}) collective-permute-start(bf16[176,1024]{1,0:T(8,128)(2,1)} %add_convert_fusion.12), channel_id=1, source_target_pairs={{0,8},{1,9},{2,10},{3,11},{4,0},{5,1},{6,2},{7,3},{8,16},{9,17},{1... | collective-permute-start | bytes 1081352 | tf_op jit(solution)/shard_map/ppermute | solution.py:773
  346.3 18.1 %mix_backward.1 = (bf16[1024,1536]{1,0:T(8,128)(2,1)}, bf16[1024,256]{1,0:T(8,128)(2,1)}, f32[1,256]{1,0:T(1,128)}, f32[1,256]{1,0:T(1,128)}) custom-call(s32[8]{0:T(128)} %fusion.38.order, bf16[1024,256]{1,0:T(8,128)(2,1)} %get-tuple-element.83.q_ref, bf16[1024,256]{1,0:T(8,128)(2,1)} %get-tuple-element.84.k_ref, ...), custom_call_target="tpu_custom_call" | custom-call | flops 6000000000 | bytes 1000 | tf_op jit(solution)/shard_map/mix_backward/pallas_call | solution.py:514
  375.1 7.4 %outer.6 = bf16[1024,1536]{1,0:T(8,128)(2,1)} custom-call(bf16[1024,1024]{1,0:T(8,128)(2,1)} %get-tuple-element.113.n_ref, bf16[1024,1536]{1,0:T(8,128)(2,1)} %get-tuple-element.121.d_ref), custom_call_target="tpu_custom_call" | custom-call | flops 1000 | bytes 1000 | tf_op jit(solution)/shard_map/outer/pallas_call | solution.py:694
  383.6 4.8 outer.7
  388.4 3.5 add_convert_fusion
  398.1 5.3 %fusion = f32[1024,1024]{1,0:T(8,128)S(1)} fusion(bf16[1024,1536]{1,0:T(8,128)(2,1)S(1)} %copy-done.11, bf16[1024,2176]{1,0:T(8,128)(2,1)} %bitcast.22.w_ref), kind=kOutput, calls=%fused_computation.22 | convolution fusion | flops 3221225472 | bytes 10485760 | tf_op jit(solution)/shard_map/dot_general | solution.py:44
  406.0 10.7 %collective-permute-done.68 = bf16[128,3456]{1,0:T(8,128)(2,1)S(1)} collective-permute-done((bf16[128,3456]{1,0:T(8,128)(2,1)S(1)}, bf16[128,3456]{1,0:T(8,128)(2,1)S(1)}, u32[]{:S(2)}, u32[]{:S(2)}) %collective-permute-start.68) | collective-permute-done | bytes 884768 | tf_op jit(solution)/shard_map/ppermute | solution.py:776
  422.5 15.4 %collective-permute-done.59 = bf16[128,3456]{1,0:T(8,128)(2,1)S(1)} collective-permute-done((bf16[128,3456]{1,0:T(8,128)(2,1)S(1)}, bf16[128,3456]{1,0:T(8,128)(2,1)S(1)}, u32[]{:S(2)}, u32[]{:S(2)}) %collective-permute-start.59) | collective-permute-done | bytes 884768 | tf_op jit(solution)/shard_map/ppermute | solution.py:773
  441.4 15.9 %collective-permute-done.60 = bf16[128,3456]{1,0:T(8,128)(2,1)S(1)} collective-permute-done((bf16[128,3456]{1,0:T(8,128)(2,1)S(1)}, bf16[128,3456]{1,0:T(8,128)(2,1)S(1)}, u32[]{:S(2)}, u32[]{:S(2)}) %collective-permute-start.60) | collective-permute-done | bytes 884768 | tf_op jit(solution)/shard_map/ppermute | solution.py:773
  465.4 4.0 collective-permute-done.66
  473.4 5.6 %collective-permute-done.67 = bf16[128,3456]{1,0:T(8,128)(2,1)} collective-permute-done((bf16[128,3456]{1,0:T(8,128)(2,1)}, bf16[128,3456]{1,0:T(8,128)(2,1)}, u32[]{:S(2)}, u32[]{:S(2)}) %collective-permute-start.67) | collective-permute-done | bytes 884768 | tf_op jit(solution)/shard_map/ppermute | solution.py:773
  480.7 3.8 collective-permute-done.62
  484.5 5.5 %collective-permute-done.63 = bf16[128,1024]{1,0:T(8,128)(2,1)S(1)} collective-permute-done((bf16[128,1024]{1,0:T(8,128)(2,1)S(1)}, bf16[128,1024]{1,0:T(8,128)(2,1)S(1)}, u32[]{:S(2)}, u32[]{:S(2)}) %collective-permute-start.63) | collective-permute-done | bytes 262176 | tf_op jit(solution)/shard_map/ppermute | solution.py:924
  490.2 2.8 collective-permute-start.72
  493.0 6.0 %collective-permute-done.72 = f32[214,128]{1,0:T(8,128)S(1)} collective-permute-done((f32[214,128]{1,0:T(8,128)S(1)}, f32[214,128]{1,0:T(8,128)S(1)}, u32[]{:S(2)}, u32[]{:S(2)}) %collective-permute-start.72) | collective-permute-done | bytes 109600 | tf_op jit(solution)/shard_map/ppermute | solution.py:851
  500.3 4.0 collective-permute-start.74
  (350 shorter events, 167.5 us)
Async XLA Ops:
  5.5 48.3 %collective-permute-start = (bf16[128,2176]{1,0:T(8,128)(2,1)S(1)}, bf16[128,2176]{1,0:T(8,128)(2,1)}, u32[]{:S(2)}, u32[]{:S(2)}) collective-permute-start(bf16[128,2176]{1,0:T(8,128)(2,1)S(1)} %concatenate.69), channel_id=1, source_target_pairs={{0,8},{1,9},{2,10},{3,11},{4,0},{5,1},{6,2},{7,3},{8,16},{9,17},{1... | collective-permute-start | bytes 1671176 | tf_op jit(solution)/shard_map/ppermute | solution.py:773
  8.6 45.2 %collective-permute-start.1 = (bf16[128,2176]{1,0:T(8,128)(2,1)S(1)}, bf16[128,2176]{1,0:T(8,128)(2,1)}, u32[]{:S(2)}, u32[]{:S(2)}) collective-permute-start(bf16[128,2176]{1,0:T(8,128)(2,1)S(1)} %concatenate.69), channel_id=1, source_target_pairs={{0,4},{1,5},{2,6},{3,7},{4,12},{5,13},{6,14},{7,15},{8,0},{9,1},{1... | collective-permute-start | bytes 1671176 | tf_op jit(solution)/shard_map/ppermute | solution.py:776
  9.6 22.1 %collective-permute-start.2 = (bf16[128,1024]{1,0:T(8,128)(2,1)}, bf16[128,1024]{1,0:T(8,128)(2,1)}, u32[]{:S(2)}, u32[]{:S(2)}) collective-permute-start(bf16[128,1024]{1,0:T(8,128)(2,1)} %get-tuple-element.191), channel_id=1, source_target_pairs={{0,0},{1,16},{2,2},{3,18},{4,4},{5,20},{6,6},{7,22},{8,8},{9,24},{... | collective-permute-start | bytes 786440 | tf_op jit(solution)/shard_map/ppermute | solution.py:912
  13.2 39.4 %collective-permute-start.3 = (bf16[128,1024]{1,0:T(8,128)(2,1)}, bf16[128,1024]{1,0:T(8,128)(2,1)}, u32[]{:S(2)}, u32[]{:S(2)}) collective-permute-start(bf16[128,1024]{1,0:T(8,128)(2,1)} %get-tuple-element.192), channel_id=1, source_target_pairs={{0,4},{1,20},{2,6},{3,22},{4,8},{5,24},{6,10},{7,26},{8,12},{9,28}... | collective-permute-start | bytes 786440 | tf_op jit(solution)/shard_map/ppermute | solution.py:912
  15.2 37.4 %collective-permute-start.4 = (bf16[128,1024]{1,0:T(8,128)(2,1)}, bf16[128,1024]{1,0:T(8,128)(2,1)}, u32[]{:S(2)}, u32[]{:S(2)}) collective-permute-start(bf16[128,1024]{1,0:T(8,128)(2,1)} %get-tuple-element.194), channel_id=1, source_target_pairs={{0,8},{1,24},{2,10},{3,26},{4,12},{5,28},{6,14},{7,30},{8,0},{9,16... | collective-permute-start | bytes 786440 | tf_op jit(solution)/shard_map/ppermute | solution.py:912
  31.7 20.9 %collective-permute-start.5 = (bf16[128,1024]{1,0:T(8,128)(2,1)S(1)}, bf16[128,1024]{1,0:T(8,128)(2,1)S(1)}, u32[]{:S(2)}, u32[]{:S(2)}) collective-permute-start(bf16[128,1024]{1,0:T(8,128)(2,1)S(1)} %copy-done.23), channel_id=1, source_target_pairs={{0,12},{1,28},{2,14},{3,30},{4,0},{5,16},{6,2},{7,18},{8,4},{9,20}... | collective-permute-start | bytes 786440 | tf_op jit(solution)/shard_map/ppermute | solution.py:912
  53.9 20.6 %collective-permute-start.6 = (bf16[512,1024]{1,0:T(8,128)(2,1)S(1)}, bf16[512,1024]{1,0:T(8,128)(2,1)S(1)}, u32[]{:S(2)}, u32[]{:S(2)}) collective-permute-start(bf16[512,1024]{1,0:T(8,128)(2,1)S(1)} %pad_maximum_fusion.5), channel_id=1, source_target_pairs={{0,1},{1,0},{2,3},{3,2},{4,5},{5,4},{6,7},{7,6},{8,9},{9,8},{10,11... | collective-permute-start | bytes 3145736 | tf_op jit(solution)/shard_map/ppermute | solution.py:736
  56.0 15.1 %collective-permute-start.8 = (bf16[128,2176]{1,0:T(8,128)(2,1)}, bf16[128,2176]{1,0:T(8,128)(2,1)S(1)}, u32[]{:S(2)}, u32[]{:S(2)}) collective-permute-start(bf16[128,2176]{1,0:T(8,128)(2,1)} %collective-permute-done.1), channel_id=1, source_target_pairs={{0,4},{1,5},{2,6},{3,7},{4,12},{5,13},{6,14},{7,15},{8,0},{9,1},{1... | collective-permute-start | bytes 1671176 | tf_op jit(solution)/shard_map/ppermute | solution.py:776
  71.1 23.8 %collective-permute-start.10 = (bf16[128,2176]{1,0:T(8,128)(2,1)S(1)}, bf16[128,2176]{1,0:T(8,128)(2,1)S(1)}, u32[]{:S(2)}, u32[]{:S(2)}) collective-permute-start(bf16[128,2176]{1,0:T(8,128)(2,1)S(1)} %collective-permute-done.8), channel_id=1, source_target_pairs={{0,4},{1,5},{2,6},{3,7},{4,12},{5,13},{6,14},{7,15},{8,0},{9,1},{1... | collective-permute-start | bytes 1671176 | tf_op jit(solution)/shard_map/ppermute | solution.py:776
  86.6 17.0 %collective-permute-start.12 = (bf16[128,1408]{1,0:T(8,128)(2,1)S(1)}, bf16[128,1408]{1,0:T(8,128)(2,1)S(1)}, u32[]{:S(2)}, u32[]{:S(2)}) collective-permute-start(bf16[128,1408]{1,0:T(8,128)(2,1)S(1)} %broadcast_select_fusion.14), channel_id=1, source_target_pairs={{0,8},{1,9},{2,10},{3,11},{4,0},{5,1},{6,2},{7,3},{8,16},{9,17},{1... | collective-permute-start | bytes 1081352 | tf_op jit(solution)/shard_map/ppermute | solution.py:773
  87.2 18.8 %collective-permute-start.27 = (bf16[128,1408]{1,0:T(8,128)(2,1)S(1)}, bf16[128,1408]{1,0:T(8,128)(2,1)S(1)}, u32[]{:S(2)}, u32[]{:S(2)}) collective-permute-start(bf16[128,1408]{1,0:T(8,128)(2,1)S(1)} %broadcast_select_fusion.14), channel_id=1, source_target_pairs={{0,4},{1,5},{2,6},{3,7},{4,12},{5,13},{6,14},{7,15},{8,0},{9,1},{1... | collective-permute-start | bytes 1081352 | tf_op jit(solution)/shard_map/ppermute | solution.py:776
  94.9 20.7 %collective-permute-start.11 = (bf16[128,2176]{1,0:T(8,128)(2,1)S(1)}, bf16[128,2176]{1,0:T(8,128)(2,1)S(1)}, u32[]{:S(2)}, u32[]{:S(2)}) collective-permute-start(bf16[128,2176]{1,0:T(8,128)(2,1)S(1)} %collective-permute-done.9), channel_id=1, source_target_pairs={{0,8},{1,9},{2,10},{3,11},{4,0},{5,1},{6,2},{7,3},{8,16},{9,17},{1... | collective-permute-start | bytes 1671176 | tf_op jit(solution)/shard_map/ppermute | solution.py:773
  96.3 42.5 %collective-permute-start.17 = (bf16[176,1024]{1,0:T(8,128)(2,1)S(1)}, bf16[176,1024]{1,0:T(8,128)(2,1)S(1)}, u32[]{:S(2)}, u32[]{:S(2)}) collective-permute-start(bf16[176,1024]{1,0:T(8,128)(2,1)S(1)} %collective-permute-done.16), channel_id=1, source_target_pairs={{0,8},{1,9},{2,10},{3,11},{4,0},{5,1},{6,2},{7,3},{8,16},{9,17},{1... | collective-permute-start | bytes 1081352 | tf_op jit(solution)/shard_map/ppermute | solution.py:773
  98.9 40.5 %collective-permute-start.38 = (bf16[176,1024]{1,0:T(8,128)(2,1)S(1)}, bf16[176,1024]{1,0:T(8,128)(2,1)S(1)}, u32[]{:S(2)}, u32[]{:S(2)}) collective-permute-start(bf16[176,1024]{1,0:T(8,128)(2,1)S(1)} %collective-permute-done.37), channel_id=1, source_target_pairs={{0,4},{1,5},{2,6},{3,7},{4,12},{5,13},{6,14},{7,15},{8,0},{9,1},{1... | collective-permute-start | bytes 1081352 | tf_op jit(solution)/shard_map/ppermute | solution.py:776
  103.7 25.4 %collective-permute-start.30 = (bf16[128,1408]{1,0:T(8,128)(2,1)S(1)}, bf16[128,1408]{1,0:T(8,128)(2,1)S(1)}, u32[]{:S(2)}, u32[]{:S(2)}) collective-permute-start(bf16[128,1408]{1,0:T(8,128)(2,1)S(1)} %collective-permute-done.12), channel_id=1, source_target_pairs={{0,2},{2,0},{1,3},{3,1},{4,6},{6,4},{5,7},{7,5},{8,10},{10,8},{9,1... | collective-permute-start | bytes 1081352 | tf_op jit(solution)/shard_map/ppermute | solution.py:740
  106.0 35.2 %collective-permute-start.31 = (bf16[128,1408]{1,0:T(8,128)(2,1)S(1)}, bf16[128,1408]{1,0:T(8,128)(2,1)}, u32[]{:S(2)}, u32[]{:S(2)}) collective-permute-start(bf16[128,1408]{1,0:T(8,128)(2,1)S(1)} %collective-permute-done.27), channel_id=1, source_target_pairs={{0,2},{2,0},{1,3},{3,1},{4,6},{6,4},{5,7},{7,5},{8,10},{10,8},{9,1... | collective-permute-start | bytes 1081352 | tf_op jit(solution)/shard_map/ppermute | solution.py:740
  115.6 15.8 %collective-permute-start.13 = (bf16[128,1408]{1,0:T(8,128)(2,1)S(1)}, bf16[128,1408]{1,0:T(8,128)(2,1)}, u32[]{:S(2)}, u32[]{:S(2)}) collective-permute-start(bf16[128,1408]{1,0:T(8,128)(2,1)S(1)} %collective-permute-done.12), channel_id=1, source_target_pairs={{0,8},{1,9},{2,10},{3,11},{4,0},{5,1},{6,2},{7,3},{8,16},{9,17},{1... | collective-permute-start | bytes 1081352 | tf_op jit(solution)/shard_map/ppermute | solution.py:773
  131.4 74.9 %collective-permute-start.21 = (bf16[1024,512]{1,0:T(8,128)(2,1)S(1)}, bf16[1024,512]{1,0:T(8,128)(2,1)S(1)}, u32[]{:S(2)}, u32[]{:S(2)}) collective-permute-start(bf16[1024,512]{1,0:T(8,128)(2,1)S(1)} %slice.190), channel_id=1, source_target_pairs={{0,1},{1,0},{2,3},{3,2},{4,5},{5,4},{6,7},{7,6},{8,9},{9,8},{10,11... | collective-permute-start | bytes 3145736 | tf_op jit(solution)/shard_map/ppermute | solution.py:736
  136.6 30.3 %collective-permute-start.32 = (bf16[128,1408]{1,0:T(8,128)(2,1)}, bf16[128,1408]{1,0:T(8,128)(2,1)S(1)}, u32[]{:S(2)}, u32[]{:S(2)}) collective-permute-start(bf16[128,1408]{1,0:T(8,128)(2,1)} %collective-permute-done.13), channel_id=1, source_target_pairs={{0,2},{2,0},{1,3},{3,1},{4,6},{6,4},{5,7},{7,5},{8,10},{10,8},{9,1... | collective-permute-start | bytes 1081352 | tf_op jit(solution)/shard_map/ppermute | solution.py:740
  138.9 29.3 %collective-permute-start.33 = (bf16[128,1408]{1,0:T(8,128)(2,1)S(1)}, bf16[128,1408]{1,0:T(8,128)(2,1)S(1)}, u32[]{:S(2)}, u32[]{:S(2)}) collective-permute-start(bf16[128,1408]{1,0:T(8,128)(2,1)S(1)} %collective-permute-done.28), channel_id=1, source_target_pairs={{0,2},{2,0},{1,3},{3,1},{4,6},{6,4},{5,7},{7,5},{8,10},{10,8},{9,1... | collective-permute-start | bytes 1081352 | tf_op jit(solution)/shard_map/ppermute | solution.py:740
  164.7 36.9 %collective-permute-start.34 = (bf16[128,1408]{1,0:T(8,128)(2,1)}, bf16[128,1408]{1,0:T(8,128)(2,1)}, u32[]{:S(2)}, u32[]{:S(2)}) collective-permute-start(bf16[128,1408]{1,0:T(8,128)(2,1)} %collective-permute-done.14), channel_id=1, source_target_pairs={{0,2},{2,0},{1,3},{3,1},{4,6},{6,4},{5,7},{7,5},{8,10},{10,8},{9,1... | collective-permute-start | bytes 1081352 | tf_op jit(solution)/shard_map/ppermute | solution.py:740
  166.9 36.4 %collective-permute-start.35 = (bf16[128,1408]{1,0:T(8,128)(2,1)S(1)}, bf16[128,1408]{1,0:T(8,128)(2,1)S(1)}, u32[]{:S(2)}, u32[]{:S(2)}) collective-permute-start(bf16[128,1408]{1,0:T(8,128)(2,1)S(1)} %collective-permute-done.29), channel_id=1, source_target_pairs={{0,2},{2,0},{1,3},{3,1},{4,6},{6,4},{5,7},{7,5},{8,10},{10,8},{9,1... | collective-permute-start | bytes 1081352 | tf_op jit(solution)/shard_map/ppermute | solution.py:740
  196.5 23.7 %collective-permute-start.20 = (bf16[1024,512]{1,0:T(8,128)(2,1)}, bf16[1024,512]{1,0:T(8,128)(2,1)S(1)}, u32[]{:S(2)}, u32[]{:S(2)}) collective-permute-start(bf16[1024,512]{1,0:T(8,128)(2,1)} %get-tuple-element.88), channel_id=1, source_target_pairs={{0,1},{1,0},{2,3},{3,2},{4,5},{5,4},{6,7},{7,6},{8,9},{9,8},{10,11... | collective-permute-start | bytes 3145736 | tf_op jit(solution)/shard_map/ppermute | solution.py:736
  196.7 15.6 %collective-permute-start.22 = (bf16[128,1024]{1,0:T(8,128)(2,1)S(1)}, bf16[128,1024]{1,0:T(8,128)(2,1)S(1)}, u32[]{:S(2)}, u32[]{:S(2)}) collective-permute-start(bf16[128,1024]{1,0:T(8,128)(2,1)S(1)} %get-tuple-element.185), channel_id=1, source_target_pairs={{0,0},{1,16},{2,2},{3,18},{4,4},{5,20},{6,6},{7,22},{8,8},{9,24},{... | collective-permute-start | bytes 786440 | tf_op jit(solution)/shard_map/ppermute | solution.py:912
  201.5 16.2 %collective-permute-start.23 = (bf16[128,1024]{1,0:T(8,128)(2,1)S(1)}, bf16[128,1024]{1,0:T(8,128)(2,1)S(1)}, u32[]{:S(2)}, u32[]{:S(2)}) collective-permute-start(bf16[128,1024]{1,0:T(8,128)(2,1)S(1)} %get-tuple-element.188), channel_id=1, source_target_pairs={{0,4},{1,20},{2,6},{3,22},{4,8},{5,24},{6,10},{7,26},{8,12},{9,28}... | collective-permute-start | bytes 786440 | tf_op jit(solution)/shard_map/ppermute | solution.py:912
  203.3 15.9 %collective-permute-start.24 = (bf16[128,1024]{1,0:T(8,128)(2,1)S(1)}, bf16[128,1024]{1,0:T(8,128)(2,1)S(1)}, u32[]{:S(2)}, u32[]{:S(2)}) collective-permute-start(bf16[128,1024]{1,0:T(8,128)(2,1)S(1)} %get-tuple-element.187), channel_id=1, source_target_pairs={{0,8},{1,24},{2,10},{3,26},{4,12},{5,28},{6,14},{7,30},{8,0},{9,16... | collective-permute-start | bytes 786440 | tf_op jit(solution)/shard_map/ppermute | solution.py:912
  212.4 26.7 %collective-permute-start.40 = (bf16[4,176,1024]{2,1,0:T(8,128)(2,1)}, bf16[4,176,1024]{2,1,0:T(8,128)(2,1)}, u32[]{:S(2)}, u32[]{:S(2)}) collective-permute-start(bf16[4,176,1024]{2,1,0:T(8,128)(2,1)} %constant_dynamic-slice_fusion.3), channel_id=1, source_target_pairs={{0,1},{1,0},{2,3},{3,2},{4,5},{5,4},{6,7},{7,6},{8,9},{9,8},{10,11... | collective-permute-start | bytes 4325384 | tf_op jit(solution)/shard_map/ppermute | solution.py:736
  217.7 19.3 %collective-permute-start.36 = (bf16[128,1408]{1,0:T(8,128)(2,1)S(1)}, bf16[128,1408]{1,0:T(8,128)(2,1)S(1)}, u32[]{:S(2)}, u32[]{:S(2)}) collective-permute-start(bf16[128,1408]{1,0:T(8,128)(2,1)S(1)} %collective-permute-done.15), channel_id=1, source_target_pairs={{0,2},{2,0},{1,3},{3,1},{4,6},{6,4},{5,7},{7,5},{8,10},{10,8},{9,1... | collective-permute-start | bytes 1081352 | tf_op jit(solution)/shard_map/ppermute | solution.py:740
  273.9 16.8 %collective-permute-start.41 = (f32[512,1024]{1,0:T(8,128)}, f32[512,1024]{1,0:T(8,128)}, u32[]{:S(2)}, u32[]{:S(2)}) collective-permute-start(f32[512,1024]{1,0:T(8,128)} %slice.147), channel_id=1, source_target_pairs={{0,1},{1,0},{2,3},{3,2},{4,5},{5,4},{6,7},{7,6},{8,9},{9,8},{10,11... | collective-permute-start | bytes 6291464 | tf_op jit(solution)/shard_map/ppermute | solution.py:736
  273.9 51.7 %collective-permute-start.46 = (f32[1024,1024]{1,0:T(8,128)}, f32[1024,1024]{1,0:T(8,128)}, u32[]{:S(2)}, u32[]{:S(2)}) collective-permute-start(f32[1024,1024]{1,0:T(8,128)} %get-tuple-element.97.dn_ref), channel_id=1, source_target_pairs={{0,1},{1,0},{2,3},{3,2},{4,5},{5,4},{6,7},{7,6},{8,9},{9,8},{10,11... | collective-permute-start | bytes 12582920 | tf_op jit(solution)/shard_map/ppermute | solution.py:736
  303.6 15.0 %collective-permute-start.47 = (bf16[4,176,1024]{2,1,0:T(8,128)(2,1)S(1)}, bf16[4,176,1024]{2,1,0:T(8,128)(2,1)S(1)}, u32[]{:S(2)}, u32[]{:S(2)}) collective-permute-start(bf16[4,176,1024]{2,1,0:T(8,128)(2,1)S(1)} %dynamic-slice_bitcast_fusion), channel_id=1, source_target_pairs={{0,1},{1,0},{2,3},{3,2},{4,5},{5,4},{6,7},{7,6},{8,9},{9,8},{10,11... | collective-permute-start | bytes 4325384 | tf_op jit(solution)/shard_map/ppermute | solution.py:736
  306.6 81.8 %collective-permute-start.55 = (bf16[1024,1408]{1,0:T(8,128)(2,1)}, bf16[1024,1408]{1,0:T(8,128)(2,1)}, u32[]{:S(2)}, u32[]{:S(2)}) collective-permute-start(bf16[1024,1408]{1,0:T(8,128)(2,1)} %outer.4), channel_id=1, source_target_pairs={{0,2},{2,0},{1,3},{3,1},{4,6},{6,4},{5,7},{7,5},{8,10},{10,8},{9,1... | collective-permute-start | bytes 8650760 | tf_op jit(solution)/shard_map/ppermute | solution.py:740
  319.7 16.9 %collective-permute-start.52 = (bf16[176,1024]{1,0:T(8,128)(2,1)S(1)}, bf16[176,1024]{1,0:T(8,128)(2,1)S(1)}, u32[]{:S(2)}, u32[]{:S(2)}) collective-permute-start(bf16[176,1024]{1,0:T(8,128)(2,1)S(1)} %get-tuple-element.153), channel_id=1, source_target_pairs={{0,4},{1,5},{2,6},{3,7},{4,12},{5,13},{6,14},{7,15},{8,0},{9,1},{1... | collective-permute-start | bytes 1081352 | tf_op jit(solution)/shard_map/ppermute | solution.py:776
  336.8 35.8 %collective-permute-start.53 = (bf16[176,1024]{1,0:T(8,128)(2,1)S(1)}, bf16[176,1024]{1,0:T(8,128)(2,1)}, u32[]{:S(2)}, u32[]{:S(2)}) collective-permute-start(bf16[176,1024]{1,0:T(8,128)(2,1)S(1)} %add_convert_fusion.9), channel_id=1, source_target_pairs={{0,4},{1,5},{2,6},{3,7},{4,12},{5,13},{6,14},{7,15},{8,0},{9,1},{1... | collective-permute-start | bytes 1081352 | tf_op jit(solution)/shard_map/ppermute | solution.py:776
  339.1 31.7 %collective-permute-start.49 = (bf16[176,1024]{1,0:T(8,128)(2,1)}, bf16[176,1024]{1,0:T(8,128)(2,1)}, u32[]{:S(2)}, u32[]{:S(2)}) collective-permute-start(bf16[176,1024]{1,0:T(8,128)(2,1)} %add_convert_fusion.12), channel_id=1, source_target_pairs={{0,8},{1,9},{2,10},{3,11},{4,0},{5,1},{6,2},{7,3},{8,16},{9,17},{1... | collective-permute-start | bytes 1081352 | tf_op jit(solution)/shard_map/ppermute | solution.py:773
  373.7 22.7 %collective-permute-start.54 = (bf16[176,1024]{1,0:T(8,128)(2,1)S(1)}, bf16[176,1024]{1,0:T(8,128)(2,1)S(1)}, u32[]{:S(2)}, u32[]{:S(2)}) collective-permute-start(bf16[176,1024]{1,0:T(8,128)(2,1)S(1)} %add_convert_fusion.8), channel_id=1, source_target_pairs={{0,4},{1,5},{2,6},{3,7},{4,12},{5,13},{6,14},{7,15},{8,0},{9,1},{1... | collective-permute-start | bytes 1081352 | tf_op jit(solution)/shard_map/ppermute | solution.py:776
  394.3 23.3 %collective-permute-start.58 = (bf16[128,3456]{1,0:T(8,128)(2,1)S(1)}, bf16[128,3456]{1,0:T(8,128)(2,1)S(1)}, u32[]{:S(2)}, u32[]{:S(2)}) collective-permute-start(bf16[128,3456]{1,0:T(8,128)(2,1)S(1)} %get-tuple-element.146), channel_id=1, source_target_pairs={{0,8},{1,9},{2,10},{3,11},{4,0},{5,1},{6,2},{7,3},{8,16},{9,17},{1... | collective-permute-start | bytes 2654216 | tf_op jit(solution)/shard_map/ppermute | solution.py:773
  395.2 21.5 %collective-permute-start.68 = (bf16[128,3456]{1,0:T(8,128)(2,1)S(1)}, bf16[128,3456]{1,0:T(8,128)(2,1)S(1)}, u32[]{:S(2)}, u32[]{:S(2)}) collective-permute-start(bf16[128,3456]{1,0:T(8,128)(2,1)S(1)} %get-tuple-element.140), channel_id=1, source_target_pairs={{0,4},{1,5},{2,6},{3,7},{4,12},{5,13},{6,14},{7,15},{8,0},{9,1},{1... | collective-permute-start | bytes 2654216 | tf_op jit(solution)/shard_map/ppermute | solution.py:776
  403.7 15.8 %collective-permute-start.56 = (f32[512,1024]{1,0:T(8,128)S(1)}, f32[512,1024]{1,0:T(8,128)S(1)}, u32[]{:S(2)}, u32[]{:S(2)}) collective-permute-start(f32[512,1024]{1,0:T(8,128)S(1)} %slice.197), channel_id=1, source_target_pairs={{0,1},{1,0},{2,3},{3,2},{4,5},{5,4},{6,7},{7,6},{8,9},{9,8},{10,11... | collective-permute-start | bytes 6291464 | tf_op jit(solution)/shard_map/ppermute | solution.py:736
  405.9 56.6 %collective-permute-start.79 = (f32[176,1024]{1,0:T(8,128)S(1)}, f32[176,1024]{1,0:T(8,128)}, u32[]{:S(2)}, u32[]{:S(2)}) collective-permute-start(f32[176,1024]{1,0:T(8,128)S(1)} %convert_add_fusion.2), channel_id=1, source_target_pairs={{0,1},{1,0},{2,3},{3,2},{4,5},{5,4},{6,7},{7,6},{8,9},{9,8},{10,11... | collective-permute-start | bytes 2162696 | tf_op jit(solution)/shard_map/ppermute | solution.py:736
  416.9 23.1 %collective-permute-start.69 = (bf16[128,3456]{1,0:T(8,128)(2,1)S(1)}, bf16[128,3456]{1,0:T(8,128)(2,1)S(1)}, u32[]{:S(2)}, u32[]{:S(2)}) collective-permute-start(bf16[128,3456]{1,0:T(8,128)(2,1)S(1)} %add_convert_fusion.4), channel_id=1, source_target_pairs={{0,4},{1,5},{2,6},{3,7},{4,12},{5,13},{6,14},{7,15},{8,0},{9,1},{1... | collective-permute-start | bytes 2654216 | tf_op jit(solution)/shard_map/ppermute | solution.py:776
  417.8 20.0 %collective-permute-start.59 = (bf16[128,3456]{1,0:T(8,128)(2,1)S(1)}, bf16[128,3456]{1,0:T(8,128)(2,1)S(1)}, u32[]{:S(2)}, u32[]{:S(2)}) collective-permute-start(bf16[128,3456]{1,0:T(8,128)(2,1)S(1)} %add_convert_fusion.6), channel_id=1, source_target_pairs={{0,8},{1,9},{2,10},{3,11},{4,0},{5,1},{6,2},{7,3},{8,16},{9,17},{1... | collective-permute-start | bytes 2654216 | tf_op jit(solution)/shard_map/ppermute | solution.py:773
  438.2 19.1 %collective-permute-start.60 = (bf16[128,3456]{1,0:T(8,128)(2,1)S(1)}, bf16[128,3456]{1,0:T(8,128)(2,1)S(1)}, u32[]{:S(2)}, u32[]{:S(2)}) collective-permute-start(bf16[128,3456]{1,0:T(8,128)(2,1)S(1)} %add_convert_fusion.5), channel_id=1, source_target_pairs={{0,8},{1,9},{2,10},{3,11},{4,0},{5,1},{6,2},{7,3},{8,16},{9,17},{1... | collective-permute-start | bytes 2654216 | tf_op jit(solution)/shard_map/ppermute | solution.py:773
  441.1 30.8 %collective-permute-start.70 = (bf16[128,3456]{1,0:T(8,128)(2,1)}, bf16[128,3456]{1,0:T(8,128)(2,1)S(1)}, u32[]{:S(2)}, u32[]{:S(2)}) collective-permute-start(bf16[128,3456]{1,0:T(8,128)(2,1)} %add_convert_fusion.3), channel_id=1, source_target_pairs={{0,4},{1,5},{2,6},{3,7},{4,12},{5,13},{6,14},{7,15},{8,0},{9,1},{1... | collective-permute-start | bytes 2654216 | tf_op jit(solution)/shard_map/ppermute | solution.py:776
  458.5 20.4 %collective-permute-start.67 = (bf16[128,3456]{1,0:T(8,128)(2,1)}, bf16[128,3456]{1,0:T(8,128)(2,1)}, u32[]{:S(2)}, u32[]{:S(2)}) collective-permute-start(bf16[128,3456]{1,0:T(8,128)(2,1)} %fusion.12), channel_id=1, source_target_pairs={{0,8},{1,9},{2,10},{3,11},{4,0},{5,1},{6,2},{7,3},{8,16},{9,17},{1... | collective-permute-start | bytes 2654216 | tf_op jit(solution)/shard_map/ppermute | solution.py:773
  470.2 19.8 %collective-permute-start.63 = (bf16[128,1024]{1,0:T(8,128)(2,1)S(1)}, bf16[128,1024]{1,0:T(8,128)(2,1)S(1)}, u32[]{:S(2)}, u32[]{:S(2)}) collective-permute-start(bf16[128,1024]{1,0:T(8,128)(2,1)S(1)} %get-tuple-element.178), channel_id=1, source_target_pairs={{8,0},{24,1},{10,2},{26,3},{12,4},{28,5},{14,6},{30,7},{0,8},{16,9... | collective-permute-start | bytes 786440 | tf_op jit(solution)/shard_map/ppermute | solution.py:924
  471.9 21.0 %collective-permute-start.64 = (bf16[128,1024]{1,0:T(8,128)(2,1)S(1)}, bf16[128,1024]{1,0:T(8,128)(2,1)S(1)}, u32[]{:S(2)}, u32[]{:S(2)}) collective-permute-start(bf16[128,1024]{1,0:T(8,128)(2,1)S(1)} %get-tuple-element.177), channel_id=1, source_target_pairs={{12,0},{28,1},{14,2},{30,3},{0,4},{16,5},{2,6},{18,7},{4,8},{20,9}... | collective-permute-start | bytes 786440 | tf_op jit(solution)/shard_map/ppermute | solution.py:924
  480.4 19.8 %collective-permute-start.73 = (bf16[128,3456]{1,0:T(8,128)(2,1)S(1)}, bf16[128,3456]{1,0:T(8,128)(2,1)S(1)}, u32[]{:S(2)}, u32[]{:S(2)}) collective-permute-start(bf16[128,3456]{1,0:T(8,128)(2,1)S(1)} %add_convert_fusion.2), channel_id=1, source_target_pairs={{0,2},{2,0},{1,3},{3,1},{4,6},{6,4},{5,7},{7,5},{8,10},{10,8},{9,1... | collective-permute-start | bytes 2654216 | tf_op jit(solution)/shard_map/ppermute | solution.py:740
  (67 other events, 755.7 us)
